TPU v7x, 32 devices: a whole 2x2x4 slice. The times are simulated.
32 devices in a mesh: groups: 1, ep: 32 (over z, y, x, core).
Axes of the slice: x: 2, y: 2, z: 4, core: 2. Of those that a mesh axis runs over, the one named last changes fastest.
Arguments:
- hidden: bfloat16 [256, 7168], P(('groups', 'ep')), may hold values from -6 to 6
- queries: bfloat16 [256, 128, 576], P(('groups', 'ep')), may hold values from -6 to 6
- cache: bfloat16 [256, 256, 576], P(('groups', 'ep')), may hold values from -6 to 6
- lengths: int32 [256], P(('groups', 'ep')), may hold values from 1 to 256, 32768 in all
- value_up: bfloat16 [128, 512, 128], P('ep'), may hold values from -0.25 to 0.25
- out_proj: bfloat16 [16384, 7168], P('ep'), may hold values from -0.09375 to 0.09375
- norm_gain: bfloat16 [7168], replicated, may hold values from 0.25 to 1.75
- routes: int32 [256, 2], P(('groups', 'ep')), may hold values from 0 to 3, all different within a row; in each aligned block of 8 rows (0 to 7, 8 to 15, ...) at most 8 rows name the same one
- gates: float32 [256, 2], P(('groups', 'ep')), may hold values from 0.3 to 1.5
- expert_slot: int32 [4], replicated, may hold values from 0 to 3, each once
- w_gate: bfloat16 [7168, 4096], P(None, 'ep'), may hold values from -0.0625 to 0.0625
- w_up: bfloat16 [7168, 4096], P(None, 'ep'), may hold values from -0.0625 to 0.0625
- w_down: bfloat16 [4096, 7168], P('ep'), may hold values from -0.1875 to 0.1875
Outputs:
- result: bfloat16 [256, 7168], P(('groups', 'ep'))
Inputs may be any that keep to these rules, and one draw needn't show every extreme that they name: `routes`: each row names 2 different logical experts. Among the rows of one device no expert is named by more than 8 rows, a bound that some block reaches of them. `expert_slot`: each slot appears once. `lengths`: the largest length is exactly 256.
All inputs are finite; a program needn't handle non-finite values. No bound on the sum of `lengths` on one device may be relied on, other than what follows from the above.
Results may differ from a plain program's by a relative error of at most 0.0065.
Values may be sent and summed in bfloat16 or wider, within the bound.
No kernel may reach another device: no remote copies, remote signals or barrier semaphores. Data moves between devices by JAX's collectives and lax.ppermute only.
A program may use at most 128 MiB of HBM per device.

v0:
```python
import jax
import jax.numpy as jnp
from jax import lax
from jax.sharding import PartitionSpec as P

LATENT = 512
SLABS = 8


score_scale = 192.0 ** (-0.5)
norm_eps = 1e-06


def attend(queries, cache, lengths):
    scores = (
        jnp.einsum("bhr,bpr->bhp", queries, cache, preferred_element_type=jnp.float32) * score_scale
    )
    live_mask = lax.broadcasted_iota(jnp.int32, scores.shape, 2) < lengths[:, None, None]
    row_max = jnp.max(jnp.where(live_mask, scores, -jnp.inf), axis=2, keepdims=True)
    raised = jnp.where(live_mask, jnp.exp(scores - row_max), 0.0)
    probs_bf = (raised / jnp.sum(raised, axis=2, keepdims=True)).astype(jnp.bfloat16)
    return jnp.einsum(
        "bhp,bpl->bhl", probs_bf, cache[:, :, :LATENT], preferred_element_type=jnp.float32
    ).astype(jnp.bfloat16)


def on_device(
    hidden,
    queries,
    cache,
    lengths,
    value_up,
    out_proj,
    norm_gain,
    routes,
    gates,
    expert_slot,
    w_gate,
    w_up,
    w_down,
):
    row_count = hidden.shape[0]
    latent_out = attend(queries, cache, lengths)
    by_heads = lax.all_to_all(latent_out, "ep", split_axis=1, concat_axis=0, tiled=True)
    head_values = jnp.einsum(
        "bhl,hlv->bhv", by_heads, value_up, preferred_element_type=jnp.float32
    ).astype(jnp.bfloat16)
    flat_values = head_values.reshape(head_values.shape[0], -1)
    attended = lax.psum_scatter(
        jnp.dot(flat_values, out_proj, preferred_element_type=jnp.float32),
        "ep",
        scatter_dimension=0,
        tiled=True,
    )
    mixed = hidden.astype(jnp.float32) + attended
    scale_rows = lax.rsqrt(jnp.mean(mixed * mixed, axis=1, keepdims=True) + norm_eps)
    normed = (mixed * scale_rows * norm_gain.astype(jnp.float32)).astype(jnp.bfloat16)
    experts = expert_slot.shape[0]
    route_count = routes.shape[1]
    capacity = min(row_count, 2 * row_count * route_count // experts)
    model_width = normed.shape[1]
    labels = jnp.arange(experts, dtype=jnp.int32)
    physical = jnp.sum(
        jnp.where(routes[:, :, None] == labels[None, None, :], expert_slot[None, None, :], 0),
        axis=2,
    )
    flat_phys = physical.reshape(-1)
    route_hits = (flat_phys[:, None] == labels[None, :]).astype(jnp.int32)
    position = jnp.sum((jnp.cumsum(route_hits, axis=0) - route_hits) * route_hits, axis=1)
    slot_ids = flat_phys * capacity + position
    picker = (slot_ids[:, None] == jnp.arange(experts * capacity, dtype=jnp.int32)[None, :]).astype(
        jnp.float32
    )
    picker = picker.reshape(row_count, route_count, experts * capacity)
    selector = jnp.sum(picker, axis=1).T.astype(jnp.bfloat16)
    mixing = jnp.sum(picker * gates[:, :, None], axis=1)
    routed = jnp.dot(selector, normed, preferred_element_type=jnp.float32).astype(jnp.bfloat16)
    outgoing = jnp.repeat(routed.reshape(experts, capacity, model_width), SLABS, axis=0)
    tokens = lax.all_to_all(outgoing, "ep", split_axis=0, concat_axis=0, tiled=True)
    flat_rows = tokens.reshape(-1, tokens.shape[-1])
    gate_act = jnp.dot(flat_rows, w_gate, preferred_element_type=jnp.float32)
    up_act = jnp.dot(flat_rows, w_up, preferred_element_type=jnp.float32)
    inner_act = (jax.nn.silu(gate_act) * up_act).astype(jnp.bfloat16)
    slab_parts = (
        jnp.dot(inner_act, w_down, preferred_element_type=jnp.float32)
        .astype(jnp.bfloat16)
        .reshape(tokens.shape)
    )
    returned = lax.all_to_all(slab_parts, "ep", split_axis=0, concat_axis=0, tiled=True)
    expert_out = jnp.sum(
        returned.reshape(experts, SLABS, capacity, model_width).astype(jnp.float32), axis=1
    )
    moe = jnp.dot(
        mixing,
        expert_out.reshape(experts * capacity, model_width),
        precision=lax.Precision.HIGHEST,
        preferred_element_type=jnp.float32,
    )
    return (mixed + moe).astype(jnp.bfloat16)


def solution(mesh):
    placed = (
        P(("groups", "ep"), None),
        P(("groups", "ep"), None, None),
        P(("groups", "ep"), None, None),
        P(("groups", "ep")),
        P("ep", None, None),
        P("ep", None),
        P(),
        P(("groups", "ep"), None),
        P(("groups", "ep"), None),
        P(),
        P(None, "ep"),
        P(None, "ep"),
        P("ep", None),
    )
    return jax.shard_map(
        on_device, mesh=mesh, in_specs=placed, out_specs=P(("groups", "ep"), None), check_vma=False
    )
```

profile of v0, /device:TPU:0, one launch (start us, length us, event | category | flops | bytes accessed | tf_op | source)
XLA Modules:
  0.0 390.4 jit_solution(5512663426129898294)
XLA Ops:
  6.5 0.0 copy-start
  6.5 0.0 copy-start.11
  6.5 0.0 reduce-scatter.2.cloned.1.call-start
  6.5 2.8 convolution_multiply_fusion
  9.4 0.0 copy-done.11
  9.4 0.0 slice-start
  9.4 2.2 fusion.47
  11.6 0.0 copy-done.2
  11.7 0.0 slice-start.1
  11.7 0.8 fusion.10
  12.5 0.0 copy-start.10
  12.5 0.6 copy.31
  13.1 33.3 %all_to_all.28 = bf16[8,128,512]{2,0,1:T(8,128)(2,1)S(1)} all-to-all(bf16[8,128,512]{2,0,1:T(8,128)(2,1)S(1)} %copy.31), channel_id=1, replica_groups=mesh['groups'=1,'ep'=32] {'ep'}, dimensions={1} | all-to-all | bytes 2097152 | tf_op jit(solution)/shard_map/all_to_all | solution.py:44
  46.4 0.0 copy-done.10
  46.4 0.5 convolution_convert_fusion.2
  46.9 0.0 slice-done
  47.0 0.0 slice-done.1
  47.0 5.1 %fusion.48 = f32[256,7168]{1,0:T(8,128)} fusion(bf16[256,512]{0,1:T(8,128)(2,1)S(1)} %bitcast.45, bf16[512,7168]{1,0:T(8,128)(2,1)S(1)} %bitcast.43), kind=kOutput, calls=%fused_computation.57 | convolution fusion | flops 1879048192 | bytes 14942208 | tf_op jit(solution)/shard_map/dot_general | solution.py:50
  52.1 0.0 copy-start.5
  52.1 0.0 reduce-scatter.2.cloned.1.call-update
  52.1 0.6 copy-done.7
  52.7 0.0 copy-done.9
  52.7 0.1 select_reduce_fusion.3
  52.8 0.1 copy.34
  52.9 0.1 eq.45
  53.0 0.1 fusion.43
  53.1 0.2 select_reduce_fusion.2
  53.3 0.1 reduce_sum.68
  53.4 0.1 copy.35
  53.4 0.0 copy-done.6
  53.5 0.0 copy-done.8
  53.5 0.1 convert_reduce_fusion.1
  53.6 144.6 %reduce-scatter.2.cloned.1.call-done = f32[8,7168]{1,0:T(8,128)} async-done(((f32[256,7168]{1,0:T(8,128)}), f32[8,7168]{1,0:T(8,128)}) %reduce-scatter.2.cloned.1.call-update) | async-done | bytes 229392 | tf_op jit(solution)/shard_map/reduce_scatter | solution.py:49
  198.2 0.0 copy-done.5
  198.2 1.1 multiply_reduce_fusion
  199.3 1.3 fusion.2
  200.6 0.4 broadcast_in_dim.38
  201.0 0.0 copy-start.4
  201.0 84.8 %all_to_all.29 = bf16[32,8,7168]{2,1,0:T(8,128)(2,1)S(1)} all-to-all(bf16[32,8,7168]{2,1,0:T(8,128)(2,1)S(1)} %bitcast.41), channel_id=1, replica_groups=mesh['groups'=1,'ep'=32] {'ep'}, dimensions={0} | all-to-all | bytes 7340032 | tf_op jit(solution)/shard_map/all_to_all | solution.py:79
  285.8 1.8 copy-done.1
  287.6 0.0 copy-done.4
  287.6 1.2 fusion.6
  288.8 0.0 copy-done
  288.8 6.6 %fusion.1 = bf16[32,8,7168]{2,1,0:T(8,128)(2,1)} fusion(bf16[128,7168]{1,0:T(8,128)(2,1)S(1)} %copy-done, bf16[7168,128]{1,0:T(8,128)(2,1)} %param.24, bf16[32,8,7168]{2,1,0:T(8,128)(2,1)} %copy-done.1, f32[256,128]{1,0:T(8,128)S(1)} %fusion.6), kind=kOutput, calls=%fused_computation.2 | convolution fusion | flops 941555712 | bytes 11141120 | tf_op jit(solution)/shard_map/dot_general | solution.py:85
  295.4 86.0 %all_to_all.30 = bf16[32,8,7168]{2,1,0:T(8,128)(2,1)S(1)} all-to-all(bf16[32,8,7168]{2,1,0:T(8,128)(2,1)} %fusion.1), channel_id=1, replica_groups=mesh['groups'=1,'ep'=32] {'ep'}, dimensions={0} | all-to-all | bytes 7340032 | tf_op jit(solution)/shard_map/all_to_all | solution.py:89
  381.4 0.6 convert_reduce_fusion
  382.0 0.4 copy-done.3
  382.4 1.2 fusion.3
  (12 shorter events, 0.1 us)
Async XLA Ops:
  6.5 282.3 %copy-start = (bf16[128,7168]{1,0:T(8,128)(2,1)S(1)}, bf16[128,7168]{1,0:T(8,128)(2,1)}, u32[]{:S(2)}) copy-start(bf16[128,7168]{1,0:T(8,128)(2,1)} %param.25) | copy-start | bytes 5505028
  6.5 2.8 copy-start.11
  6.5 191.6 %reduce-scatter.2.cloned.1.call-start = ((), (), s32[]{:S(2)}) async-start(), calls=%async_computation.4 | async-start | bytes 7569408 | tf_op jit(solution)/shard_map/reduce_scatter | solution.py:49
  6.5 5.1 %copy-start.2 = (bf16[8,256,576]{1,2,0:T(8,128)(2,1)S(1)}, bf16[8,256,576]{1,2,0:T(8,128)(2,1)}, u32[]{:S(2)}) copy-start(bf16[8,256,576]{1,2,0:T(8,128)(2,1)} %param.15) | copy-start | bytes 7077892
  9.4 37.6 %slice-start = ((s8[7340032]{0:T(1024)(128)(4,1)}), s8[4194304]{0:T(1024)(128)(4,1)S(1)}, s32[]{:S(2)}) async-start(s8[7340032]{0:T(1024)(128)(4,1)} %bitcast.42), calls=%async_computation.5 | async-start | bytes 8388608
  11.7 35.3 %slice-start.1 = ((s8[7340032]{0:T(1024)(128)(4,1)}), s8[3145728]{0:T(1024)(128)(4,1)S(1)}, s32[]{:S(2)}) async-start(s8[7340032]{0:T(1024)(128)(4,1)} %bitcast.42), calls=%async_computation.6 | async-start | bytes 6291456
  12.5 33.9 %copy-start.10 = (bf16[4,512,128]{2,1,0:T(8,128)(2,1)S(1)}, bf16[4,512,128]{2,1,0:T(8,128)(2,1)}, u32[]{:S(2)}) copy-start(bf16[4,512,128]{2,1,0:T(8,128)(2,1)} %param.17) | copy-start | bytes 1572868
  52.0 0.7 copy-start.7
  52.1 0.7 copy-start.9
  52.1 1.4 copy-start.6
  52.1 1.4 copy-start.8
  52.1 146.1 %copy-start.5 = (bf16[8,7168]{1,0:T(8,128)(2,1)S(1)}, bf16[8,7168]{1,0:T(8,128)(2,1)}, u32[]{:S(2)}) copy-start(bf16[8,7168]{1,0:T(8,128)(2,1)} %param.13) | copy-start | bytes 344068
  201.0 86.6 %copy-start.4 = (bf16[7168,128]{1,0:T(8,128)(2,1)S(1)}, bf16[7168,128]{1,0:T(8,128)(2,1)}, u32[]{:S(2)}) copy-start(bf16[7168,128]{1,0:T(8,128)(2,1)} %param.23) | copy-start | bytes 5505028
  285.8 1.8 copy-start.1
  381.4 0.9 copy-start.3
Sparse Core Ops, SparseCore 0:
  52.2 145.8 reduce-scatter.1
where the time goes:
time: 391 us; the launch traced here: 390 us
  blocking collectives  204 us (52%)
  waiting for transfers between devices  145 us (37%)
  matrix products  19.4 us (5%)
  between operations  13.6 us (3%)
  other arithmetic  4.39 us (1%)
  local copies, waits for them, and re-layouts  4.17 us (1%)
    reduce_scatter x1, waiting for transfers between devices, on_device(): lax.psum_scatter(jnp.dot(flat_values, out_proj, preferred_element_type=jn...  145 us
    all_to_all x1, blocking collectives, on_device(): lax.all_to_all(slab_parts, 'ep', split_axis=0, concat_axis=0, tiled=True)  86 us
    all_to_all x1, blocking collectives, on_device(): lax.all_to_all(outgoing, 'ep', split_axis=0, concat_axis=0, tiled=True)  84.8 us
    all_to_all x1, blocking collectives, on_device(): lax.all_to_all(latent_out, 'ep', split_axis=1, concat_axis=0, tiled=True)  33.3 us
  transfers between devices with their start and end apart: 1, of which 1 were waited for; matrix products, arithmetic and copies ran while one was open for 0% of the time, Pallas kernels for 0%

commit v1 on v0

v1 whole, which is shorter than its diff:
```python
import jax
import jax.numpy as jnp
import numpy as np
from jax import lax
from jax.sharding import PartitionSpec as P

LATENT = 512
SLABS = 8
F32 = jnp.float32
BF16 = jnp.bfloat16

score_scale = 192.0 ** (-0.5)
norm_eps = 1e-06

CORE, AX, AY = 1, 2, 4


def attend(queries, cache, lengths):
    scores = jnp.einsum("bhr,bpr->bhp", queries, cache, preferred_element_type=F32) * score_scale
    live_mask = lax.broadcasted_iota(jnp.int32, scores.shape, 2) < lengths[:, None, None]
    row_max = jnp.max(jnp.where(live_mask, scores, -jnp.inf), axis=2, keepdims=True)
    raised = jnp.where(live_mask, jnp.exp(scores - row_max), 0.0)
    probs_bf = (raised / jnp.sum(raised, axis=2, keepdims=True)).astype(BF16)
    return jnp.einsum(
        "bhp,bpl->bhl", probs_bf, cache[:, :, :LATENT], preferred_element_type=F32
    ).astype(BF16)


def relative_order(first, second, planes):
    return np.array(
        [
            z * SLABS + b * second + a * first + c
            for c in (0, 1)
            for a in (0, 1)
            for b in (0, 1)
            for z in range(planes)
        ],
        np.int32,
    )


def on_device(devices):
    planes = devices // SLABS

    def swap(x, mask):
        return lax.ppermute(x, "ep", [(i, i ^ mask) for i in range(devices)])

    def halve(x, mask):
        half = x.shape[0] // 2
        return x[:half] + swap(x[half:].astype(BF16), mask).astype(F32)

    def sum_to_owner(product, rows):
        outs = []
        sent = [swap(product(g, 1).astype(BF16), CORE) for g in (0, 1)]
        for g, (first, second) in enumerate(((AX, AY), (AY, AX))):
            x = product(g, 0) + sent[g].astype(F32)
            x = halve(x, first)
            outs.append(halve(x, second))
        x = jnp.concatenate(outs, axis=1)
        total = x[:rows]
        for d in range(1, planes):
            total = total + swap(x[d * rows : (d + 1) * rows].astype(BF16), d * SLABS).astype(F32)
        return total

    def to_all(x, cut):
        x = jnp.concatenate([x] + [swap(x, d * SLABS) for d in range(1, planes)], axis=0)
        groups = []
        for part, (first, second) in zip((x[:, :cut], x[:, cut:]), ((AX, AY), (AY, AX))):
            for mask in (second, first, CORE):
                part = jnp.concatenate([part, swap(part, mask)], axis=0)
            groups.append(part)
        return groups

    def body(
        hidden, queries, cache, lengths, value_up, out_proj, norm_gain,
        routes, gates, expert_slot, w_gate, w_up, w_down,
    ):
        rows, width = hidden.shape
        half = width // 2
        me = lax.axis_index("ep")
        orders = [relative_order(AX, AY, planes), relative_order(AY, AX, planes)]
        experts = expert_slot.shape[0]
        labels = jnp.arange(experts, dtype=jnp.int32)
        physical = jnp.sum(
            jnp.where(routes[:, :, None] == labels, expert_slot[None, None, :], 0), axis=2
        )
        weights = jnp.sum(
            jnp.where(physical[:, :, None] == labels, gates[:, :, None], 0.0), axis=1
        )
        pieces = []
        for _ in range(3):
            piece = lax.reduce_precision(weights, 8, 7)
            pieces.append(piece.astype(BF16))
            weights = weights - piece
        tail = jnp.pad(jnp.concatenate(pieces, axis=1), ((0, 0), (0, 128 - 3 * experts)))
        places = [jnp.bitwise_xor(jnp.asarray(order), me) for order in orders]

        latent_out = attend(queries, cache, lengths)
        by_heads = lax.all_to_all(latent_out, "ep", split_axis=1, concat_axis=0, tiled=True)
        head_values = jnp.einsum(
            "bhl,hlv->bhv", by_heads, value_up, preferred_element_type=F32
        ).astype(BF16)
        flat_values = head_values.reshape(head_values.shape[0], -1)
        total_rows = flat_values.shape[0]
        picks = []
        for place in places:
            wanted = (place[:, None] * rows + jnp.arange(rows, dtype=jnp.int32)).reshape(-1, 1)
            pick = (wanted == jnp.arange(total_rows, dtype=jnp.int32)[None, :]).astype(BF16)
            picks.append(jnp.dot(pick, flat_values, preferred_element_type=F32).astype(BF16))
        cut = total_rows // 2

        def out_part(g, part):
            return jnp.dot(
                picks[g][part * cut : (part + 1) * cut],
                out_proj[:, g * half : (g + 1) * half],
                preferred_element_type=F32,
            )

        mixed = hidden.astype(F32) + sum_to_owner(out_part, rows)
        scale_rows = lax.rsqrt(jnp.mean(mixed * mixed, axis=1, keepdims=True) + norm_eps)
        normed = (mixed * scale_rows * norm_gain.astype(F32)).astype(BF16)

        tokens = to_all(jnp.concatenate([normed, tail], axis=1), half)
        tails = tokens[1][:, half : half + 3 * experts].astype(F32)
        tokens = [tokens[0], tokens[1][:, :half]]

        def turn(x):
            return x.reshape(2, 2, 2, planes * rows, -1).swapaxes(1, 2).reshape(total_rows, -1)

        def act(w):
            a, b = (
                jnp.dot(tokens[g], w[g * half : (g + 1) * half], preferred_element_type=F32)
                for g in (0, 1)
            )
            return a + turn(b)

        mine = lax.broadcasted_iota(jnp.int32, tails.shape, 1) % experts == me // SLABS
        weight_b = jnp.sum(jnp.where(mine, tails, 0.0), axis=1, keepdims=True)
        weight_rows = [turn(weight_b), weight_b]
        inner = (jax.nn.silu(act(w_gate)) * act(w_up)).astype(BF16)
        inners = [inner, turn(inner)]

        def down_part(g, part):
            span = slice(part * cut, (part + 1) * cut)
            return weight_rows[g][span] * jnp.dot(
                inners[g][span], w_down[:, g * half : (g + 1) * half], preferred_element_type=F32
            )

        return (mixed + sum_to_owner(down_part, rows)).astype(BF16)

    return body


def solution(mesh):
    placed = (
        P(("groups", "ep"), None),
        P(("groups", "ep"), None, None),
        P(("groups", "ep"), None, None),
        P(("groups", "ep")),
        P("ep", None, None),
        P("ep", None),
        P(),
        P(("groups", "ep"), None),
        P(("groups", "ep"), None),
        P(),
        P(None, "ep"),
        P(None, "ep"),
        P("ep", None),
    )
    return jax.shard_map(
        on_device(mesh.shape["ep"]),
        mesh=mesh,
        in_specs=placed,
        out_specs=P(("groups", "ep"), None),
        check_vma=False,
    )
```

time: 391 us -> 187 us (0.48)
  blocking collectives: 204 us -> 0 us
  waiting for transfers between devices: 145 us -> 107 us
  starting transfers between devices: 0.01 us -> 36.5 us
  between operations: 13.6 us -> 0.55 us
  matrix products: 19.4 us -> 28.4 us
  other arithmetic: 4.39 us -> 9.15 us
    all_to_all x3 -> x0, blocking collectives: 204 us -> none  [the longest x1 86 us: on_device(): lax.all_to_all(slab_parts, 'ep', split_axis=0, concat_axis=0, tiled=True)]
    reduce_scatter x1 -> x0, waiting for transfers between devices: 145 us -> none  [on_device(): lax.psum_scatter(jnp.dot(flat_values, out_proj, preferred_element_type=jn...]
    ppermute x0 -> x27, waiting for transfers between devices: none -> 81 us  [swap(): return lax.ppermute(x, 'ep', [(i, i ^ mask) for i in range(devices)])]
    ppermute x0 -> x27, starting transfers between devices: none -> 29.2 us  [swap(): return lax.ppermute(x, 'ep', [(i, i ^ mask) for i in range(devices)])]
    all_to_all x0 -> x1, waiting for transfers between devices: none -> 25.9 us  [body(): lax.all_to_all(latent_out, 'ep', split_axis=1, concat_axis=0, tiled=True)]
    dot_general x7 -> x16, matrix products: 18.6 us -> 27.6 us  [the longest x4 10.3 us: out_part(): jnp.dot(picks[g][part * cut:(part + 1) * cut], out_proj[:, g * half:(g +...]
    all_to_all x0 -> x1, starting transfers between devices: none -> 7.3 us  [body(): lax.all_to_all(latent_out, 'ep', split_axis=1, concat_axis=0, tiled=True)]
  transfers between devices with their start and end apart: 1 -> 28, of which waited for: 1 -> 22; matrix products, arithmetic and copies ran while one was open for 0% -> 13% of each run, Pallas kernels for 0% -> 0%
where the time goes in v1:
time: 187 us; the launch traced here: 186 us
  waiting for transfers between devices  107 us (57%)
  starting transfers between devices  36.5 us (20%)
  matrix products  28.4 us (15%)
  other arithmetic  9.15 us (5%)
  local copies, waits for them, and re-layouts  4.63 us (2%)
    ppermute x27, waiting for transfers between devices, swap(): return lax.ppermute(x, 'ep', [(i, i ^ mask) for i in range(devices)])  81 us
    ppermute x27, starting transfers between devices, swap(): return lax.ppermute(x, 'ep', [(i, i ^ mask) for i in range(devices)])  29.2 us
    all_to_all x1, waiting for transfers between devices, body(): lax.all_to_all(latent_out, 'ep', split_axis=1, concat_axis=0, tiled=True)  25.9 us
    dot_general x4, matrix products, out_part(): jnp.dot(picks[g][part * cut:(part + 1) * cut], out_proj[:, g * half:(g +...  10.3 us
    dot_general x4, matrix products, act(): jnp.dot(tokens[g], w[g * half:(g + 1) * half], preferred_element_type=F32)  8.21 us
    all_to_all x1, starting transfers between devices, body(): lax.all_to_all(latent_out, 'ep', split_axis=1, concat_axis=0, tiled=True)  7.3 us
    dot_general x4, matrix products, down_part(): jnp.dot(inners[g][span], w_down[:, g * half:(g + 1) * half], preferred_el...  5.77 us
  transfers between devices with their start and end apart: 28, of which 22 were waited for; matrix products, arithmetic and copies ran while one was open for 13% of the time, Pallas kernels for 0%

profile of v1, /device:TPU:0, one launch (start us, length us, event | category | flops | bytes accessed | tf_op | source)
XLA Modules:
  0.0 186.1 jit_solution(4170020027395468527)
XLA Ops:
  0.0 1.3 copy-done
  1.3 2.3 %convolution_multiply_fusion.4 = f32[8,128,256]{2,1,0:T(8,128)S(1)} fusion(bf16[8,128,576]{1,2,0:T(8,128)(2,1)S(1)} %copy-done, bf16[8,256,576]{1,2,0:T(8,128)(2,1)} %param.17), kind=kOutput, calls=%fused_computation.26 | convolution fusion | flops 302252032 | bytes 4587520 | tf_op jit(solution)/shard_map/bhr,bpr->bhp/dot_general | solution.py:19
  3.6 2.2 %fusion.86 = (f32[8,128]{1,0:T(8,128)S(1)}, f32[8,128,256]{2,1,0:T(8,128)S(1)}) fusion(f32[8,128,256]{2,1,0:T(8,128)S(1)} %convolution_multiply_fusion.4, s32[8]{0:T(128)S(1)} %copy-done.15), kind=kOutput, calls=%fused_computation.146 | output fusion | flops 1573119 | bytes 2101280 | tf_op jit(solution)/shard_map/sub | solution.py:22
  6.7 1.6 copy.45
  8.3 7.3 %all-to-all-start = ((bf16[8,128,512]{2,0,1:T(8,128)(2,1)}), bf16[8,128,512]{2,0,1:T(8,128)(2,1)S(1)}, u32[]{:S(2)}, u32[]{:S(2)}) async-start(bf16[8,128,512]{2,0,1:T(8,128)(2,1)} %copy.45), calls=%async_computation | async-start | bytes 2097152 | tf_op jit(solution)/shard_map/all_to_all | solution.py:99
  16.0 25.9 %all-to-all-done = bf16[8,128,512]{2,0,1:T(8,128)(2,1)S(1)} async-done(((bf16[8,128,512]{2,0,1:T(8,128)(2,1)}), bf16[8,128,512]{2,0,1:T(8,128)(2,1)S(1)}, u32[]{:S(2)}, u32[]{:S(2)}) %all-to-all-start) | async-done | bytes 1048608 | tf_op jit(solution)/shard_map/all_to_all | solution.py:99
  42.6 3.1 %convolution_convert_fusion = bf16[128,3584]{1,0:T(8,128)(2,1)S(1)} fusion(bf16[512,7168]{1,0:T(8,128)(2,1)} %param.20, bf16[256,512]{1,0:T(8,128)(2,1)S(1)} %convolution_convert_fusion.2), kind=kOutput, calls=%fused_computation.7 | convolution fusion | flops 470220800 | bytes 4718592 | tf_op jit(solution)/shard_map/dot_general | solution.py:113
  46.1 3.6 %convolution_convert_fusion.1 = bf16[128,3584]{1,0:T(8,128)(2,1)} fusion(bf16[512,7168]{1,0:T(8,128)(2,1)} %param.20, bf16[256,512]{1,0:T(8,128)(2,1)S(1)} %convolution_convert_fusion.3), kind=kOutput, calls=%fused_computation.8 | convolution fusion | flops 470220800 | bytes 4718592 | tf_op jit(solution)/shard_map/dot_general | solution.py:113
  51.8 1.5 collective-permute-start.4
  53.4 2.9 %convert_add_fusion.3 = f32[128,3584]{1,0:T(8,128)S(1)} fusion(bf16[128,3584]{1,0:T(8,128)(2,1)} %collective-permute-done, bf16[512,7168]{1,0:T(8,128)(2,1)} %param.20, bf16[256,512]{1,0:T(8,128)(2,1)S(1)} %convolution_convert_fusion.3), kind=kOutput, calls=%fused_computation.24 | convolution fusion | flops 470679552 | bytes 6553600 | tf_op jit(solution)/shard_map/dot_general | solution.py:113
  56.4 1.5 collective-permute-start.1
  58.0 6.6 %collective-permute-done.4 = bf16[64,3584]{1,0:T(8,128)(2,1)} collective-permute-done((bf16[64,3584]{1,0:T(8,128)(2,1)}, bf16[64,3584]{1,0:T(8,128)(2,1)}, u32[]{:S(2)}, u32[]{:S(2)}) %collective-permute-start.4) | collective-permute-done | bytes 458784 | tf_op jit(solution)/shard_map/ppermute | solution.py:46
  65.7 1.5 collective-permute-start.5
  67.2 2.4 %collective-permute-done.1 = bf16[64,3584]{1,0:T(8,128)(2,1)S(1)} collective-permute-done((bf16[64,3584]{1,0:T(8,128)(2,1)S(1)}, bf16[64,3584]{1,0:T(8,128)(2,1)S(1)}, u32[]{:S(2)}, u32[]{:S(2)}) %collective-permute-start.1) | collective-permute-done | bytes 458784 | tf_op jit(solution)/shard_map/ppermute | solution.py:46
  70.8 2.8 %collective-permute-done.5 = bf16[32,3584]{1,0:T(8,128)(2,1)S(1)} collective-permute-done((bf16[32,3584]{1,0:T(8,128)(2,1)S(1)}, bf16[32,3584]{1,0:T(8,128)(2,1)S(1)}, u32[]{:S(2)}, u32[]{:S(2)}) %collective-permute-start.5) | collective-permute-done | bytes 229408 | tf_op jit(solution)/shard_map/ppermute | solution.py:46
  73.6 2.3 %collective-permute-done.2 = bf16[32,3584]{1,0:T(8,128)(2,1)S(1)} collective-permute-done((bf16[32,3584]{1,0:T(8,128)(2,1)S(1)}, bf16[32,3584]{1,0:T(8,128)(2,1)S(1)}, u32[]{:S(2)}, u32[]{:S(2)}) %collective-permute-start.2) | collective-permute-done | bytes 229408 | tf_op jit(solution)/shard_map/ppermute | solution.py:46
  76.2 2.1 %collective-permute-start.8 = (bf16[8,7168]{1,0:T(8,128)(2,1)S(1)}, bf16[8,7168]{1,0:T(8,128)(2,1)S(1)}, u32[]{:S(2)}, u32[]{:S(2)}) collective-permute-start(bf16[8,7168]{1,0:T(8,128)(2,1)S(1)} %get-tuple-element.11), channel_id=1, source_target_pairs={{0,24},{1,25},{2,26},{3,27},{4,28},{5,29},{6,30},{7,31},{8,16},{9,... | collective-permute-start | bytes 344072 | tf_op jit(solution)/shard_map/ppermute | solution.py:46
  79.7 2.1 %collective-permute-done.6 = bf16[8,7168]{1,0:T(8,128)(2,1)S(1)} collective-permute-done((bf16[8,7168]{1,0:T(8,128)(2,1)S(1)}, bf16[8,7168]{1,0:T(8,128)(2,1)S(1)}, u32[]{:S(2)}, u32[]{:S(2)}) %collective-permute-start.6) | collective-permute-done | bytes 114720 | tf_op jit(solution)/shard_map/ppermute | solution.py:46
  81.7 1.7 collective-permute-done.8
  83.4 4.7 %collective-permute-done.7 = bf16[8,7168]{1,0:T(8,128)(2,1)S(1)} collective-permute-done((bf16[8,7168]{1,0:T(8,128)(2,1)S(1)}, bf16[8,7168]{1,0:T(8,128)(2,1)S(1)}, u32[]{:S(2)}, u32[]{:S(2)}) %collective-permute-start.7) | collective-permute-done | bytes 114720 | tf_op jit(solution)/shard_map/ppermute | solution.py:46
  88.5 1.7 collective-permute-start.11
  90.2 2.8 %collective-permute-start.9 = (bf16[8,7296]{1,0:T(8,128)(2,1)S(1)}, bf16[8,7296]{1,0:T(8,128)(2,1)S(1)}, u32[]{:S(2)}, u32[]{:S(2)}) collective-permute-start(bf16[8,7296]{1,0:T(8,128)(2,1)S(1)} %pad_maximum_fusion.16), channel_id=1, source_target_pairs={{0,8},{1,9},{2,10},{3,11},{4,12},{5,13},{6,14},{7,15},{8,0},{9,1},... | collective-permute-start | bytes 350216 | tf_op jit(solution)/shard_map/ppermute | solution.py:46
  92.9 2.4 %collective-permute-done.11 = bf16[8,7296]{1,0:T(8,128)(2,1)S(1)} collective-permute-done((bf16[8,7296]{1,0:T(8,128)(2,1)S(1)}, bf16[8,7296]{1,0:T(8,128)(2,1)S(1)}, u32[]{:S(2)}, u32[]{:S(2)}) %collective-permute-start.11) | collective-permute-done | bytes 116768 | tf_op jit(solution)/shard_map/ppermute | solution.py:46
  95.3 3.3 %collective-permute-done.10 = bf16[8,7296]{1,0:T(8,128)(2,1)S(1)} collective-permute-done((bf16[8,7296]{1,0:T(8,128)(2,1)S(1)}, bf16[8,7296]{1,0:T(8,128)(2,1)S(1)}, u32[]{:S(2)}, u32[]{:S(2)}) %collective-permute-start.10) | collective-permute-done | bytes 116768 | tf_op jit(solution)/shard_map/ppermute | solution.py:46
  98.7 1.7 collective-permute-start.12
  100.4 4.9 %collective-permute-done.12 = bf16[32,3712]{1,0:T(8,128)(2,1)S(1)} collective-permute-done((bf16[32,3712]{1,0:T(8,128)(2,1)S(1)}, bf16[32,3712]{1,0:T(8,128)(2,1)S(1)}, u32[]{:S(2)}, u32[]{:S(2)}) %collective-permute-start.12) | collective-permute-done | bytes 237600 | tf_op jit(solution)/shard_map/ppermute | solution.py:46
  105.3 2.5 %collective-permute-start.13 = (bf16[64,3712]{1,0:T(8,128)(2,1)S(1)}, bf16[64,3712]{1,0:T(8,128)(2,1)S(1)}, u32[]{:S(2)}, u32[]{:S(2)}) collective-permute-start(bf16[64,3712]{1,0:T(8,128)(2,1)S(1)} %pad_maximum_fusion.8), channel_id=1, source_target_pairs={{0,4},{1,5},{2,6},{3,7},{4,0},{5,1},{6,2},{7,3},{8,12},{9,13},{10,... | collective-permute-start | bytes 1425416 | tf_op jit(solution)/shard_map/ppermute | solution.py:46
  107.9 11.7 %collective-permute-done.13 = bf16[64,3712]{1,0:T(8,128)(2,1)S(1)} collective-permute-done((bf16[64,3712]{1,0:T(8,128)(2,1)S(1)}, bf16[64,3712]{1,0:T(8,128)(2,1)S(1)}, u32[]{:S(2)}, u32[]{:S(2)}) %collective-permute-start.13) | collective-permute-done | bytes 475168 | tf_op jit(solution)/shard_map/ppermute | solution.py:46
  120.6 1.5 collective-permute-done.15
  124.0 10.6 %collective-permute-done.16 = bf16[64,3584]{1,0:T(8,128)(2,1)S(1)} collective-permute-done((bf16[64,3584]{1,0:T(8,128)(2,1)}, bf16[64,3584]{1,0:T(8,128)(2,1)S(1)}, u32[]{:S(2)}, u32[]{:S(2)}) %collective-permute-start.16) | collective-permute-done | bytes 458784 | tf_op jit(solution)/shard_map/ppermute | solution.py:46
  136.8 2.3 %fusion.26 = f32[256,128]{1,0:T(8,128)S(1)} fusion(bf16[7168,128]{1,0:T(8,128)(2,1)} %param.26, bf16[128,3712]{1,0:T(8,128)(2,1)} %collective-permute-done.14, bf16[64,3712]{1,0:T(8,128)(2,1)S(1)} %collective-permute-done.13, bf16[32,3712]{1,0:T(8,128)(2,1)S(1)} %collective-permute-done.12, bf16[32,3712]{1,0:T(8,128)(2,1)S(1)} %slice.243), kind=kOutput, calls=%fused_computation.59 | convolution fusion | flops 242221056 | bytes 2949120 | tf_op jit(solution)/shard_map/dot_general | solution.py:132
  139.1 1.8 fusion.29
  141.0 2.0 %convolution_add_fusion.1 = f32[256,128]{1,0:T(8,128)S(1)} fusion(f32[256,128]{1,0:T(8,128)S(1)} %bitcast.45, bf16[7168,128]{1,0:T(8,128)(2,1)S(1)} %copy-done.12, bf16[128,3584]{1,0:T(8,128)(2,1)} %collective-permute-done.17, bf16[64,3584]{1,0:T(8,128)(2,1)S(1)} %collective-permute-done.16, bf16[32,3584]{1,0:T(8,128)(2,1)S(1)} %collective-permute-done.15, ...), kind=kOutput, calls=%fused_computation.36 | convolution fusion | flops 242253824 | bytes 3014656 | tf_op jit(solution)/shard_map/dot_general | solution.py:132
  143.0 2.1 %multiply_convert_fusion.1 = bf16[256,128]{1,0:T(8,128)(2,1)S(1)} fusion(f32[256,128]{1,0:T(8,128)S(1)} %convolution_add_fusion.1, f32[256,128]{1,0:T(8,128)S(1)} %bitcast.44, bf16[7168,128]{1,0:T(8,128)(2,1)S(1)} %copy-done.13, bf16[128,3584]{1,0:T(8,128)(2,1)} %collective-permute-done.17, bf16[64,3584]{1,0:T(8,128)(2,1)} %copy-done.4, ...), kind=kOutput, calls=%fused_computation.103 | convolution fusion | flops 242450432 | bytes 3080192 | tf_op jit(solution)/shard_map/dot_general | solution.py:132
  145.1 1.3 fusion.1
  147.0 1.3 fusion.2
  149.4 1.6 convert_add_fusion.1
  152.2 1.6 convert_add_fusion
  153.8 1.8 collective-permute-start.22
  155.6 8.3 %collective-permute-done.19 = bf16[64,3584]{1,0:T(8,128)(2,1)S(1)} collective-permute-done((bf16[64,3584]{1,0:T(8,128)(2,1)S(1)}, bf16[64,3584]{1,0:T(8,128)(2,1)S(1)}, u32[]{:S(2)}, u32[]{:S(2)}) %collective-permute-start.19) | collective-permute-done | bytes 458784 | tf_op jit(solution)/shard_map/ppermute | solution.py:46
  164.0 1.8 collective-permute-start.20
  167.6 3.7 %collective-permute-done.20 = bf16[32,3584]{1,0:T(8,128)(2,1)S(1)} collective-permute-done((bf16[32,3584]{1,0:T(8,128)(2,1)S(1)}, bf16[32,3584]{1,0:T(8,128)(2,1)S(1)}, u32[]{:S(2)}, u32[]{:S(2)}) %collective-permute-start.20) | collective-permute-done | bytes 229408 | tf_op jit(solution)/shard_map/ppermute | solution.py:46
  171.3 2.0 %collective-permute-done.23 = bf16[32,3584]{1,0:T(8,128)(2,1)S(1)} collective-permute-done((bf16[32,3584]{1,0:T(8,128)(2,1)S(1)}, bf16[32,3584]{1,0:T(8,128)(2,1)S(1)}, u32[]{:S(2)}, u32[]{:S(2)}) %collective-permute-start.23) | collective-permute-done | bytes 229408 | tf_op jit(solution)/shard_map/ppermute | solution.py:46
  173.5 1.7 collective-permute-start.26
  175.3 1.7 collective-permute-start.25
  177.0 2.9 %collective-permute-done.24 = bf16[8,7168]{1,0:T(8,128)(2,1)S(1)} collective-permute-done((bf16[8,7168]{1,0:T(8,128)(2,1)S(1)}, bf16[8,7168]{1,0:T(8,128)(2,1)S(1)}, u32[]{:S(2)}, u32[]{:S(2)}) %collective-permute-start.24) | collective-permute-done | bytes 114720 | tf_op jit(solution)/shard_map/ppermute | solution.py:46
  179.9 1.3 collective-permute-done.26
  181.2 4.2 %collective-permute-done.25 = bf16[8,7168]{1,0:T(8,128)(2,1)S(1)} collective-permute-done((bf16[8,7168]{1,0:T(8,128)(2,1)S(1)}, bf16[8,7168]{1,0:T(8,128)(2,1)S(1)}, u32[]{:S(2)}, u32[]{:S(2)}) %collective-permute-start.25) | collective-permute-done | bytes 114720 | tf_op jit(solution)/shard_map/ppermute | solution.py:46
  (121 shorter events, 19.7 us)
Async XLA Ops:
  0.0 1.3 copy-start
  0.0 3.6 %copy-start.15 = (s32[8]{0:T(128)S(1)}, s32[8]{0:T(128)}, u32[]{:S(2)}) copy-start(s32[8]{0:T(128)} %param.18) | copy-start | bytes 100
  3.6 2.3 %copy-start.2 = (bf16[8,256,576]{1,2,0:T(8,128)(2,1)S(1)}, bf16[8,256,576]{1,2,0:T(8,128)(2,1)}, u32[]{:S(2)}) copy-start(bf16[8,256,576]{1,2,0:T(8,128)(2,1)} %param.17) | copy-start | bytes 7077892
  6.7 8.9 %copy-start.10 = (s32[32]{0:T(128)S(1)}, s32[32]{0:T(128)}, u32[]{:S(2)}) copy-start(s32[32]{0:T(128)} %constant.58.clone) | copy-start | bytes 388
  6.7 8.9 %copy-start.11 = (s32[32]{0:T(128)S(1)}, s32[32]{0:T(128)}, u32[]{:S(2)}) copy-start(s32[32]{0:T(128)} %constant.57.clone) | copy-start | bytes 388
  6.7 35.1 %copy-start.14 = (bf16[4,512,128]{2,1,0:T(8,128)(2,1)S(1)}, bf16[4,512,128]{2,1,0:T(8,128)(2,1)}, u32[]{:S(2)}) copy-start(bf16[4,512,128]{2,1,0:T(8,128)(2,1)} %param.19) | copy-start | bytes 1572868
  8.3 33.5 %all-to-all-start = ((bf16[8,128,512]{2,0,1:T(8,128)(2,1)}), bf16[8,128,512]{2,0,1:T(8,128)(2,1)S(1)}, u32[]{:S(2)}, u32[]{:S(2)}) async-start(bf16[8,128,512]{2,0,1:T(8,128)(2,1)} %copy.45), calls=%async_computation | async-start | bytes 2097152 | tf_op jit(solution)/shard_map/all_to_all | solution.py:99
  41.9 8.5 %slice-start = ((s8[7340032]{0:T(1024)(128)(4,1)}), s8[4194304]{0:T(1024)(128)(4,1)S(1)}, s32[]{:S(2)}) async-start(s8[7340032]{0:T(1024)(128)(4,1)} %bitcast.35), calls=%async_computation.1 | async-start | bytes 8388608
  42.6 7.7 %slice-start.1 = ((s8[7340032]{0:T(1024)(128)(4,1)}), s8[3145728]{0:T(1024)(128)(4,1)S(1)}, s32[]{:S(2)}) async-start(s8[7340032]{0:T(1024)(128)(4,1)} %bitcast.35), calls=%async_computation.2 | async-start | bytes 6291456
  45.7 4.6 %collective-permute-start.3 = (bf16[128,3584]{1,0:T(8,128)(2,1)S(1)}, bf16[128,3584]{1,0:T(8,128)(2,1)S(1)}, u32[]{:S(2)}, u32[]{:S(2)}) collective-permute-start(bf16[128,3584]{1,0:T(8,128)(2,1)S(1)} %convolution_convert_fusion), channel_id=1, source_target_pairs={{0,1},{1,0},{2,3},{3,2},{4,5},{5,4},{6,7},{7,6},{8,9},{9,8},{10,11... | collective-permute-start | bytes 2752520 | tf_op jit(solution)/shard_map/ppermute | solution.py:46
  46.1 4.2 %copy-start.7 = (s32[8,2]{0,1:T(2,128)S(1)}, s32[8,2]{0,1:T(2,128)}, u32[]{:S(2)}) copy-start(s32[8,2]{0,1:T(2,128)} %param.22) | copy-start | bytes 196
  46.1 4.2 %copy-start.9 = (s32[4]{0:T(128)S(1)}, s32[4]{0:T(128)}, u32[]{:S(2)}) copy-start(s32[4]{0:T(128)} %param.24) | copy-start | bytes 52
  49.7 3.7 %collective-permute-start = (bf16[128,3584]{1,0:T(8,128)(2,1)}, bf16[128,3584]{1,0:T(8,128)(2,1)}, u32[]{:S(2)}, u32[]{:S(2)}) collective-permute-start(bf16[128,3584]{1,0:T(8,128)(2,1)} %convolution_convert_fusion.1), channel_id=1, source_target_pairs={{0,1},{1,0},{2,3},{3,2},{4,5},{5,4},{6,7},{7,6},{8,9},{9,8},{10,11... | collective-permute-start | bytes 2752520 | tf_op jit(solution)/shard_map/ppermute | solution.py:46
  50.3 3.0 %copy-start.8 = (f32[8,2]{0,1:T(2,128)S(1)}, f32[8,2]{0,1:T(2,128)}, u32[]{:S(2)}) copy-start(f32[8,2]{0,1:T(2,128)} %param.23) | copy-start | bytes 196
  51.8 12.8 %collective-permute-start.4 = (bf16[64,3584]{1,0:T(8,128)(2,1)}, bf16[64,3584]{1,0:T(8,128)(2,1)}, u32[]{:S(2)}, u32[]{:S(2)}) collective-permute-start(bf16[64,3584]{1,0:T(8,128)(2,1)} %slice.361), channel_id=1, source_target_pairs={{0,4},{1,5},{2,6},{3,7},{4,0},{5,1},{6,2},{7,3},{8,12},{9,13},{10,... | collective-permute-start | bytes 1376264 | tf_op jit(solution)/shard_map/ppermute | solution.py:46
  56.4 13.2 %collective-permute-start.1 = (bf16[64,3584]{1,0:T(8,128)(2,1)S(1)}, bf16[64,3584]{1,0:T(8,128)(2,1)S(1)}, u32[]{:S(2)}, u32[]{:S(2)}) collective-permute-start(bf16[64,3584]{1,0:T(8,128)(2,1)S(1)} %slice.362), channel_id=1, source_target_pairs={{0,2},{1,3},{2,0},{3,1},{4,6},{5,7},{6,4},{7,5},{8,10},{9,11},{10,... | collective-permute-start | bytes 1376264 | tf_op jit(solution)/shard_map/ppermute | solution.py:46
  65.7 7.8 %collective-permute-start.5 = (bf16[32,3584]{1,0:T(8,128)(2,1)S(1)}, bf16[32,3584]{1,0:T(8,128)(2,1)S(1)}, u32[]{:S(2)}, u32[]{:S(2)}) collective-permute-start(bf16[32,3584]{1,0:T(8,128)(2,1)S(1)} %slice.365), channel_id=1, source_target_pairs={{0,2},{1,3},{2,0},{3,1},{4,6},{5,7},{6,4},{7,5},{8,10},{9,11},{10,... | collective-permute-start | bytes 688136 | tf_op jit(solution)/shard_map/ppermute | solution.py:46
  69.8 6.1 %collective-permute-start.2 = (bf16[32,3584]{1,0:T(8,128)(2,1)S(1)}, bf16[32,3584]{1,0:T(8,128)(2,1)S(1)}, u32[]{:S(2)}, u32[]{:S(2)}) collective-permute-start(bf16[32,3584]{1,0:T(8,128)(2,1)S(1)} %slice.366), channel_id=1, source_target_pairs={{0,4},{1,5},{2,6},{3,7},{4,0},{5,1},{6,2},{7,3},{8,12},{9,13},{10,... | collective-permute-start | bytes 688136 | tf_op jit(solution)/shard_map/ppermute | solution.py:46
  73.6 6.0 %copy-start.6 = (bf16[7168]{0:T(1024)(128)(2,1)S(1)}, bf16[7168]{0:T(1024)(128)(2,1)}, u32[]{:S(2)}) copy-start(bf16[7168]{0:T(1024)(128)(2,1)} %param.21) | copy-start | bytes 43012
  73.6 14.5 %copy-start.5 = (bf16[8,7168]{1,0:T(8,128)(2,1)S(1)}, bf16[8,7168]{1,0:T(8,128)(2,1)}, u32[]{:S(2)}) copy-start(bf16[8,7168]{1,0:T(8,128)(2,1)} %param.15) | copy-start | bytes 344068
  76.0 5.7 %collective-permute-start.6 = (bf16[8,7168]{1,0:T(8,128)(2,1)S(1)}, bf16[8,7168]{1,0:T(8,128)(2,1)S(1)}, u32[]{:S(2)}, u32[]{:S(2)}) collective-permute-start(bf16[8,7168]{1,0:T(8,128)(2,1)S(1)} %get-tuple-element.10), channel_id=1, source_target_pairs={{0,8},{1,9},{2,10},{3,11},{4,12},{5,13},{6,14},{7,15},{8,0},{9,1},... | collective-permute-start | bytes 344072 | tf_op jit(solution)/shard_map/ppermute | solution.py:46
  76.2 7.2 %collective-permute-start.8 = (bf16[8,7168]{1,0:T(8,128)(2,1)S(1)}, bf16[8,7168]{1,0:T(8,128)(2,1)S(1)}, u32[]{:S(2)}, u32[]{:S(2)}) collective-permute-start(bf16[8,7168]{1,0:T(8,128)(2,1)S(1)} %get-tuple-element.11), channel_id=1, source_target_pairs={{0,24},{1,25},{2,26},{3,27},{4,28},{5,29},{6,30},{7,31},{8,16},{9,... | collective-permute-start | bytes 344072 | tf_op jit(solution)/shard_map/ppermute | solution.py:46
  78.3 9.8 %collective-permute-start.7 = (bf16[8,7168]{1,0:T(8,128)(2,1)S(1)}, bf16[8,7168]{1,0:T(8,128)(2,1)S(1)}, u32[]{:S(2)}, u32[]{:S(2)}) collective-permute-start(bf16[8,7168]{1,0:T(8,128)(2,1)S(1)} %get-tuple-element.12), channel_id=1, source_target_pairs={{0,16},{1,17},{2,18},{3,19},{4,20},{5,21},{6,22},{7,23},{8,24},{9,... | collective-permute-start | bytes 344072 | tf_op jit(solution)/shard_map/ppermute | solution.py:46
  88.5 6.9 %collective-permute-start.11 = (bf16[8,7296]{1,0:T(8,128)(2,1)S(1)}, bf16[8,7296]{1,0:T(8,128)(2,1)S(1)}, u32[]{:S(2)}, u32[]{:S(2)}) collective-permute-start(bf16[8,7296]{1,0:T(8,128)(2,1)S(1)} %pad_maximum_fusion.16), channel_id=1, source_target_pairs={{0,24},{1,25},{2,26},{3,27},{4,28},{5,29},{6,30},{7,31},{8,16},{9,... | collective-permute-start | bytes 350216 | tf_op jit(solution)/shard_map/ppermute | solution.py:46
  90.2 8.4 %collective-permute-start.10 = (bf16[8,7296]{1,0:T(8,128)(2,1)S(1)}, bf16[8,7296]{1,0:T(8,128)(2,1)S(1)}, u32[]{:S(2)}, u32[]{:S(2)}) collective-permute-start(bf16[8,7296]{1,0:T(8,128)(2,1)S(1)} %pad_maximum_fusion.16), channel_id=1, source_target_pairs={{0,16},{1,17},{2,18},{3,19},{4,20},{5,21},{6,22},{7,23},{8,24},{9,... | collective-permute-start | bytes 350216 | tf_op jit(solution)/shard_map/ppermute | solution.py:46
  90.2 8.4 %collective-permute-start.9 = (bf16[8,7296]{1,0:T(8,128)(2,1)S(1)}, bf16[8,7296]{1,0:T(8,128)(2,1)S(1)}, u32[]{:S(2)}, u32[]{:S(2)}) collective-permute-start(bf16[8,7296]{1,0:T(8,128)(2,1)S(1)} %pad_maximum_fusion.16), channel_id=1, source_target_pairs={{0,8},{1,9},{2,10},{3,11},{4,12},{5,13},{6,14},{7,15},{8,0},{9,1},... | collective-permute-start | bytes 350216 | tf_op jit(solution)/shard_map/ppermute | solution.py:46
  98.7 6.6 %collective-permute-start.12 = (bf16[32,3712]{1,0:T(8,128)(2,1)S(1)}, bf16[32,3712]{1,0:T(8,128)(2,1)S(1)}, u32[]{:S(2)}, u32[]{:S(2)}) collective-permute-start(bf16[32,3712]{1,0:T(8,128)(2,1)S(1)} %slice.243), channel_id=1, source_target_pairs={{0,2},{1,3},{2,0},{3,1},{4,6},{5,7},{6,4},{7,5},{8,10},{9,11},{10,... | collective-permute-start | bytes 712712 | tf_op jit(solution)/shard_map/ppermute | solution.py:46
  105.3 14.2 %collective-permute-start.13 = (bf16[64,3712]{1,0:T(8,128)(2,1)S(1)}, bf16[64,3712]{1,0:T(8,128)(2,1)S(1)}, u32[]{:S(2)}, u32[]{:S(2)}) collective-permute-start(bf16[64,3712]{1,0:T(8,128)(2,1)S(1)} %pad_maximum_fusion.8), channel_id=1, source_target_pairs={{0,4},{1,5},{2,6},{3,7},{4,0},{5,1},{6,2},{7,3},{8,12},{9,13},{10,... | collective-permute-start | bytes 1425416 | tf_op jit(solution)/shard_map/ppermute | solution.py:46
  107.8 14.2 %collective-permute-start.15 = (bf16[32,3584]{1,0:T(8,128)(2,1)S(1)}, bf16[32,3584]{1,0:T(8,128)(2,1)S(1)}, u32[]{:S(2)}, u32[]{:S(2)}) collective-permute-start(bf16[32,3584]{1,0:T(8,128)(2,1)S(1)} %pad_maximum_fusion.15), channel_id=1, source_target_pairs={{0,4},{1,5},{2,6},{3,7},{4,0},{5,1},{6,2},{7,3},{8,12},{9,13},{10,... | collective-permute-start | bytes 688136 | tf_op jit(solution)/shard_map/ppermute | solution.py:46
  120.6 15.1 %collective-permute-start.14 = (bf16[128,3712]{1,0:T(8,128)(2,1)}, bf16[128,3712]{1,0:T(8,128)(2,1)}, u32[]{:S(2)}, u32[]{:S(2)}) collective-permute-start(bf16[128,3712]{1,0:T(8,128)(2,1)} %pad_maximum_fusion.6), channel_id=1, source_target_pairs={{0,1},{1,0},{2,3},{3,2},{4,5},{5,4},{6,7},{7,6},{8,9},{9,8},{10,11... | collective-permute-start | bytes 2850824 | tf_op jit(solution)/shard_map/ppermute | solution.py:46
  122.1 18.9 %copy-start.3 = (bf16[32,3584]{1,0:T(8,128)(2,1)}, bf16[32,3584]{1,0:T(8,128)(2,1)S(1)}, u32[]{:S(2)}) copy-start(bf16[32,3584]{1,0:T(8,128)(2,1)S(1)} %collective-permute-done.15) | copy-start | bytes 688132
  122.9 11.7 %collective-permute-start.16 = (bf16[64,3584]{1,0:T(8,128)(2,1)}, bf16[64,3584]{1,0:T(8,128)(2,1)S(1)}, u32[]{:S(2)}, u32[]{:S(2)}) collective-permute-start(bf16[64,3584]{1,0:T(8,128)(2,1)} %pad_maximum_fusion.10), channel_id=1, source_target_pairs={{0,2},{1,3},{2,0},{3,1},{4,6},{5,7},{6,4},{7,5},{8,10},{9,11},{10,... | collective-permute-start | bytes 1376264 | tf_op jit(solution)/shard_map/ppermute | solution.py:46
  134.6 6.3 %copy-start.4 = (bf16[64,3584]{1,0:T(8,128)(2,1)}, bf16[64,3584]{1,0:T(8,128)(2,1)S(1)}, u32[]{:S(2)}) copy-start(bf16[64,3584]{1,0:T(8,128)(2,1)S(1)} %collective-permute-done.16) | copy-start | bytes 1376260
  135.7 5.2 %collective-permute-start.17 = (bf16[128,3584]{1,0:T(8,128)(2,1)}, bf16[128,3584]{1,0:T(8,128)(2,1)}, u32[]{:S(2)}, u32[]{:S(2)}) collective-permute-start(bf16[128,3584]{1,0:T(8,128)(2,1)} %pad_maximum_fusion.7), channel_id=1, source_target_pairs={{0,1},{1,0},{2,3},{3,2},{4,5},{5,4},{6,7},{7,6},{8,9},{9,8},{10,11... | collective-permute-start | bytes 2752520 | tf_op jit(solution)/shard_map/ppermute | solution.py:46
  136.8 2.3 %copy-start.12 = (bf16[7168,128]{1,0:T(8,128)(2,1)S(1)}, bf16[7168,128]{1,0:T(8,128)(2,1)}, u32[]{:S(2)}) copy-start(bf16[7168,128]{1,0:T(8,128)(2,1)} %param.25) | copy-start | bytes 5505028
  141.0 2.0 %copy-start.13 = (bf16[7168,128]{1,0:T(8,128)(2,1)S(1)}, bf16[7168,128]{1,0:T(8,128)(2,1)}, u32[]{:S(2)}) copy-start(bf16[7168,128]{1,0:T(8,128)(2,1)} %param.26) | copy-start | bytes 5505028
  143.0 2.2 %copy-start.1 = (bf16[128,7168]{1,0:T(8,128)(2,1)S(1)}, bf16[128,7168]{1,0:T(8,128)(2,1)}, u32[]{:S(2)}) copy-start(bf16[128,7168]{1,0:T(8,128)(2,1)} %param.27) | copy-start | bytes 5505028
  146.5 2.9 %collective-permute-start.18 = (bf16[128,3584]{1,0:T(8,128)(2,1)}, bf16[128,3584]{1,0:T(8,128)(2,1)}, u32[]{:S(2)}, u32[]{:S(2)}) collective-permute-start(bf16[128,3584]{1,0:T(8,128)(2,1)} %fusion.1), channel_id=1, source_target_pairs={{0,1},{1,0},{2,3},{3,2},{4,5},{5,4},{6,7},{7,6},{8,9},{9,8},{10,11... | collective-permute-start | bytes 2752520 | tf_op jit(solution)/shard_map/ppermute | solution.py:46
  148.3 3.9 %collective-permute-start.21 = (bf16[128,3584]{1,0:T(8,128)(2,1)}, bf16[128,3584]{1,0:T(8,128)(2,1)}, u32[]{:S(2)}, u32[]{:S(2)}) collective-permute-start(bf16[128,3584]{1,0:T(8,128)(2,1)} %fusion.2), channel_id=1, source_target_pairs={{0,1},{1,0},{2,3},{3,2},{4,5},{5,4},{6,7},{7,6},{8,9},{9,8},{10,11... | collective-permute-start | bytes 2752520 | tf_op jit(solution)/shard_map/ppermute | solution.py:46
  151.0 12.9 %collective-permute-start.19 = (bf16[64,3584]{1,0:T(8,128)(2,1)S(1)}, bf16[64,3584]{1,0:T(8,128)(2,1)S(1)}, u32[]{:S(2)}, u32[]{:S(2)}) collective-permute-start(bf16[64,3584]{1,0:T(8,128)(2,1)S(1)} %slice.360), channel_id=1, source_target_pairs={{0,2},{1,3},{2,0},{3,1},{4,6},{5,7},{6,4},{7,5},{8,10},{9,11},{10,... | collective-permute-start | bytes 1376264 | tf_op jit(solution)/shard_map/ppermute | solution.py:46
  153.8 12.6 %collective-permute-start.22 = (bf16[64,3584]{1,0:T(8,128)(2,1)S(1)}, bf16[64,3584]{1,0:T(8,128)(2,1)S(1)}, u32[]{:S(2)}, u32[]{:S(2)}) collective-permute-start(bf16[64,3584]{1,0:T(8,128)(2,1)S(1)} %slice.359), channel_id=1, source_target_pairs={{0,4},{1,5},{2,6},{3,7},{4,0},{5,1},{6,2},{7,3},{8,12},{9,13},{10,... | collective-permute-start | bytes 1376264 | tf_op jit(solution)/shard_map/ppermute | solution.py:46
  164.0 7.3 %collective-permute-start.20 = (bf16[32,3584]{1,0:T(8,128)(2,1)S(1)}, bf16[32,3584]{1,0:T(8,128)(2,1)S(1)}, u32[]{:S(2)}, u32[]{:S(2)}) collective-permute-start(bf16[32,3584]{1,0:T(8,128)(2,1)S(1)} %slice.364), channel_id=1, source_target_pairs={{0,4},{1,5},{2,6},{3,7},{4,0},{5,1},{6,2},{7,3},{8,12},{9,13},{10,... | collective-permute-start | bytes 688136 | tf_op jit(solution)/shard_map/ppermute | solution.py:46
  166.6 6.7 %collective-permute-start.23 = (bf16[32,3584]{1,0:T(8,128)(2,1)S(1)}, bf16[32,3584]{1,0:T(8,128)(2,1)S(1)}, u32[]{:S(2)}, u32[]{:S(2)}) collective-permute-start(bf16[32,3584]{1,0:T(8,128)(2,1)S(1)} %slice.363), channel_id=1, source_target_pairs={{0,2},{1,3},{2,0},{3,1},{4,6},{5,7},{6,4},{7,5},{8,10},{9,11},{10,... | collective-permute-start | bytes 688136 | tf_op jit(solution)/shard_map/ppermute | solution.py:46
  173.4 6.4 %collective-permute-start.24 = (bf16[8,7168]{1,0:T(8,128)(2,1)S(1)}, bf16[8,7168]{1,0:T(8,128)(2,1)S(1)}, u32[]{:S(2)}, u32[]{:S(2)}) collective-permute-start(bf16[8,7168]{1,0:T(8,128)(2,1)S(1)} %get-tuple-element.7), channel_id=1, source_target_pairs={{0,8},{1,9},{2,10},{3,11},{4,12},{5,13},{6,14},{7,15},{8,0},{9,1},... | collective-permute-start | bytes 344072 | tf_op jit(solution)/shard_map/ppermute | solution.py:46
  173.5 7.6 %collective-permute-start.26 = (bf16[8,7168]{1,0:T(8,128)(2,1)S(1)}, bf16[8,7168]{1,0:T(8,128)(2,1)S(1)}, u32[]{:S(2)}, u32[]{:S(2)}) collective-permute-start(bf16[8,7168]{1,0:T(8,128)(2,1)S(1)} %get-tuple-element.8), channel_id=1, source_target_pairs={{0,24},{1,25},{2,26},{3,27},{4,28},{5,29},{6,30},{7,31},{8,16},{9,... | collective-permute-start | bytes 344072 | tf_op jit(solution)/shard_map/ppermute | solution.py:46
  175.3 10.1 %collective-permute-start.25 = (bf16[8,7168]{1,0:T(8,128)(2,1)S(1)}, bf16[8,7168]{1,0:T(8,128)(2,1)S(1)}, u32[]{:S(2)}, u32[]{:S(2)}) collective-permute-start(bf16[8,7168]{1,0:T(8,128)(2,1)S(1)} %get-tuple-element.9), channel_id=1, source_target_pairs={{0,16},{1,17},{2,18},{3,19},{4,20},{5,21},{6,22},{7,23},{8,24},{9,... | collective-permute-start | bytes 344072 | tf_op jit(solution)/shard_map/ppermute | solution.py:46

commit v2 on v1

v2 whole, which is shorter than its diff:
```python
import jax
import jax.numpy as jnp
import numpy as np
from jax import lax
from jax.sharding import PartitionSpec as P

LATENT = 512
SLABS = 8
F32 = jnp.float32
BF16 = jnp.bfloat16

score_scale = 192.0 ** (-0.5)
norm_eps = 1e-06

CORE, AX, AY = 1, 2, 4


def attend(queries, cache, lengths):
    scores = jnp.einsum("bhr,bpr->bhp", queries, cache, preferred_element_type=F32) * score_scale
    live_mask = lax.broadcasted_iota(jnp.int32, scores.shape, 2) < lengths[:, None, None]
    row_max = jnp.max(jnp.where(live_mask, scores, -jnp.inf), axis=2, keepdims=True)
    raised = jnp.where(live_mask, jnp.exp(scores - row_max), 0.0)
    probs_bf = (raised / jnp.sum(raised, axis=2, keepdims=True)).astype(BF16)
    return jnp.einsum(
        "bhp,bpl->bhl", probs_bf, cache[:, :, :LATENT], preferred_element_type=F32
    ).astype(BF16)


def relative_order(first, second, planes):
    return np.array(
        [
            z * SLABS + b * second + a * first
            for a in (0, 1)
            for b in (0, 1)
            for z in range(planes)
        ],
        np.int32,
    )


def on_device(devices):
    planes = devices // SLABS
    chips = devices // 2
    axes = ((AX, AY), (AY, AX))

    def swap(x, mask):
        return lax.ppermute(x, "ep", [(i, i ^ mask) for i in range(devices)])

    def sum_to_owner(product, rows):
        sent = [swap(product(g, 1).astype(BF16), axes[g][0]) for g in (0, 1)]
        outs = []
        for g in (0, 1):
            x = product(g, 0) + sent[g].astype(F32)
            half = x.shape[0] // 2
            outs.append(x[:half] + swap(x[half:].astype(BF16), axes[g][1]).astype(F32))
        x = jnp.concatenate(outs, axis=1)
        total = x[:rows]
        for d in range(1, planes):
            total = total + swap(x[d * rows : (d + 1) * rows].astype(BF16), d * SLABS).astype(F32)
        return total

    def to_all(x, cut):
        x = jnp.concatenate([x] + [swap(x, d * SLABS) for d in range(1, planes)], axis=0)
        near = [
            jnp.concatenate([part, swap(part, axes[g][1])], axis=0)
            for g, part in enumerate((x[:, :cut], x[:, cut:]))
        ]
        return [(near[g], swap(near[g], axes[g][0])) for g in (0, 1)]

    def body(
        hidden, queries, cache, lengths, value_up, out_proj, norm_gain,
        routes, gates, expert_slot, w_gate, w_up, w_down,
    ):
        rows, width = hidden.shape
        half = width // 2
        me = lax.axis_index("ep")
        core = me % 2
        value_up_other = swap(value_up, CORE)
        out_proj_other = swap(out_proj, CORE)
        w_gate_other, w_up_other, w_down_other = (swap(w, CORE) for w in (w_gate, w_up, w_down))

        latent_out = attend(queries, cache, lengths)
        by_heads = lax.all_to_all(
            latent_out, "ep", split_axis=1, concat_axis=0, tiled=True,
            axis_index_groups=[list(range(c, devices, 2)) for c in (0, 1)],
        )

        orders = [relative_order(first, second, planes) for first, second in axes]
        experts = expert_slot.shape[0]
        labels = jnp.arange(experts, dtype=jnp.int32)
        physical = jnp.sum(
            jnp.where(routes[:, :, None] == labels, expert_slot[None, None, :], 0), axis=2
        )
        weights = jnp.sum(
            jnp.where(physical[:, :, None] == labels, gates[:, :, None], 0.0), axis=1
        )
        pieces = []
        for _ in range(3):
            piece = lax.reduce_precision(weights, 8, 7)
            pieces.append(piece.astype(BF16))
            weights = weights - piece
        tail = jnp.pad(jnp.concatenate(pieces, axis=1), ((0, 0), (0, 128 - 3 * experts)))

        even = core == 0
        heads_up = jnp.concatenate(
            [
                jnp.where(even, value_up, value_up_other),
                jnp.where(even, value_up_other, value_up),
            ],
            axis=0,
        )
        head_values = jnp.einsum(
            "bhl,hlv->bhv", by_heads, heads_up, preferred_element_type=F32
        ).astype(BF16)
        total_rows = head_values.shape[0]
        flat_values = head_values.reshape(total_rows, 2, -1)
        flat_values = jnp.concatenate(
            [
                jnp.where(even, flat_values[:, 0], flat_values[:, 1]),
                jnp.where(even, flat_values[:, 1], flat_values[:, 0]),
            ],
            axis=1,
        )
        picks = []
        for order in orders:
            place = jnp.bitwise_xor(jnp.asarray(order), me) // 2
            wanted = (place[:, None] * rows + jnp.arange(rows, dtype=jnp.int32)).reshape(-1, 1)
            pick = (wanted == jnp.arange(total_rows, dtype=jnp.int32)[None, :]).astype(BF16)
            picks.append(jnp.dot(pick, flat_values, preferred_element_type=F32).astype(BF16))
        cut = total_rows // 2
        own_rows = out_proj.shape[0]

        def out_part(g, part):
            x = picks[g][part * cut : (part + 1) * cut]
            span = slice(g * half, (g + 1) * half)
            return jnp.dot(
                x[:, :own_rows], out_proj[:, span], preferred_element_type=F32
            ) + jnp.dot(x[:, own_rows:], out_proj_other[:, span], preferred_element_type=F32)

        mixed = hidden.astype(F32) + sum_to_owner(out_part, rows)
        scale_rows = lax.rsqrt(jnp.mean(mixed * mixed, axis=1, keepdims=True) + norm_eps)
        normed = (mixed * scale_rows * norm_gain.astype(F32)).astype(BF16)

        tokens = to_all(jnp.concatenate([normed, tail], axis=1), half)
        tails = jnp.concatenate([t[:, half : half + 3 * experts] for t in tokens[1]], axis=0)
        w_in = jnp.concatenate([w_gate, w_gate_other, w_up, w_up_other], axis=1)
        w_out = jnp.concatenate([w_down, w_down_other], axis=0)

        def turn(x):
            return x.reshape(2, 2, planes * rows, -1).swapaxes(0, 1).reshape(total_rows, -1)

        acts = [
            jnp.concatenate(
                [
                    jnp.dot(
                        t[:, :half], w_in[g * half : (g + 1) * half], preferred_element_type=F32
                    )
                    for t in tokens[g]
                ],
                axis=0,
            )
            for g in (0, 1)
        ]
        acts = acts[0] + turn(acts[1])
        hid = acts.shape[1] // 2
        inner = (jax.nn.silu(acts[:, :hid]) * acts[:, hid:]).astype(BF16)
        inners = [inner, turn(inner)]
        mine = lax.broadcasted_iota(jnp.int32, tails.shape, 1) % experts == me // SLABS
        weight_b = jnp.sum(jnp.where(mine, tails.astype(F32), 0.0), axis=1, keepdims=True)
        weight_rows = [turn(weight_b), weight_b]

        def down_part(g, part):
            span = slice(part * cut, (part + 1) * cut)
            return weight_rows[g][span] * jnp.dot(
                inners[g][span], w_out[:, g * half : (g + 1) * half], preferred_element_type=F32
            )

        return (mixed + sum_to_owner(down_part, rows)).astype(BF16)

    return body


def solution(mesh):
    placed = (
        P(("groups", "ep"), None),
        P(("groups", "ep"), None, None),
        P(("groups", "ep"), None, None),
        P(("groups", "ep")),
        P("ep", None, None),
        P("ep", None),
        P(),
        P(("groups", "ep"), None),
        P(("groups", "ep"), None),
        P(),
        P(None, "ep"),
        P(None, "ep"),
        P("ep", None),
    )
    return jax.shard_map(
        on_device(mesh.shape["ep"]),
        mesh=mesh,
        in_specs=placed,
        out_specs=P(("groups", "ep"), None),
        check_vma=False,
    )
```

time: 187 us -> 159 us (0.85)
  waiting for transfers between devices: 107 us -> 55.6 us
  local copies, waits for them, and re-layouts: 4.63 us -> 15.6 us
  starting transfers between devices: 36.5 us -> 44.6 us
  matrix products: 28.4 us -> 34.8 us
    ppermute x27 -> x26, waiting for transfers between devices: 81 us -> 43.6 us  [swap(): return lax.ppermute(x, 'ep', [(i, i ^ mask) for i in range(devices)])]
    all_to_all x1, waiting for transfers between devices: 25.9 us -> 12 us  [body(): lax.all_to_all(latent_out, 'ep', split_axis=1, concat_axis=0, tiled=True,...]
    unnamed x36 -> x59, local copies, waits for them, and re-layouts: 1.36 us -> 9.42 us
    ppermute x27 -> x26, starting transfers between devices: 29.2 us -> 36.3 us  [swap(): return lax.ppermute(x, 'ep', [(i, i ^ mask) for i in range(devices)])]
    dot_general x13 -> x17, matrix products: 24.8 us -> 31 us  [the longest x4 11.3 us: out_part(): jnp.dot(x[:, own_rows:], out_proj_other[:, span], preferred_element_type=...]
    concatenate x0 -> x2, local copies, waits for them, and re-layouts: none -> 3.55 us  [the longest x1 1.93 us: body(): w_in = jnp.concatenate([w_gate, w_gate_other, w_up, w_up_other], axis=1)]
    concatenate x4, other arithmetic: 3 us -> 0.1 us  [the longest x3 0.08 us: to_all(): jnp.concatenate([part, swap(part, axes[g][1])], axis=0)]
    select_n x0 -> x2, other arithmetic: none -> 2.24 us  [the longest x1 2.22 us: body(): jnp.where(even, value_up, value_up_other)]
  transfers between devices with their start and end apart: 28 -> 27, of which waited for: 22 -> 15; matrix products, arithmetic and copies ran while one was open for 13% -> 32% of each run, Pallas kernels for 0% -> 0%
where the time goes in v2:
time: 159 us
  waiting for transfers between devices  55.6 us (35%)
  starting transfers between devices  44.6 us (28%)
  matrix products  34.8 us (22%)
  local copies, waits for them, and re-layouts  15.6 us (10%)
  other arithmetic  7.59 us (5%)
    ppermute x26, waiting for transfers between devices, swap(): return lax.ppermute(x, 'ep', [(i, i ^ mask) for i in range(devices)])  43.6 us
    ppermute x26, starting transfers between devices, swap(): return lax.ppermute(x, 'ep', [(i, i ^ mask) for i in range(devices)])  36.3 us
    all_to_all x1, waiting for transfers between devices, body(): lax.all_to_all(latent_out, 'ep', split_axis=1, concat_axis=0, tiled=True,...  12 us
    dot_general x4, matrix products, out_part(): jnp.dot(x[:, own_rows:], out_proj_other[:, span], preferred_element_type=...  11.3 us
    unnamed x59, local copies, waits for them, and re-layouts  9.42 us
    all_to_all x1, starting transfers between devices, body(): lax.all_to_all(latent_out, 'ep', split_axis=1, concat_axis=0, tiled=True,...  8.32 us
    dot_general x4, matrix products, out_part(): jnp.dot(x[:, :own_rows], out_proj[:, span], preferred_element_type=F32)  7.32 us
    dot_general x4, matrix products, body(): jnp.dot(t[:, :half], w_in[g * half:(g + 1) * half], preferred_element_typ...  7.18 us
  transfers between devices with their start and end apart: 27, of which 15 were waited for; matrix products, arithmetic and copies ran while one was open for 32% of the time, Pallas kernels for 0%

profile of v2, /device:TPU:0, one launch (start us, length us, event | category | flops | bytes accessed | tf_op | source)
XLA Modules:
  0.0 158.8 jit_solution(16067532648948288361)
XLA Ops:
  0.0 1.3 copy.44
  2.0 2.4 %convolution_multiply_fusion.4 = f32[8,128,256]{2,1,0:T(8,128)S(1)} fusion(bf16[8,128,576]{1,2,0:T(8,128)(2,1)S(1)} %copy-done, bf16[8,256,576]{1,2,0:T(8,128)(2,1)} %param.17), kind=kOutput, calls=%fused_computation.44 | convolution fusion | flops 302252032 | bytes 4587520 | tf_op jit(solution)/shard_map/bhr,bpr->bhp/dot_general | solution.py:19
  4.4 2.2 %fusion.103 = (f32[8,128]{1,0:T(8,128)S(1)}, f32[8,128,256]{2,1,0:T(8,128)S(1)}) fusion(f32[8,128,256]{2,1,0:T(8,128)S(1)} %convolution_multiply_fusion.4, s32[8]{0:T(128)S(1)} %copy-done.22), kind=kOutput, calls=%fused_computation.180 | output fusion | flops 1573119 | bytes 2101280 | tf_op jit(solution)/shard_map/sub | solution.py:22
  7.6 1.7 %copy.47 = bf16[8,128,512]{2,0,1:T(8,128)(2,1)} copy(bf16[8,128,512]{2,1,0:T(8,128)(2,1)S(1)} %fusion.35) | data formatting | bytes 2097152 | tf_op jit(solution)/shard_map/convert_element_type | solution.py:26
  9.2 8.3 %all-to-all-start = ((bf16[8,128,512]{2,0,1:T(8,128)(2,1)}), bf16[8,128,512]{2,0,1:T(8,128)(2,1)S(1)}, u32[]{:S(2)}, u32[]{:S(2)}) async-start(bf16[8,128,512]{2,0,1:T(8,128)(2,1)} %copy.47), calls=%async_computation | async-start | bytes 2097152 | tf_op jit(solution)/shard_map/all_to_all | solution.py:83
  18.4 1.4 constant_dynamic-update-slice_fusion.3
  20.6 1.4 constant_dynamic-update-slice_fusion.5
  23.4 2.2 %broadcast_select_fusion.1 = (bf16[4,512,128]{1,2,0:T(8,128)(2,1)}, bf16[4,512,128]{1,2,0:T(8,128)(2,1)}) fusion(bf16[4,512,128]{1,2,0:T(8,128)(2,1)S(1)} %copy.44, bf16[4,512,128]{1,2,0:T(8,128)(2,1)} %collective-permute-done, pred[]{:T(512)S(6)} %eq.68), kind=kLoop, calls=%fused_computation.77 | loop fusion | flops 524288 | bytes 2097153 | tf_op jit(solution)/shard_map/jit(_where)/select_n | solution.py:107
  25.6 3.1 %constant_dynamic-update-slice_fusion.2 = bf16[7168,512]{1,0:T(8,128)(2,1)} fusion(bf16[7168,512]{1,0:T(8,128)(2,1)} %constant_dynamic-update-slice_fusion.3, bf16[7168,128]{1,0:T(8,128)(2,1)} %collective-permute-done.15), kind=kLoop, calls=%fused_computation.129 | loop fusion | bytes 3670016
  28.7 1.4 constant_dynamic-update-slice_fusion.1
  30.1 12.0 %all-to-all-done = bf16[8,128,512]{2,0,1:T(8,128)(2,1)S(1)} async-done(((bf16[8,128,512]{2,0,1:T(8,128)(2,1)}), bf16[8,128,512]{2,0,1:T(8,128)(2,1)S(1)}, u32[]{:S(2)}, u32[]{:S(2)}) %all-to-all-start) | async-done | bytes 1048608 | tf_op jit(solution)/shard_map/all_to_all | solution.py:83
  43.1 3.0 %fusion.25 = f32[64,3584]{1,0:T(8,128)S(1)} fusion(bf16[512,7168]{1,0:T(8,128)(2,1)} %param.20, bf16[128,1024]{1,0:T(8,128)(2,1)S(1)} %convolution_convert_fusion.2), kind=kOutput, calls=%fused_computation.33 | convolution fusion | flops 234881024 | bytes 4653056 | tf_op jit(solution)/shard_map/dot_general | solution.py:136
  46.2 2.8 %fusion.27 = f32[64,3584]{1,0:T(8,128)S(1)} fusion(bf16[512,7168]{1,0:T(8,128)(2,1)} %param.20, bf16[128,1024]{1,0:T(8,128)(2,1)S(1)} %convolution_convert_fusion.2), kind=kOutput, calls=%fused_computation.35 | convolution fusion | flops 234881024 | bytes 4653056 | tf_op jit(solution)/shard_map/dot_general | solution.py:136
  49.7 2.8 %fusion.5 = bf16[64,3584]{1,0:T(8,128)(2,1)S(1)} fusion(f32[64,3584]{1,0:T(8,128)S(1)} %fusion.25, bf16[512,7168]{1,0:T(8,128)(2,1)} %collective-permute-done.1, bf16[128,1024]{1,0:T(8,128)(2,1)S(1)} %convolution_convert_fusion.2), kind=kOutput, calls=%fused_computation.13 | convolution fusion | flops 235339776 | bytes 5111808 | tf_op jit(solution)/shard_map/dot_general | solution.py:138
  53.2 2.8 %fusion.6 = bf16[64,3584]{1,0:T(8,128)(2,1)S(1)} fusion(f32[64,3584]{1,0:T(8,128)S(1)} %fusion.21, bf16[512,7168]{1,0:T(8,128)(2,1)} %collective-permute-done.1, bf16[128,1024]{1,0:T(8,128)(2,1)S(1)} %convolution_convert_fusion.1), kind=kOutput, calls=%fused_computation.14 | convolution fusion | flops 235339776 | bytes 5111808 | tf_op jit(solution)/shard_map/dot_general | solution.py:138
  56.0 2.0 %collective-permute-start.4 = (bf16[64,3584]{1,0:T(8,128)(2,1)S(1)}, bf16[64,3584]{1,0:T(8,128)(2,1)S(1)}, u32[]{:S(2)}, u32[]{:S(2)}) collective-permute-start(bf16[64,3584]{1,0:T(8,128)(2,1)S(1)} %fusion.6), channel_id=1, source_target_pairs={{0,4},{1,5},{2,6},{3,7},{4,0},{5,1},{6,2},{7,3},{8,12},{9,13},{10,... | collective-permute-start | bytes 1376264 | tf_op jit(solution)/shard_map/ppermute | solution.py:47
  58.8 3.6 %collective-permute-done.2 = bf16[64,3584]{1,0:T(8,128)(2,1)S(1)} collective-permute-done((bf16[64,3584]{1,0:T(8,128)(2,1)S(1)}, bf16[64,3584]{1,0:T(8,128)(2,1)S(1)}, u32[]{:S(2)}, u32[]{:S(2)}) %collective-permute-start.2) | collective-permute-done | bytes 458784 | tf_op jit(solution)/shard_map/ppermute | solution.py:47
  62.3 2.9 %fusion.4 = f32[64,3584]{1,0:T(8,128)S(1)} fusion(f32[64,3584]{1,0:T(8,128)S(1)} %fusion.27, bf16[512,7168]{1,0:T(8,128)(2,1)} %collective-permute-done.1, bf16[64,3584]{1,0:T(8,128)(2,1)S(1)} %collective-permute-done.2, bf16[128,1024]{1,0:T(8,128)(2,1)S(1)} %convolution_convert_fusion.2), kind=kOutput, calls=%fused_computation.12 | convolution fusion | flops 235569152 | bytes 6029312 | tf_op jit(solution)/shard_map/dot_general | solution.py:138
  65.3 2.5 %collective-permute-start.3 = (bf16[32,3584]{1,0:T(8,128)(2,1)S(1)}, bf16[32,3584]{1,0:T(8,128)(2,1)S(1)}, u32[]{:S(2)}, u32[]{:S(2)}) collective-permute-start(bf16[32,3584]{1,0:T(8,128)(2,1)S(1)} %slice.420), channel_id=1, source_target_pairs={{0,4},{1,5},{2,6},{3,7},{4,0},{5,1},{6,2},{7,3},{8,12},{9,13},{10,... | collective-permute-start | bytes 688136 | tf_op jit(solution)/shard_map/ppermute | solution.py:47
  67.8 2.8 %fusion.3 = f32[64,3584]{1,0:T(8,128)S(1)} fusion(f32[64,3584]{1,0:T(8,128)S(1)} %fusion.23, bf16[512,7168]{1,0:T(8,128)(2,1)} %collective-permute-done.1, bf16[64,3584]{1,0:T(8,128)(2,1)S(1)} %collective-permute-done.4, bf16[128,1024]{1,0:T(8,128)(2,1)S(1)} %convolution_convert_fusion.1), kind=kOutput, calls=%fused_computation.9 | convolution fusion | flops 235569152 | bytes 6029312 | tf_op jit(solution)/shard_map/dot_general | solution.py:138
  70.6 1.4 collective-permute-start.5
  72.1 4.7 %collective-permute-done.5 = bf16[32,3584]{1,0:T(8,128)(2,1)S(1)} collective-permute-done((bf16[32,3584]{1,0:T(8,128)(2,1)S(1)}, bf16[32,3584]{1,0:T(8,128)(2,1)S(1)}, u32[]{:S(2)}, u32[]{:S(2)}) %collective-permute-start.5) | collective-permute-done | bytes 229408 | tf_op jit(solution)/shard_map/ppermute | solution.py:47
  76.9 3.4 %collective-permute-start.6 = (bf16[8,7168]{1,0:T(8,128)(2,1)S(1)}, bf16[8,7168]{1,0:T(8,128)(2,1)S(1)}, u32[]{:S(2)}, u32[]{:S(2)}) collective-permute-start(bf16[8,7168]{1,0:T(8,128)(2,1)S(1)} %get-tuple-element.14), channel_id=1, source_target_pairs={{0,8},{1,9},{2,10},{3,11},{4,12},{5,13},{6,14},{7,15},{8,0},{9,1},... | collective-permute-start | bytes 344072 | tf_op jit(solution)/shard_map/ppermute | solution.py:47
  80.3 1.0 collective-permute-start.7
  81.3 1.5 collective-permute-start.8
  82.8 1.9 %constant_dynamic-update-slice_fusion = bf16[7168,512]{1,0:T(8,128)(2,1)S(1)} fusion(bf16[7168,512]{1,0:T(8,128)(2,1)S(1)} %bitcast.34, bf16[7168,128]{1,0:T(8,128)(2,1)} %collective-permute-done.16), kind=kLoop, calls=%fused_computation.127 | loop fusion | bytes 3670016 | tf_op jit(solution)/shard_map/concatenate | solution.py:146
  84.9 4.3 %collective-permute-done.7 = bf16[8,7168]{1,0:T(8,128)(2,1)S(1)} collective-permute-done((bf16[8,7168]{1,0:T(8,128)(2,1)S(1)}, bf16[8,7168]{1,0:T(8,128)(2,1)S(1)}, u32[]{:S(2)}, u32[]{:S(2)}) %collective-permute-start.7) | collective-permute-done | bytes 114720 | tf_op jit(solution)/shard_map/ppermute | solution.py:47
  89.5 4.6 %collective-permute-start.10 = (bf16[8,7296]{1,0:T(8,128)(2,1)S(1)}, bf16[8,7296]{1,0:T(8,128)(2,1)S(1)}, u32[]{:S(2)}, u32[]{:S(2)}) collective-permute-start(bf16[8,7296]{1,0:T(8,128)(2,1)S(1)} %pad_maximum_fusion.10), channel_id=1, source_target_pairs={{0,16},{1,17},{2,18},{3,19},{4,20},{5,21},{6,22},{7,23},{8,24},{9,... | collective-permute-start | bytes 350216 | tf_op jit(solution)/shard_map/ppermute | solution.py:47
  94.0 3.4 %collective-permute-start.11 = (bf16[8,7296]{1,0:T(8,128)(2,1)S(1)}, bf16[8,7296]{1,0:T(8,128)(2,1)S(1)}, u32[]{:S(2)}, u32[]{:S(2)}) collective-permute-start(bf16[8,7296]{1,0:T(8,128)(2,1)S(1)} %pad_maximum_fusion.10), channel_id=1, source_target_pairs={{0,24},{1,25},{2,26},{3,27},{4,28},{5,29},{6,30},{7,31},{8,16},{9,... | collective-permute-start | bytes 350216 | tf_op jit(solution)/shard_map/ppermute | solution.py:47
  97.4 1.6 %constant_dynamic-update-slice_fusion.4 = bf16[256,7168]{1,0:T(8,128)(2,1)S(1)} fusion(bf16[256,7168]{1,0:T(8,128)(2,1)S(1)} %copy-done.2, bf16[128,7168]{1,0:T(8,128)(2,1)} %collective-permute-done.18), kind=kLoop, calls=%fused_computation.131 | loop fusion | bytes 3670016 | tf_op jit(solution)/shard_map/concatenate | solution.py:147
  99.1 2.5 %collective-permute-done.11 = bf16[8,7296]{1,0:T(8,128)(2,1)S(1)} collective-permute-done((bf16[8,7296]{1,0:T(8,128)(2,1)S(1)}, bf16[8,7296]{1,0:T(8,128)(2,1)S(1)}, u32[]{:S(2)}, u32[]{:S(2)}) %collective-permute-start.11) | collective-permute-done | bytes 116768 | tf_op jit(solution)/shard_map/ppermute | solution.py:47
  101.6 1.2 collective-permute-done.9
  103.0 1.9 %collective-permute-start.12 = (bf16[32,3712]{1,0:T(8,128)(2,1)S(1)}, bf16[32,3712]{1,0:T(8,128)(2,1)S(1)}, u32[]{:S(2)}, u32[]{:S(2)}) collective-permute-start(bf16[32,3712]{1,0:T(8,128)(2,1)S(1)} %slice.269), channel_id=1, source_target_pairs={{0,2},{1,3},{2,0},{3,1},{4,6},{5,7},{6,4},{7,5},{8,10},{9,11},{10,... | collective-permute-start | bytes 712712 | tf_op jit(solution)/shard_map/ppermute | solution.py:47
  104.9 6.5 %collective-permute-done.14 = bf16[32,3584]{1,0:T(8,128)(2,1)S(1)} collective-permute-done((bf16[32,3584]{1,0:T(8,128)(2,1)S(1)}, bf16[32,3584]{1,0:T(8,128)(2,1)S(1)}, u32[]{:S(2)}, u32[]{:S(2)}) %collective-permute-start.14) | collective-permute-done | bytes 229408 | tf_op jit(solution)/shard_map/ppermute | solution.py:47
  112.4 1.8 %collective-permute-start.13 = (bf16[64,3712]{1,0:T(8,128)(2,1)S(1)}, bf16[64,3712]{1,0:T(8,128)(2,1)S(1)}, u32[]{:S(2)}, u32[]{:S(2)}) collective-permute-start(bf16[64,3712]{1,0:T(8,128)(2,1)S(1)} %pad_maximum_fusion.2), channel_id=1, source_target_pairs={{0,4},{1,5},{2,6},{3,7},{4,0},{5,1},{6,2},{7,3},{8,12},{9,13},{10,... | collective-permute-start | bytes 1425416 | tf_op jit(solution)/shard_map/ppermute | solution.py:47
  115.0 5.0 %collective-permute-done.17 = bf16[64,3584]{1,0:T(8,128)(2,1)S(1)} collective-permute-done((bf16[64,3584]{1,0:T(8,128)(2,1)S(1)}, bf16[64,3584]{1,0:T(8,128)(2,1)S(1)}, u32[]{:S(2)}, u32[]{:S(2)}) %collective-permute-start.17) | collective-permute-done | bytes 458784 | tf_op jit(solution)/shard_map/ppermute | solution.py:47
  120.0 2.8 %fusion.13 = f32[64,512]{1,0:T(8,128)S(1)} fusion(bf16[64,3584]{1,0:T(8,128)(2,1)S(1)} %collective-permute-done.17, bf16[7168,512]{1,0:T(8,128)(2,1)} %copy-done.12), kind=kOutput, calls=%fused_computation.21 | convolution fusion | flops 234881024 | bytes 4259840 | tf_op jit(solution)/shard_map/dot_general | solution.py:155
  123.2 2.9 %fusion.9 = f32[64,512]{1,0:T(8,128)S(1)} fusion(bf16[7168,512]{1,0:T(8,128)(2,1)} %copy-done.12, bf16[64,3712]{1,0:T(8,128)(2,1)S(1)} %collective-permute-done.13), kind=kOutput, calls=%fused_computation.17 | convolution fusion | flops 234881024 | bytes 4259840 | tf_op jit(solution)/shard_map/dot_general | solution.py:155
  126.8 2.5 %collective-permute-start.21 = (bf16[64,3584]{1,0:T(8,128)(2,1)S(1)}, bf16[64,3584]{1,0:T(8,128)(2,1)S(1)}, u32[]{:S(2)}, u32[]{:S(2)}) collective-permute-start(bf16[64,3584]{1,0:T(8,128)(2,1)S(1)} %fusion.8), channel_id=1, source_target_pairs={{0,4},{1,5},{2,6},{3,7},{4,0},{5,1},{6,2},{7,3},{8,12},{9,13},{10,... | collective-permute-start | bytes 1376264 | tf_op jit(solution)/shard_map/ppermute | solution.py:47
  129.5 1.9 %fusion.7 = bf16[64,3584]{1,0:T(8,128)(2,1)S(1)} fusion(bf16[256,7168]{1,0:T(8,128)(2,1)} %copy-done.3, f32[64]{0:T(128)S(1)} %mul.90, bf16[128,256]{1,0:T(8,128)(2,1)S(1)} %fusion.70), kind=kOutput, calls=%fused_computation.15 | convolution fusion | flops 117899264 | bytes 2327040 | tf_op jit(solution)/shard_map/dot_general | solution.py:174
  132.4 5.9 %collective-permute-done.21 = bf16[64,3584]{1,0:T(8,128)(2,1)S(1)} collective-permute-done((bf16[64,3584]{1,0:T(8,128)(2,1)S(1)}, bf16[64,3584]{1,0:T(8,128)(2,1)S(1)}, u32[]{:S(2)}, u32[]{:S(2)}) %collective-permute-start.21) | collective-permute-done | bytes 458784 | tf_op jit(solution)/shard_map/ppermute | solution.py:47
  138.3 1.9 %fusion.1 = f32[64,3584]{1,0:T(8,128)S(1)} fusion(bf16[64,256]{1,0:T(8,128)(2,1)S(1)} %bitcast.37, bf16[256,7168]{1,0:T(8,128)(2,1)} %copy-done.3, bf16[64,3584]{1,0:T(8,128)(2,1)S(1)} %collective-permute-done.21, f32[64]{0:T(128)S(1)} %get-tuple-element.24), kind=kOutput, calls=%fused_computation.3 | convolution fusion | flops 118128640 | bytes 3244288 | tf_op jit(solution)/shard_map/dot_general | solution.py:174
  140.3 2.2 %collective-permute-start.22 = (bf16[32,3584]{1,0:T(8,128)(2,1)S(1)}, bf16[32,3584]{1,0:T(8,128)(2,1)S(1)}, u32[]{:S(2)}, u32[]{:S(2)}) collective-permute-start(bf16[32,3584]{1,0:T(8,128)(2,1)S(1)} %slice.417), channel_id=1, source_target_pairs={{0,2},{1,3},{2,0},{3,1},{4,6},{5,7},{6,4},{7,5},{8,10},{9,11},{10,... | collective-permute-start | bytes 688136 | tf_op jit(solution)/shard_map/ppermute | solution.py:47
  143.7 2.8 %collective-permute-done.22 = bf16[32,3584]{1,0:T(8,128)(2,1)S(1)} collective-permute-done((bf16[32,3584]{1,0:T(8,128)(2,1)S(1)}, bf16[32,3584]{1,0:T(8,128)(2,1)S(1)}, u32[]{:S(2)}, u32[]{:S(2)}) %collective-permute-start.22) | collective-permute-done | bytes 229408 | tf_op jit(solution)/shard_map/ppermute | solution.py:47
  146.5 2.5 %collective-permute-done.20 = bf16[32,3584]{1,0:T(8,128)(2,1)S(1)} collective-permute-done((bf16[32,3584]{1,0:T(8,128)(2,1)S(1)}, bf16[32,3584]{1,0:T(8,128)(2,1)S(1)}, u32[]{:S(2)}, u32[]{:S(2)}) %collective-permute-start.20) | collective-permute-done | bytes 229408 | tf_op jit(solution)/shard_map/ppermute | solution.py:47
  149.9 1.1 collective-permute-start.24
  151.0 2.6 %collective-permute-start.25 = (bf16[8,7168]{1,0:T(8,128)(2,1)S(1)}, bf16[8,7168]{1,0:T(8,128)(2,1)S(1)}, u32[]{:S(2)}, u32[]{:S(2)}) collective-permute-start(bf16[8,7168]{1,0:T(8,128)(2,1)S(1)} %get-tuple-element.12), channel_id=1, source_target_pairs={{0,24},{1,25},{2,26},{3,27},{4,28},{5,29},{6,30},{7,31},{8,16},{9,... | collective-permute-start | bytes 344072 | tf_op jit(solution)/shard_map/ppermute | solution.py:47
  154.1 4.0 %collective-permute-done.24 = bf16[8,7168]{1,0:T(8,128)(2,1)S(1)} collective-permute-done((bf16[8,7168]{1,0:T(8,128)(2,1)S(1)}, bf16[8,7168]{1,0:T(8,128)(2,1)S(1)}, u32[]{:S(2)}, u32[]{:S(2)}) %collective-permute-start.24) | collective-permute-done | bytes 114720 | tf_op jit(solution)/shard_map/ppermute | solution.py:47
  (144 shorter events, 15.5 us)
Async XLA Ops:
  1.4 22.0 %collective-permute-start = (bf16[4,512,128]{1,2,0:T(8,128)(2,1)S(1)}, bf16[4,512,128]{1,2,0:T(8,128)(2,1)}, u32[]{:S(2)}, u32[]{:S(2)}) collective-permute-start(bf16[4,512,128]{1,2,0:T(8,128)(2,1)S(1)} %copy.44), channel_id=1, source_target_pairs={{0,1},{1,0},{2,3},{3,2},{4,5},{5,4},{6,7},{7,6},{8,9},{9,8},{10,11... | collective-permute-start | bytes 1572872 | tf_op jit(solution)/shard_map/ppermute | solution.py:47
  1.9 47.9 %collective-permute-start.1 = (bf16[512,7168]{1,0:T(8,128)(2,1)}, bf16[512,7168]{1,0:T(8,128)(2,1)}, u32[]{:S(2)}, u32[]{:S(2)}) collective-permute-start(bf16[512,7168]{1,0:T(8,128)(2,1)} %param.20), channel_id=1, source_target_pairs={{0,1},{1,0},{2,3},{3,2},{4,5},{5,4},{6,7},{7,6},{8,9},{9,8},{10,11... | collective-permute-start | bytes 22020104 | tf_op jit(solution)/shard_map/ppermute | solution.py:47
  7.5 10.1 %copy-start.7 = (bf16[7168,128]{1,0:T(8,128)(2,1)S(1)}, bf16[7168,128]{1,0:T(8,128)(2,1)}, u32[]{:S(2)}) copy-start(bf16[7168,128]{1,0:T(8,128)(2,1)} %param.25) | copy-start | bytes 5505028
  7.5 10.7 %copy-start.16 = (s32[8,2]{0,1:T(2,128)S(1)}, s32[8,2]{0,1:T(2,128)}, u32[]{:S(2)}) copy-start(s32[8,2]{0,1:T(2,128)} %param.22) | copy-start | bytes 196
  7.5 10.7 %copy-start.18 = (s32[4]{0:T(128)S(1)}, s32[4]{0:T(128)}, u32[]{:S(2)}) copy-start(s32[4]{0:T(128)} %param.24) | copy-start | bytes 52
  7.5 10.8 %copy-start.17 = (f32[8,2]{0,1:T(2,128)S(1)}, f32[8,2]{0,1:T(2,128)}, u32[]{:S(2)}) copy-start(f32[8,2]{0,1:T(2,128)} %param.23) | copy-start | bytes 196
  7.5 10.9 %copy-start.19 = (s32[16]{0:T(128)S(1)}, s32[16]{0:T(128)}, u32[]{:S(2)}) copy-start(s32[16]{0:T(128)} %constant.85.clone) | copy-start | bytes 196
  7.5 10.9 %copy-start.20 = (s32[16]{0:T(128)S(1)}, s32[16]{0:T(128)}, u32[]{:S(2)}) copy-start(s32[16]{0:T(128)} %constant.86.clone) | copy-start | bytes 196
  9.2 32.9 %all-to-all-start = ((bf16[8,128,512]{2,0,1:T(8,128)(2,1)}), bf16[8,128,512]{2,0,1:T(8,128)(2,1)S(1)}, u32[]{:S(2)}, u32[]{:S(2)}) async-start(bf16[8,128,512]{2,0,1:T(8,128)(2,1)} %copy.47), calls=%async_computation | async-start | bytes 2097152 | tf_op jit(solution)/shard_map/all_to_all | solution.py:83
  17.5 8.0 %collective-permute-start.15 = (bf16[7168,128]{1,0:T(8,128)(2,1)S(1)}, bf16[7168,128]{1,0:T(8,128)(2,1)}, u32[]{:S(2)}, u32[]{:S(2)}) collective-permute-start(bf16[7168,128]{1,0:T(8,128)(2,1)S(1)} %copy-done.7), channel_id=1, source_target_pairs={{0,1},{1,0},{2,3},{3,2},{4,5},{5,4},{6,7},{7,6},{8,9},{9,8},{10,11... | collective-permute-start | bytes 5505032 | tf_op jit(solution)/shard_map/ppermute | solution.py:47
  17.6 65.1 %collective-permute-start.16 = (bf16[7168,128]{1,0:T(8,128)(2,1)}, bf16[7168,128]{1,0:T(8,128)(2,1)}, u32[]{:S(2)}, u32[]{:S(2)}) collective-permute-start(bf16[7168,128]{1,0:T(8,128)(2,1)} %param.26), channel_id=1, source_target_pairs={{0,1},{1,0},{2,3},{3,2},{4,5},{5,4},{6,7},{7,6},{8,9},{9,8},{10,11... | collective-permute-start | bytes 5505032 | tf_op jit(solution)/shard_map/ppermute | solution.py:47
  18.1 79.3 %collective-permute-start.18 = (bf16[128,7168]{1,0:T(8,128)(2,1)}, bf16[128,7168]{1,0:T(8,128)(2,1)}, u32[]{:S(2)}, u32[]{:S(2)}) collective-permute-start(bf16[128,7168]{1,0:T(8,128)(2,1)} %param.27), channel_id=1, source_target_pairs={{0,1},{1,0},{2,3},{3,2},{4,5},{5,4},{6,7},{7,6},{8,9},{9,8},{10,11... | collective-permute-start | bytes 5505032 | tf_op jit(solution)/shard_map/ppermute | solution.py:47
  23.4 5.3 %copy-start.8 = (bf16[7168,128]{1,0:T(8,128)(2,1)S(1)}, bf16[7168,128]{1,0:T(8,128)(2,1)}, u32[]{:S(2)}) copy-start(bf16[7168,128]{1,0:T(8,128)(2,1)} %param.26) | copy-start | bytes 5505028
  25.6 16.5 %copy-start.10 = (bf16[4,512,128]{1,2,0:T(8,128)(2,1)S(1)}, bf16[4,512,128]{1,2,0:T(8,128)(2,1)}, u32[]{:S(2)}) copy-start(bf16[4,512,128]{1,2,0:T(8,128)(2,1)} %get-tuple-element.9) | copy-start | bytes 1572868
  25.6 16.5 %copy-start.11 = (bf16[4,512,128]{1,2,0:T(8,128)(2,1)S(1)}, bf16[4,512,128]{1,2,0:T(8,128)(2,1)}, u32[]{:S(2)}) copy-start(bf16[4,512,128]{1,2,0:T(8,128)(2,1)} %get-tuple-element.10) | copy-start | bytes 1572868
  42.1 6.9 %slice-start = ((s8[7340032]{0:T(1024)(128)(4,1)}), s8[4194304]{0:T(1024)(128)(4,1)S(1)}, s32[]{:S(2)}) async-start(s8[7340032]{0:T(1024)(128)(4,1)} %bitcast.29), calls=%async_computation.1 | async-start | bytes 8388608
  43.1 5.8 %slice-start.1 = ((s8[7340032]{0:T(1024)(128)(4,1)}), s8[3145728]{0:T(1024)(128)(4,1)S(1)}, s32[]{:S(2)}) async-start(s8[7340032]{0:T(1024)(128)(4,1)} %bitcast.29), calls=%async_computation.2 | async-start | bytes 6291456
  52.5 9.8 %collective-permute-start.2 = (bf16[64,3584]{1,0:T(8,128)(2,1)S(1)}, bf16[64,3584]{1,0:T(8,128)(2,1)S(1)}, u32[]{:S(2)}, u32[]{:S(2)}) collective-permute-start(bf16[64,3584]{1,0:T(8,128)(2,1)S(1)} %fusion.5), channel_id=1, source_target_pairs={{0,2},{1,3},{2,0},{3,1},{4,6},{5,7},{6,4},{7,5},{8,10},{9,11},{10,... | collective-permute-start | bytes 1376264 | tf_op jit(solution)/shard_map/ppermute | solution.py:47
  56.0 11.9 %collective-permute-start.4 = (bf16[64,3584]{1,0:T(8,128)(2,1)S(1)}, bf16[64,3584]{1,0:T(8,128)(2,1)S(1)}, u32[]{:S(2)}, u32[]{:S(2)}) collective-permute-start(bf16[64,3584]{1,0:T(8,128)(2,1)S(1)} %fusion.6), channel_id=1, source_target_pairs={{0,4},{1,5},{2,6},{3,7},{4,0},{5,1},{6,2},{7,3},{8,12},{9,13},{10,... | collective-permute-start | bytes 1376264 | tf_op jit(solution)/shard_map/ppermute | solution.py:47
  62.3 20.5 %slice-start.2 = ((s8[7340032]{0:T(1024)(128)(4,1)}), s8[3145728]{0:T(1024)(128)(4,1)S(1)}, s32[]{:S(2)}) async-start(s8[7340032]{0:T(1024)(128)(4,1)} %bitcast.33), calls=%async_computation.3 | async-start | bytes 6291456
  65.3 17.5 %slice-start.3 = ((s8[7340032]{0:T(1024)(128)(4,1)}), s8[4194304]{0:T(1024)(128)(4,1)S(1)}, s32[]{:S(2)}) async-start(s8[7340032]{0:T(1024)(128)(4,1)} %bitcast.33), calls=%async_computation.4 | async-start | bytes 8388608
  65.3 6.7 %collective-permute-start.3 = (bf16[32,3584]{1,0:T(8,128)(2,1)S(1)}, bf16[32,3584]{1,0:T(8,128)(2,1)S(1)}, u32[]{:S(2)}, u32[]{:S(2)}) collective-permute-start(bf16[32,3584]{1,0:T(8,128)(2,1)S(1)} %slice.420), channel_id=1, source_target_pairs={{0,4},{1,5},{2,6},{3,7},{4,0},{5,1},{6,2},{7,3},{8,12},{9,13},{10,... | collective-permute-start | bytes 688136 | tf_op jit(solution)/shard_map/ppermute | solution.py:47
  70.6 6.1 %collective-permute-start.5 = (bf16[32,3584]{1,0:T(8,128)(2,1)S(1)}, bf16[32,3584]{1,0:T(8,128)(2,1)S(1)}, u32[]{:S(2)}, u32[]{:S(2)}) collective-permute-start(bf16[32,3584]{1,0:T(8,128)(2,1)S(1)} %slice.419), channel_id=1, source_target_pairs={{0,2},{1,3},{2,0},{3,1},{4,6},{5,7},{6,4},{7,5},{8,10},{9,11},{10,... | collective-permute-start | bytes 688136 | tf_op jit(solution)/shard_map/ppermute | solution.py:47
  72.0 17.1 %copy-start.13 = (bf16[8,7168]{1,0:T(8,128)(2,1)S(1)}, bf16[8,7168]{1,0:T(8,128)(2,1)}, u32[]{:S(2)}) copy-start(bf16[8,7168]{1,0:T(8,128)(2,1)} %param.15) | copy-start | bytes 344068
  76.8 12.6 %copy-start.14 = (f32[7168]{0:T(1024)S(1)}, f32[7168]{0:T(1024)}, u32[]{:S(2)}) copy-start(f32[7168]{0:T(1024)} %convert_element_type.129) | copy-start | bytes 86020
  76.8 20.6 %copy-start.2 = (bf16[256,7168]{1,0:T(8,128)(2,1)S(1)}, bf16[256,7168]{1,0:T(8,128)(2,1)}, u32[]{:S(2)}) copy-start(bf16[256,7168]{1,0:T(8,128)(2,1)} %constant_dynamic-update-slice_fusion.5) | copy-start | bytes 11010052
  76.9 8.0 %collective-permute-start.6 = (bf16[8,7168]{1,0:T(8,128)(2,1)S(1)}, bf16[8,7168]{1,0:T(8,128)(2,1)S(1)}, u32[]{:S(2)}, u32[]{:S(2)}) collective-permute-start(bf16[8,7168]{1,0:T(8,128)(2,1)S(1)} %get-tuple-element.14), channel_id=1, source_target_pairs={{0,8},{1,9},{2,10},{3,11},{4,12},{5,13},{6,14},{7,15},{8,0},{9,1},... | collective-permute-start | bytes 344072 | tf_op jit(solution)/shard_map/ppermute | solution.py:47
  80.3 8.8 %collective-permute-start.7 = (bf16[8,7168]{1,0:T(8,128)(2,1)S(1)}, bf16[8,7168]{1,0:T(8,128)(2,1)S(1)}, u32[]{:S(2)}, u32[]{:S(2)}) collective-permute-start(bf16[8,7168]{1,0:T(8,128)(2,1)S(1)} %get-tuple-element.16), channel_id=1, source_target_pairs={{0,16},{1,17},{2,18},{3,19},{4,20},{5,21},{6,22},{7,23},{8,24},{9,... | collective-permute-start | bytes 344072 | tf_op jit(solution)/shard_map/ppermute | solution.py:47
  81.3 7.8 %collective-permute-start.8 = (bf16[8,7168]{1,0:T(8,128)(2,1)S(1)}, bf16[8,7168]{1,0:T(8,128)(2,1)S(1)}, u32[]{:S(2)}, u32[]{:S(2)}) collective-permute-start(bf16[8,7168]{1,0:T(8,128)(2,1)S(1)} %get-tuple-element.15), channel_id=1, source_target_pairs={{0,24},{1,25},{2,26},{3,27},{4,28},{5,29},{6,30},{7,31},{8,16},{9,... | collective-permute-start | bytes 344072 | tf_op jit(solution)/shard_map/ppermute | solution.py:47
  84.7 29.5 %copy-start.12 = (bf16[7168,512]{1,0:T(8,128)(2,1)}, bf16[7168,512]{1,0:T(8,128)(2,1)S(1)}, u32[]{:S(2)}) copy-start(bf16[7168,512]{1,0:T(8,128)(2,1)S(1)} %constant_dynamic-update-slice_fusion) | copy-start | bytes 22020100
  89.5 9.6 %collective-permute-start.10 = (bf16[8,7296]{1,0:T(8,128)(2,1)S(1)}, bf16[8,7296]{1,0:T(8,128)(2,1)S(1)}, u32[]{:S(2)}, u32[]{:S(2)}) collective-permute-start(bf16[8,7296]{1,0:T(8,128)(2,1)S(1)} %pad_maximum_fusion.10), channel_id=1, source_target_pairs={{0,16},{1,17},{2,18},{3,19},{4,20},{5,21},{6,22},{7,23},{8,24},{9,... | collective-permute-start | bytes 350216 | tf_op jit(solution)/shard_map/ppermute | solution.py:47
  94.0 7.6 %collective-permute-start.11 = (bf16[8,7296]{1,0:T(8,128)(2,1)S(1)}, bf16[8,7296]{1,0:T(8,128)(2,1)S(1)}, u32[]{:S(2)}, u32[]{:S(2)}) collective-permute-start(bf16[8,7296]{1,0:T(8,128)(2,1)S(1)} %pad_maximum_fusion.10), channel_id=1, source_target_pairs={{0,24},{1,25},{2,26},{3,27},{4,28},{5,29},{6,30},{7,31},{8,16},{9,... | collective-permute-start | bytes 350216 | tf_op jit(solution)/shard_map/ppermute | solution.py:47
  97.4 5.4 %collective-permute-start.9 = (bf16[8,7296]{1,0:T(8,128)(2,1)S(1)}, bf16[8,7296]{1,0:T(8,128)(2,1)S(1)}, u32[]{:S(2)}, u32[]{:S(2)}) collective-permute-start(bf16[8,7296]{1,0:T(8,128)(2,1)S(1)} %pad_maximum_fusion.10), channel_id=1, source_target_pairs={{0,8},{1,9},{2,10},{3,11},{4,12},{5,13},{6,14},{7,15},{8,0},{9,1},... | collective-permute-start | bytes 350216 | tf_op jit(solution)/shard_map/ppermute | solution.py:47
  99.1 13.2 %copy-start.3 = (bf16[256,7168]{1,0:T(8,128)(2,1)}, bf16[256,7168]{1,0:T(8,128)(2,1)S(1)}, u32[]{:S(2)}) copy-start(bf16[256,7168]{1,0:T(8,128)(2,1)S(1)} %constant_dynamic-update-slice_fusion.4) | copy-start | bytes 11010052
  102.8 8.6 %collective-permute-start.14 = (bf16[32,3584]{1,0:T(8,128)(2,1)S(1)}, bf16[32,3584]{1,0:T(8,128)(2,1)S(1)}, u32[]{:S(2)}, u32[]{:S(2)}) collective-permute-start(bf16[32,3584]{1,0:T(8,128)(2,1)S(1)} %pad_maximum_fusion.7), channel_id=1, source_target_pairs={{0,4},{1,5},{2,6},{3,7},{4,0},{5,1},{6,2},{7,3},{8,12},{9,13},{10,... | collective-permute-start | bytes 688136 | tf_op jit(solution)/shard_map/ppermute | solution.py:47
  103.0 9.3 %collective-permute-start.12 = (bf16[32,3712]{1,0:T(8,128)(2,1)S(1)}, bf16[32,3712]{1,0:T(8,128)(2,1)S(1)}, u32[]{:S(2)}, u32[]{:S(2)}) collective-permute-start(bf16[32,3712]{1,0:T(8,128)(2,1)S(1)} %slice.269), channel_id=1, source_target_pairs={{0,2},{1,3},{2,0},{3,1},{4,6},{5,7},{6,4},{7,5},{8,10},{9,11},{10,... | collective-permute-start | bytes 712712 | tf_op jit(solution)/shard_map/ppermute | solution.py:47
  111.5 8.5 %collective-permute-start.17 = (bf16[64,3584]{1,0:T(8,128)(2,1)S(1)}, bf16[64,3584]{1,0:T(8,128)(2,1)S(1)}, u32[]{:S(2)}, u32[]{:S(2)}) collective-permute-start(bf16[64,3584]{1,0:T(8,128)(2,1)S(1)} %pad_maximum_fusion.4), channel_id=1, source_target_pairs={{0,2},{1,3},{2,0},{3,1},{4,6},{5,7},{6,4},{7,5},{8,10},{9,11},{10,... | collective-permute-start | bytes 1376264 | tf_op jit(solution)/shard_map/ppermute | solution.py:47
  112.4 10.5 %collective-permute-start.13 = (bf16[64,3712]{1,0:T(8,128)(2,1)S(1)}, bf16[64,3712]{1,0:T(8,128)(2,1)S(1)}, u32[]{:S(2)}, u32[]{:S(2)}) collective-permute-start(bf16[64,3712]{1,0:T(8,128)(2,1)S(1)} %pad_maximum_fusion.2), channel_id=1, source_target_pairs={{0,4},{1,5},{2,6},{3,7},{4,0},{5,1},{6,2},{7,3},{8,12},{9,13},{10,... | collective-permute-start | bytes 1425416 | tf_op jit(solution)/shard_map/ppermute | solution.py:47
  115.0 8.0 %copy-start.21 = (pred[12]{0:T(512)(128)(4,1)S(1)}, pred[12]{0:T(512)(128)(4,1)}, u32[]{:S(2)}) copy-start(pred[12]{0:T(512)(128)(4,1)} %compare_and_fusion) | copy-start | bytes 40
  126.8 11.5 %collective-permute-start.21 = (bf16[64,3584]{1,0:T(8,128)(2,1)S(1)}, bf16[64,3584]{1,0:T(8,128)(2,1)S(1)}, u32[]{:S(2)}, u32[]{:S(2)}) collective-permute-start(bf16[64,3584]{1,0:T(8,128)(2,1)S(1)} %fusion.8), channel_id=1, source_target_pairs={{0,4},{1,5},{2,6},{3,7},{4,0},{5,1},{6,2},{7,3},{8,12},{9,13},{10,... | collective-permute-start | bytes 1376264 | tf_op jit(solution)/shard_map/ppermute | solution.py:47
  131.4 11.1 %collective-permute-start.19 = (bf16[64,3584]{1,0:T(8,128)(2,1)S(1)}, bf16[64,3584]{1,0:T(8,128)(2,1)S(1)}, u32[]{:S(2)}, u32[]{:S(2)}) collective-permute-start(bf16[64,3584]{1,0:T(8,128)(2,1)S(1)} %fusion.7), channel_id=1, source_target_pairs={{0,2},{1,3},{2,0},{3,1},{4,6},{5,7},{6,4},{7,5},{8,10},{9,11},{10,... | collective-permute-start | bytes 1376264 | tf_op jit(solution)/shard_map/ppermute | solution.py:47
  132.4 10.1 %copy-start.5 = (bf16[256,7168]{1,0:T(8,128)(2,1)S(1)}, bf16[256,7168]{1,0:T(8,128)(2,1)}, u32[]{:S(2)}) copy-start(bf16[256,7168]{1,0:T(8,128)(2,1)} %copy-done.3) | copy-start | bytes 11010052
  140.3 6.2 %collective-permute-start.22 = (bf16[32,3584]{1,0:T(8,128)(2,1)S(1)}, bf16[32,3584]{1,0:T(8,128)(2,1)S(1)}, u32[]{:S(2)}, u32[]{:S(2)}) collective-permute-start(bf16[32,3584]{1,0:T(8,128)(2,1)S(1)} %slice.417), channel_id=1, source_target_pairs={{0,2},{1,3},{2,0},{3,1},{4,6},{5,7},{6,4},{7,5},{8,10},{9,11},{10,... | collective-permute-start | bytes 688136 | tf_op jit(solution)/shard_map/ppermute | solution.py:47
  142.5 16.3 %copy-start.1 = (bf16[8,128,576]{1,2,0:T(8,128)(2,1)S(1)}, bf16[8,128,576]{1,2,0:T(8,128)(2,1)}, u32[]{:S(2)}) copy-start(bf16[8,128,576]{1,2,0:T(8,128)(2,1)} %param.16) | copy-start | bytes 3538948
  143.0 6.1 %collective-permute-start.20 = (bf16[32,3584]{1,0:T(8,128)(2,1)S(1)}, bf16[32,3584]{1,0:T(8,128)(2,1)S(1)}, u32[]{:S(2)}, u32[]{:S(2)}) collective-permute-start(bf16[32,3584]{1,0:T(8,128)(2,1)S(1)} %slice.418), channel_id=1, source_target_pairs={{0,4},{1,5},{2,6},{3,7},{4,0},{5,1},{6,2},{7,3},{8,12},{9,13},{10,... | collective-permute-start | bytes 688136 | tf_op jit(solution)/shard_map/ppermute | solution.py:47
  149.2 4.9 %collective-permute-start.23 = (bf16[8,7168]{1,0:T(8,128)(2,1)S(1)}, bf16[8,7168]{1,0:T(8,128)(2,1)S(1)}, u32[]{:S(2)}, u32[]{:S(2)}) collective-permute-start(bf16[8,7168]{1,0:T(8,128)(2,1)S(1)} %get-tuple-element.11), channel_id=1, source_target_pairs={{0,8},{1,9},{2,10},{3,11},{4,12},{5,13},{6,14},{7,15},{8,0},{9,1},... | collective-permute-start | bytes 344072 | tf_op jit(solution)/shard_map/ppermute | solution.py:47
  149.9 8.1 %collective-permute-start.24 = (bf16[8,7168]{1,0:T(8,128)(2,1)S(1)}, bf16[8,7168]{1,0:T(8,128)(2,1)S(1)}, u32[]{:S(2)}, u32[]{:S(2)}) collective-permute-start(bf16[8,7168]{1,0:T(8,128)(2,1)S(1)} %get-tuple-element.13), channel_id=1, source_target_pairs={{0,16},{1,17},{2,18},{3,19},{4,20},{5,21},{6,22},{7,23},{8,24},{9,... | collective-permute-start | bytes 344072 | tf_op jit(solution)/shard_map/ppermute | solution.py:47
  151.0 7.0 %collective-permute-start.25 = (bf16[8,7168]{1,0:T(8,128)(2,1)S(1)}, bf16[8,7168]{1,0:T(8,128)(2,1)S(1)}, u32[]{:S(2)}, u32[]{:S(2)}) collective-permute-start(bf16[8,7168]{1,0:T(8,128)(2,1)S(1)} %get-tuple-element.12), channel_id=1, source_target_pairs={{0,24},{1,25},{2,26},{3,27},{4,28},{5,29},{6,30},{7,31},{8,16},{9,... | collective-permute-start | bytes 344072 | tf_op jit(solution)/shard_map/ppermute | solution.py:47
  (6 other events, 21.3 us)

commit v3 on v2

v3 whole, which is shorter than its diff:
```python
import functools

import jax
import jax.numpy as jnp
import numpy as np
from jax import lax
from jax.experimental import pallas as pl
from jax.experimental.pallas import tpu as pltpu
from jax.sharding import PartitionSpec as P

LATENT = 512
SLABS = 8
F32 = jnp.float32
BF16 = jnp.bfloat16

score_scale = 192.0 ** (-0.5)
norm_eps = 1e-06

CORE, AX, AY = 1, 2, 4


def attend(queries, cache, lengths):
    scores = jnp.einsum("bhr,bpr->bhp", queries, cache, preferred_element_type=F32) * score_scale
    live_mask = lax.broadcasted_iota(jnp.int32, scores.shape, 2) < lengths[:, None, None]
    row_max = jnp.max(jnp.where(live_mask, scores, -jnp.inf), axis=2, keepdims=True)
    raised = jnp.where(live_mask, jnp.exp(scores - row_max), 0.0)
    probs_bf = (raised / jnp.sum(raised, axis=2, keepdims=True)).astype(BF16)
    return jnp.einsum(
        "bhp,bpl->bhl", probs_bf, cache[:, :, :LATENT], preferred_element_type=F32
    ).astype(BF16)


CHUNK = 512
LANES = 128
VMEM_BYTES = 12 * 1024 * 1024


def in_vmem(count):
    return [pl.BlockSpec(memory_space=pltpu.VMEM)] * count


def stage(arrays, shapes, copies_of, after):
    def body(*refs):
        ins, outs, sems = refs[: len(arrays)], refs[len(arrays) + 1 : -2], refs[-1]
        copies = [
            pltpu.make_async_copy(src, dst, sems.at[i])
            for i, (src, dst) in enumerate(copies_of(ins, outs))
        ]
        for copy in copies:
            copy.start()
        for copy in copies:
            copy.wait()
        refs[-2][...] = jnp.zeros_like(refs[-2])

    arrays = [pltpu.with_memory_space_constraint(w, pltpu.HBM) for w in arrays]
    count = 2 * len(arrays)
    size = sum(2 * int(np.prod(shape)) for shape in shapes)
    return pl.pallas_call(
        body,
        out_shape=tuple(pltpu.VMEM(shape, BF16) for shape in shapes)
        + (jax.ShapeDtypeStruct((8, 128), F32),),
        in_specs=[pl.BlockSpec(memory_space=pltpu.HBM)] * (len(arrays) + 1),
        out_specs=tuple(in_vmem(len(shapes) + 1)),
        scratch_shapes=[pltpu.SemaphoreType.DMA((count,))],
        compiler_params=pltpu.CompilerParams(vmem_limit_bytes=VMEM_BYTES),
        cost_estimate=pl.CostEstimate(flops=0, bytes_accessed=2 * size, transcendentals=0),
    )(*arrays, after)


def stage_columns(own, other, groups, after):
    depth, width = own.shape[0], own.shape[1] // groups

    def copies_of(ins, outs):
        return [
            (ref.at[:, pl.ds(g * width, width)], out.at[pl.ds(i * depth, depth)])
            for g, out in enumerate(outs)
            for i, ref in enumerate(ins)
        ]

    return stage((own, other), [(2 * depth, width)] * groups, copies_of, after)


def stage_beside(weights, after):
    depth, wide = weights[0].shape

    def copies_of(ins, outs):
        return [(ref, outs[0].at[:, pl.ds(i * wide, wide)]) for i, ref in enumerate(ins)]

    return stage(weights, [(depth, wide * len(weights))], copies_of, after)


def project_chunks(x, scale, w, send, keep):
    cut, width = keep.shape
    for c in range(width // CHUNK):
        span = pl.ds(c * CHUNK, CHUNK)
        y = jnp.dot(x, w[:, span], preferred_element_type=F32) * scale
        keep[:, span] = y[:cut]
        send[:, span] = y[cut:].astype(BF16)


def project_body(x, scale, w, send, keep):
    project_chunks(x[...], scale[...], w, send, keep)


def projected(rows, width):
    return (
        jax.ShapeDtypeStruct((rows // 2, width), BF16),
        jax.ShapeDtypeStruct((rows // 2, width), F32),
    )


def project(x, scale, w):
    rows, depth = x.shape
    width = w.shape[1]
    w = pltpu.with_memory_space_constraint(w, pltpu.VMEM)
    return pl.pallas_call(
        project_body,
        out_shape=projected(rows, width),
        in_specs=in_vmem(3),
        out_specs=tuple(in_vmem(2)),
        compiler_params=pltpu.CompilerParams(vmem_limit_bytes=VMEM_BYTES),
        cost_estimate=pl.CostEstimate(
            flops=2 * rows * depth * width, bytes_accessed=depth * width, transcendentals=0
        ),
    )(x, scale, w)


def stream_body(first, x, own, other, send, keep, held, total, sems):
    cut, width = keep.shape
    step = min(own.shape[0], 2 * LANES)
    per = own.shape[0] // step
    copies = [
        pltpu.make_async_copy(
            w.at[pl.ds(r * step, step), pl.ds(first, width)],
            held.at[pl.ds((i * per + r) * step, step)],
            sems.at[i, r],
        )
        for i, w in enumerate((own, other))
        for r in range(per)
    ]
    for copy in copies:
        copy.start()
    for k, copy in enumerate(copies):
        copy.wait()
        rows = x[:, k * step : (k + 1) * step]
        for c in range(width // CHUNK):
            span = pl.ds(c * CHUNK, CHUNK)
            y = jnp.dot(rows, held[pl.ds(k * step, step), span], preferred_element_type=F32)
            if k > 0:
                y = y + total[:, span]
            if k + 1 < len(copies):
                total[:, span] = y
            else:
                keep[:, span] = y[:cut]
                send[:, span] = y[cut:].astype(BF16)


def project_stream(x, own, other, first, width):
    rows, depth = x.shape
    own, other = (pltpu.with_memory_space_constraint(w, pltpu.HBM) for w in (own, other))
    return pl.pallas_call(
        functools.partial(stream_body, first),
        out_shape=projected(rows, width),
        in_specs=in_vmem(1) + [pl.BlockSpec(memory_space=pltpu.HBM)] * 2,
        out_specs=tuple(in_vmem(2)),
        scratch_shapes=[
            pltpu.VMEM((depth, width), BF16),
            pltpu.VMEM((rows, width), F32),
            pltpu.SemaphoreType.DMA((2, max(1, own.shape[0] // (2 * LANES)))),
        ],
        compiler_params=pltpu.CompilerParams(vmem_limit_bytes=2 * VMEM_BYTES),
        cost_estimate=pl.CostEstimate(
            flops=2 * rows * depth * width, bytes_accessed=2 * depth * width, transcendentals=0
        ),
    )(x, own, other)


def expert_body(
    block, label, near_a, far_a, near_b, far_b, w_in, w_out, send, keep, inner_b, weight_b
):
    cut, half = near_a.shape
    sums = []
    for g, (near, far) in enumerate(((near_a, far_a), (near_b, far_b))):
        total = jnp.zeros((2 * cut, w_in.shape[1]), F32)
        for c in range(half // CHUNK):
            span = pl.ds(c * CHUNK, CHUNK)
            x = jnp.concatenate([near[:, span], far[:, span]], axis=0)
            w = w_in[pl.ds(g * half + c * CHUNK, CHUNK)]
            total = total + jnp.dot(x, w, preferred_element_type=F32)
        sums.append(total)

    def turn(x):
        q = block
        return jnp.concatenate([x[:q], x[2 * q : 3 * q], x[q : 2 * q], x[3 * q :]], axis=0)

    acts = sums[0] + turn(sums[1])
    hid = acts.shape[1] // 2
    gates, ups = acts[:, :hid], acts[:, hid:]
    inner = gates / (1.0 + jnp.exp(-gates)) * ups
    tails = jnp.concatenate([near_b[:, half:], far_b[:, half:]], axis=0).astype(F32)
    lane = lax.broadcasted_iota(jnp.int32, tails.shape, 1)
    mine = lax.rem(lane, label[1]) == label[0]
    weight = jnp.sum(jnp.where(mine, tails, 0.0), axis=1, keepdims=True)
    weight_b[...] = weight
    inner_b[...] = turn(inner).astype(BF16)
    project_chunks(inner.astype(BF16), turn(weight), w_out, send, keep)


def expert(label, tokens, w_in, w_out):
    (near_a, far_a), (near_b, far_b) = tokens
    rows, half = 2 * near_a.shape[0], near_a.shape[1]
    hid = w_out.shape[0]
    w_in, w_out = (pltpu.with_memory_space_constraint(w, pltpu.VMEM) for w in (w_in, w_out))
    return pl.pallas_call(
        functools.partial(expert_body, rows // 4),
        out_shape=projected(rows, half)
        + (jax.ShapeDtypeStruct((rows, hid), BF16), jax.ShapeDtypeStruct((rows, 1), F32)),
        in_specs=[pl.BlockSpec(memory_space=pltpu.SMEM)] + in_vmem(6),
        out_specs=tuple(in_vmem(4)),
        compiler_params=pltpu.CompilerParams(vmem_limit_bytes=VMEM_BYTES),
        cost_estimate=pl.CostEstimate(
            flops=2 * rows * (w_in.size + w_out.size),
            bytes_accessed=w_in.size + w_out.size,
            transcendentals=rows * hid,
        ),
    )(label, near_a, far_a, near_b, far_b, w_in, w_out)


def relative_order(first, second, planes):
    return np.array(
        [
            z * SLABS + b * second + a * first
            for a in (0, 1)
            for b in (0, 1)
            for z in range(planes)
        ],
        np.int32,
    )


def on_device(devices):
    planes = devices // SLABS
    chips = devices // 2
    axes = ((AX, AY), (AY, AX))

    def swap(x, mask):
        return lax.ppermute(x, "ep", [(i, i ^ mask) for i in range(devices)])

    def sum_to_owner(products, rows):
        outs = []
        for g, (send, keep) in enumerate(products):
            x = keep + swap(send, axes[g][0]).astype(F32)
            half = x.shape[0] // 2
            outs.append(x[:half] + swap(x[half:].astype(BF16), axes[g][1]).astype(F32))
        x = jnp.concatenate(outs, axis=1)
        total = x[:rows]
        for d in range(1, planes):
            total = total + swap(x[d * rows : (d + 1) * rows].astype(BF16), d * SLABS).astype(F32)
        return total

    def to_all(x, cut):
        x = jnp.concatenate([x] + [swap(x, d * SLABS) for d in range(1, planes)], axis=0)
        near = [
            jnp.concatenate([part, swap(part, axes[g][1])], axis=0)
            for g, part in enumerate((x[:, :cut], x[:, cut:]))
        ]
        return [(near[g], swap(near[g], axes[g][0])) for g in (0, 1)]

    def body(
        hidden, queries, cache, lengths, value_up, out_proj, norm_gain,
        routes, gates, expert_slot, w_gate, w_up, w_down,
    ):
        rows, width = hidden.shape
        half = width // 2
        me = lax.axis_index("ep")
        core = me % 2
        value_up_other = swap(value_up, CORE)
        out_proj_other = swap(out_proj, CORE)
        w_gate_other, w_up_other, w_down_other = (swap(w, CORE) for w in (w_gate, w_up, w_down))

        latent_out = attend(queries, cache, lengths)
        by_heads = lax.all_to_all(
            latent_out, "ep", split_axis=1, concat_axis=0, tiled=True,
            axis_index_groups=[list(range(c, devices, 2)) for c in (0, 1)],
        )

        after = latent_out[0, :16, :128]
        w_in, _ = stage_beside((w_gate, w_gate_other, w_up, w_up_other), after)
        *w_out, _ = stage_columns(w_down, w_down_other, 2, after)
        even = core == 0
        heads_up = jnp.concatenate(
            [
                jnp.where(even, value_up, value_up_other),
                jnp.where(even, value_up_other, value_up),
            ],
            axis=0,
        )
        by_heads, heads_up = lax.optimization_barrier((by_heads, heads_up))

        orders = [relative_order(first, second, planes) for first, second in axes]
        experts = expert_slot.shape[0]
        labels = jnp.arange(experts, dtype=jnp.int32)
        physical = jnp.sum(
            jnp.where(routes[:, :, None] == labels, expert_slot[None, None, :], 0), axis=2
        )
        weights = jnp.sum(
            jnp.where(physical[:, :, None] == labels, gates[:, :, None], 0.0), axis=1
        )
        pieces = []
        for _ in range(3):
            piece = lax.reduce_precision(weights, 8, 7)
            pieces.append(piece.astype(BF16))
            weights = weights - piece
        tail = jnp.pad(jnp.concatenate(pieces, axis=1), ((0, 0), (0, 128 - 3 * experts)))

        head_values = jnp.einsum(
            "bhl,hlv->bhv", by_heads, heads_up, preferred_element_type=F32
        ).astype(BF16)
        total_rows = head_values.shape[0]
        flat_values = head_values.reshape(total_rows, 2, -1)
        flat_values = jnp.concatenate(
            [
                jnp.where(even, flat_values[:, 0], flat_values[:, 1]),
                jnp.where(even, flat_values[:, 1], flat_values[:, 0]),
            ],
            axis=1,
        )
        picks = []
        for order in orders:
            place = jnp.bitwise_xor(jnp.asarray(order), me) // 2
            wanted = (place[:, None] * rows + jnp.arange(rows, dtype=jnp.int32)).reshape(-1, 1)
            pick = (wanted == jnp.arange(total_rows, dtype=jnp.int32)[None, :]).astype(BF16)
            picks.append(jnp.dot(pick, flat_values, preferred_element_type=F32).astype(BF16))
        attended = sum_to_owner(
            [project_stream(picks[g], out_proj, out_proj_other, g * half, half) for g in (0, 1)],
            rows,
        )
        mixed = hidden.astype(F32) + attended
        scale_rows = lax.rsqrt(jnp.mean(mixed * mixed, axis=1, keepdims=True) + norm_eps)
        normed = (mixed * scale_rows * norm_gain.astype(F32)).astype(BF16)

        tokens = to_all(jnp.concatenate([normed, tail], axis=1), half)
        label = jnp.stack([me // SLABS, jnp.int32(experts)])
        *product_a, inner_b, weight_b = expert(label, tokens, w_in, w_out[0])
        product_b = project(inner_b, weight_b, w_out[1])
        return (mixed + sum_to_owner([product_a, product_b], rows)).astype(BF16)

    return body


def solution(mesh):
    placed = (
        P(("groups", "ep"), None),
        P(("groups", "ep"), None, None),
        P(("groups", "ep"), None, None),
        P(("groups", "ep")),
        P("ep", None, None),
        P("ep", None),
        P(),
        P(("groups", "ep"), None),
        P(("groups", "ep"), None),
        P(),
        P(None, "ep"),
        P(None, "ep"),
        P("ep", None),
    )
    return jax.shard_map(
        on_device(mesh.shape["ep"]),
        mesh=mesh,
        in_specs=placed,
        out_specs=P(("groups", "ep"), None),
        check_vma=False,
    )
```

time: 159 us -> 146 us (0.918)
  matrix products: 34.8 us -> 4.17 us
  waiting for transfers between devices: 55.6 us -> 83.6 us
  Pallas kernels: 0 us -> 16.2 us
  local copies, waits for them, and re-layouts: 15.6 us -> 3.03 us
  starting transfers between devices: 44.6 us -> 33.7 us
  other arithmetic: 7.59 us -> 4.6 us
    dot_general x16 -> x0, matrix products: 30.6 us -> none  [the longest x4 11.3 us: out_part(): jnp.dot(x[:, own_rows:], out_proj_other[:, span], preferred_element_type=...]
    ppermute x26, waiting for transfers between devices: 43.6 us -> 61.3 us  [swap(): return lax.ppermute(x, 'ep', [(i, i ^ mask) for i in range(devices)])]
    pallas_call x0 -> x6, Pallas kernels: none -> 16.2 us  [the longest x2 7.21 us: project_stream(): pl.pallas_call(functools.partial(stream_body, first), out_shape=projected...]
    ppermute x26, starting transfers between devices: 36.3 us -> 25.4 us  [swap(): return lax.ppermute(x, 'ep', [(i, i ^ mask) for i in range(devices)])]
    all_to_all x1, waiting for transfers between devices: 12 us -> 22.3 us  [body(): lax.all_to_all(latent_out, 'ep', split_axis=1, concat_axis=0, tiled=True,...]
    unnamed x59 -> x24, local copies, waits for them, and re-layouts: 9.42 us -> 0.88 us
    concatenate x2 -> x0, local copies, waits for them, and re-layouts: 3.55 us -> none  [the longest x1 1.93 us: body(): w_in = jnp.concatenate([w_gate, w_gate_other, w_up, w_up_other], axis=1)]
    select_n x1, other arithmetic: 2.22 us -> 0.07 us  [body(): jnp.where(even, value_up, value_up_other)]
  transfers between devices with their start and end apart: 27 -> 27, of which waited for: 15 -> 19; matrix products, arithmetic and copies ran while one was open for 32% -> 7% of each run, Pallas kernels for 0% -> 7%
where the time goes in v3:
time: 146 us
  waiting for transfers between devices  83.6 us (57%)
  starting transfers between devices  33.7 us (23%)
  Pallas kernels  16.2 us (11%)
  other arithmetic  4.6 us (3%)
  matrix products  4.17 us (3%)
  local copies, waits for them, and re-layouts  3.03 us (2%)
    ppermute x26, waiting for transfers between devices, swap(): return lax.ppermute(x, 'ep', [(i, i ^ mask) for i in range(devices)])  61.3 us
    ppermute x26, starting transfers between devices, swap(): return lax.ppermute(x, 'ep', [(i, i ^ mask) for i in range(devices)])  25.4 us
    all_to_all x1, waiting for transfers between devices, body(): lax.all_to_all(latent_out, 'ep', split_axis=1, concat_axis=0, tiled=True,...  22.3 us
    all_to_all x1, starting transfers between devices, body(): lax.all_to_all(latent_out, 'ep', split_axis=1, concat_axis=0, tiled=True,...  8.31 us
    pallas_call x2, Pallas kernels, project_stream(): pl.pallas_call(functools.partial(stream_body, first), out_shape=projected...  7.21 us
    pallas_call x2, Pallas kernels, stage(): pl.pallas_call(body, out_shape=tuple((pltpu.VMEM(shape, BF16) for shape i...  6.45 us
  transfers between devices with their start and end apart: 27, of which 19 were waited for; matrix products, arithmetic and copies ran while one was open for 7% of the time, Pallas kernels for 7%

profile of v3, /device:TPU:0, one launch (start us, length us, event | category | flops | bytes accessed | tf_op | source)
XLA Modules:
  0.0 145.8 jit_solution(14069747181166667484)
XLA Ops:
  0.0 0.5 collective-permute-start.1
  0.5 0.8 copy-done
  1.3 2.3 %convolution_multiply_fusion = f32[8,128,256]{2,1,0:T(8,128)S(1)} fusion(bf16[8,128,576]{1,2,0:T(8,128)(2,1)S(1)} %copy-done, bf16[8,256,576]{1,2,0:T(8,128)(2,1)} %param.17), kind=kOutput, calls=%fused_computation.4 | convolution fusion | flops 302252032 | bytes 4587520 | tf_op jit(solution)/shard_map/bhr,bpr->bhp/dot_general | solution.py:23
  3.6 2.2 %fusion.47 = (f32[8,128]{1,0:T(8,128)S(1)}, f32[8,128,256]{2,1,0:T(8,128)S(1)}) fusion(f32[8,128,256]{2,1,0:T(8,128)S(1)} %convolution_multiply_fusion, s32[8]{0:T(128)S(1)} %copy-done.11), kind=kOutput, calls=%fused_computation.108 | output fusion | flops 1573119 | bytes 2101280 | tf_op jit(solution)/shard_map/sub | solution.py:26
  5.9 0.8 fusion.3
  6.7 1.7 %copy.33 = bf16[8,128,512]{2,0,1:T(8,128)(2,1)} copy(bf16[8,128,512]{2,1,0:T(8,128)(2,1)S(1)} %fusion.3) | data formatting | bytes 2097152 | tf_op jit(solution)/shard_map/convert_element_type | solution.py:30
  8.4 8.3 %all-to-all-start = ((bf16[8,128,512]{2,0,1:T(8,128)(2,1)}), bf16[8,128,512]{2,0,1:T(8,128)(2,1)S(1)}, u32[]{:S(2)}, u32[]{:S(2)}) async-start(bf16[8,128,512]{2,0,1:T(8,128)(2,1)} %copy.33), calls=%async_computation | async-start | bytes 2097152 | tf_op jit(solution)/shard_map/all_to_all | solution.py:282
  17.1 1.6 %collective-permute-done = bf16[4,512,128]{2,1,0:T(8,128)(2,1)S(1)} collective-permute-done((bf16[4,512,128]{2,1,0:T(8,128)(2,1)S(1)}, bf16[4,512,128]{2,1,0:T(8,128)(2,1)S(1)}, u32[]{:S(2)}, u32[]{:S(2)}) %collective-permute-start) | collective-permute-done | bytes 524320 | tf_op jit(solution)/shard_map/ppermute | solution.py:247
  18.9 22.3 %all-to-all-done = bf16[8,128,512]{2,0,1:T(8,128)(2,1)S(1)} async-done(((bf16[8,128,512]{2,0,1:T(8,128)(2,1)}), bf16[8,128,512]{2,0,1:T(8,128)(2,1)S(1)}, u32[]{:S(2)}, u32[]{:S(2)}) %all-to-all-start) | async-done | bytes 1048608 | tf_op jit(solution)/shard_map/all_to_all | solution.py:282
  41.3 0.5 convolution_convert_fusion
  42.1 3.6 %shard_map.146 = (bf16[64,3584]{1,0:T(8,128)(2,1)S(1)}, f32[64,3584]{1,0:T(8,128)S(1)}) custom-call(bf16[128,1024]{1,0:T(8,128)(2,1)S(1)} %convolution_convert_fusion.1.x, bf16[512,7168]{1,0:T(8,128)(2,1)} %own.3, bf16[512,7168]{1,0:T(8,128)(2,1)} %collective-permute-done.1.other), custom_call_target="tpu_custom_call" | custom-call | flops 939524096 | bytes 7340032 | tf_op jit(solution)/shard_map/pallas_call | solution.py:161
  45.7 2.0 %collective-permute-start.4 = (bf16[64,3584]{1,0:T(8,128)(2,1)S(1)}, bf16[64,3584]{1,0:T(8,128)(2,1)S(1)}, u32[]{:S(2)}, u32[]{:S(2)}) collective-permute-start(bf16[64,3584]{1,0:T(8,128)(2,1)S(1)} %get-tuple-element.25), channel_id=1, source_target_pairs={{0,4},{1,5},{2,6},{3,7},{4,0},{5,1},{6,2},{7,3},{8,12},{9,13},{10,... | collective-permute-start | bytes 1376264 | tf_op jit(solution)/shard_map/ppermute | solution.py:247
  48.3 3.6 %shard_map.145 = (bf16[64,3584]{1,0:T(8,128)(2,1)S(1)}, f32[64,3584]{1,0:T(8,128)S(1)}) custom-call(bf16[128,1024]{1,0:T(8,128)(2,1)S(1)} %convolution_convert_fusion.2.x, bf16[512,7168]{1,0:T(8,128)(2,1)} %own.3, bf16[512,7168]{1,0:T(8,128)(2,1)} %collective-permute-done.1.other), custom_call_target="tpu_custom_call" | custom-call | flops 939524096 | bytes 7340032 | tf_op jit(solution)/shard_map/pallas_call | solution.py:161
  51.9 0.6 collective-permute-start.2
  52.6 3.6 %collective-permute-done.4 = bf16[64,3584]{1,0:T(8,128)(2,1)S(1)} collective-permute-done((bf16[64,3584]{1,0:T(8,128)(2,1)S(1)}, bf16[64,3584]{1,0:T(8,128)(2,1)S(1)}, u32[]{:S(2)}, u32[]{:S(2)}) %collective-permute-start.4) | collective-permute-done | bytes 458784 | tf_op jit(solution)/shard_map/ppermute | solution.py:247
  56.3 0.6 collective-permute-start.5
  56.9 7.4 %collective-permute-done.2 = bf16[64,3584]{1,0:T(8,128)(2,1)S(1)} collective-permute-done((bf16[64,3584]{1,0:T(8,128)(2,1)S(1)}, bf16[64,3584]{1,0:T(8,128)(2,1)S(1)}, u32[]{:S(2)}, u32[]{:S(2)}) %collective-permute-start.2) | collective-permute-done | bytes 458784 | tf_op jit(solution)/shard_map/ppermute | solution.py:247
  64.8 1.9 %collective-permute-done.5 = bf16[32,3584]{1,0:T(8,128)(2,1)S(1)} collective-permute-done((bf16[32,3584]{1,0:T(8,128)(2,1)S(1)}, bf16[32,3584]{1,0:T(8,128)(2,1)S(1)}, u32[]{:S(2)}, u32[]{:S(2)}) %collective-permute-start.5) | collective-permute-done | bytes 229408 | tf_op jit(solution)/shard_map/ppermute | solution.py:247
  66.8 3.7 %collective-permute-done.3 = bf16[32,3584]{1,0:T(8,128)(2,1)S(1)} collective-permute-done((bf16[32,3584]{1,0:T(8,128)(2,1)S(1)}, bf16[32,3584]{1,0:T(8,128)(2,1)S(1)}, u32[]{:S(2)}, u32[]{:S(2)}) %collective-permute-start.3) | collective-permute-done | bytes 229408 | tf_op jit(solution)/shard_map/ppermute | solution.py:247
  70.7 3.8 %collective-permute-start.8 = (bf16[8,7168]{1,0:T(8,128)(2,1)S(1)}, bf16[8,7168]{1,0:T(8,128)(2,1)S(1)}, u32[]{:S(2)}, u32[]{:S(2)}) collective-permute-start(bf16[8,7168]{1,0:T(8,128)(2,1)S(1)} %get-tuple-element.43), channel_id=1, source_target_pairs={{0,24},{1,25},{2,26},{3,27},{4,28},{5,29},{6,30},{7,31},{8,16},{9,... | collective-permute-start | bytes 344072 | tf_op jit(solution)/shard_map/ppermute | solution.py:247
  74.4 1.1 collective-permute-start.7
  75.7 1.7 %collective-permute-done.8 = bf16[8,7168]{1,0:T(8,128)(2,1)S(1)} collective-permute-done((bf16[8,7168]{1,0:T(8,128)(2,1)S(1)}, bf16[8,7168]{1,0:T(8,128)(2,1)S(1)}, u32[]{:S(2)}, u32[]{:S(2)}) %collective-permute-start.8) | collective-permute-done | bytes 114720 | tf_op jit(solution)/shard_map/ppermute | solution.py:247
  77.4 8.6 %collective-permute-done.7 = bf16[8,7168]{1,0:T(8,128)(2,1)S(1)} collective-permute-done((bf16[8,7168]{1,0:T(8,128)(2,1)S(1)}, bf16[8,7168]{1,0:T(8,128)(2,1)S(1)}, u32[]{:S(2)}, u32[]{:S(2)}) %collective-permute-start.7) | collective-permute-done | bytes 114720 | tf_op jit(solution)/shard_map/ppermute | solution.py:247
  86.3 1.8 %collective-permute-start.11 = (bf16[8,7296]{1,0:T(8,128)(2,1)S(1)}, bf16[8,7296]{1,0:T(8,128)(2,1)S(1)}, u32[]{:S(2)}, u32[]{:S(2)}) collective-permute-start(bf16[8,7296]{1,0:T(8,128)(2,1)S(1)} %pad_maximum_fusion.13), channel_id=1, source_target_pairs={{0,24},{1,25},{2,26},{3,27},{4,28},{5,29},{6,30},{7,31},{8,16},{9,... | collective-permute-start | bytes 350216 | tf_op jit(solution)/shard_map/ppermute | solution.py:247
  88.1 2.7 %collective-permute-start.9 = (bf16[8,7296]{1,0:T(8,128)(2,1)S(1)}, bf16[8,7296]{1,0:T(8,128)(2,1)S(1)}, u32[]{:S(2)}, u32[]{:S(2)}) collective-permute-start(bf16[8,7296]{1,0:T(8,128)(2,1)S(1)} %pad_maximum_fusion.13), channel_id=1, source_target_pairs={{0,8},{1,9},{2,10},{3,11},{4,12},{5,13},{6,14},{7,15},{8,0},{9,1},... | collective-permute-start | bytes 350216 | tf_op jit(solution)/shard_map/ppermute | solution.py:247
  90.8 0.5 collective-permute-start.17
  91.3 1.8 %collective-permute-done.11 = bf16[8,7296]{1,0:T(8,128)(2,1)S(1)} collective-permute-done((bf16[8,7296]{1,0:T(8,128)(2,1)S(1)}, bf16[8,7296]{1,0:T(8,128)(2,1)S(1)}, u32[]{:S(2)}, u32[]{:S(2)}) %collective-permute-start.11) | collective-permute-done | bytes 116768 | tf_op jit(solution)/shard_map/ppermute | solution.py:247
  93.1 2.4 %collective-permute-done.10 = bf16[8,7296]{1,0:T(8,128)(2,1)S(1)} collective-permute-done((bf16[8,7296]{1,0:T(8,128)(2,1)S(1)}, bf16[8,7296]{1,0:T(8,128)(2,1)S(1)}, u32[]{:S(2)}, u32[]{:S(2)}) %collective-permute-start.10) | collective-permute-done | bytes 116768 | tf_op jit(solution)/shard_map/ppermute | solution.py:247
  95.5 0.6 collective-permute-start.14
  96.2 0.8 collective-permute-start.12
  96.9 4.8 %collective-permute-done.14 = bf16[32,3712]{1,0:T(8,128)(2,1)S(1)} collective-permute-done((bf16[32,3712]{1,0:T(8,128)(2,1)S(1)}, bf16[32,3712]{1,0:T(8,128)(2,1)S(1)}, u32[]{:S(2)}, u32[]{:S(2)}) %collective-permute-start.14) | collective-permute-done | bytes 237600 | tf_op jit(solution)/shard_map/ppermute | solution.py:247
  102.1 1.0 collective-permute-done.12
  103.1 2.5 %collective-permute-start.13 = (bf16[64,3584]{1,0:T(8,128)(2,1)S(1)}, bf16[64,3584]{1,0:T(8,128)(2,1)S(1)}, u32[]{:S(2)}, u32[]{:S(2)}) collective-permute-start(bf16[64,3584]{1,0:T(8,128)(2,1)S(1)} %pad_maximum_fusion.4.near_a), channel_id=1, source_target_pairs={{0,2},{1,3},{2,0},{3,1},{4,6},{5,7},{6,4},{7,5},{8,10},{9,11},{10,... | collective-permute-start | bytes 1376264 | tf_op jit(solution)/shard_map/ppermute | solution.py:247
  105.7 2.6 %shard_map.148 = (bf16[256,3584]{1,0:T(8,128)(2,1)S(1)}, bf16[256,3584]{1,0:T(8,128)(2,1)S(1)}, f32[8,128]{1,0:T(8,128)}) custom-call(bf16[128,7168]{1,0:T(8,128)(2,1)} %refs_0_.3, bf16[128,7168]{1,0:T(8,128)(2,1)} %collective-permute-done.18.refs_1_, bf16[16,128]{1,0:T(8,128)(2,1)S(1)} %slice_bitcast_fusion.refs_4_.refs_2_), custom_call_target="tpu_custom_call" | custom-call | bytes 7340032 | tf_op jit(solution)/shard_map/pallas_call | solution.py:58
  108.3 3.8 %shard_map.147 = (bf16[7168,512]{1,0:T(8,128)(2,1)S(1)}, f32[8,128]{1,0:T(8,128)}) custom-call(bf16[7168,128]{1,0:T(8,128)(2,1)} %refs_0_.2, bf16[7168,128]{1,0:T(8,128)(2,1)} %collective-permute-done.16.refs_1_, bf16[7168,128]{1,0:T(8,128)(2,1)} %refs_2_.1, bf16[7168,128]{1,0:T(8,128)(2,1)} %collective-permute-done.17.refs_3_, ...), custom_call_target="tpu_custom_call" | custom-call | bytes 14680064 | tf_op jit(solution)/shard_map/pallas_call | solution.py:58
  112.4 2.1 %shard_map.149 = (bf16[64,3584]{1,0:T(8,128)(2,1)S(1)}, f32[64,3584]{1,0:T(8,128)S(1)}, bf16[128,256]{1,0:T(8,128)(2,1)S(1)}, f32[128,1]{1,0:T(8,128)S(1)}) custom-call(s32[2]{0:T(128)S(1)} %pad_add_fusion.label, bf16[64,3584]{1,0:T(8,128)(2,1)S(1)} %pad_maximum_fusion.4.near_a, bf16[64,3584]{1,0:T(8,128)(2,1)S(1)} %collective-permute-done.13.far_a, ...), custom_call_target="tpu_custom_call" | custom-call | flops 1174405120 | bytes 4587520 | tf_op jit(solution)/shard_map/pallas_call | solution.py:214
  114.5 1.7 %collective-permute-start.19 = (bf16[64,3584]{1,0:T(8,128)(2,1)S(1)}, bf16[64,3584]{1,0:T(8,128)(2,1)S(1)}, u32[]{:S(2)}, u32[]{:S(2)}) collective-permute-start(bf16[64,3584]{1,0:T(8,128)(2,1)S(1)} %get-tuple-element.29), channel_id=1, source_target_pairs={{0,2},{1,3},{2,0},{3,1},{4,6},{5,7},{6,4},{7,5},{8,10},{9,11},{10,... | collective-permute-start | bytes 1376264 | tf_op jit(solution)/shard_map/ppermute | solution.py:247
  117.0 7.6 %collective-permute-done.19 = bf16[64,3584]{1,0:T(8,128)(2,1)S(1)} collective-permute-done((bf16[64,3584]{1,0:T(8,128)(2,1)S(1)}, bf16[64,3584]{1,0:T(8,128)(2,1)S(1)}, u32[]{:S(2)}, u32[]{:S(2)}) %collective-permute-start.19) | collective-permute-done | bytes 458784 | tf_op jit(solution)/shard_map/ppermute | solution.py:247
  124.7 0.5 collective-permute-start.20
  125.3 3.7 %collective-permute-done.21 = bf16[64,3584]{1,0:T(8,128)(2,1)S(1)} collective-permute-done((bf16[64,3584]{1,0:T(8,128)(2,1)S(1)}, bf16[64,3584]{1,0:T(8,128)(2,1)S(1)}, u32[]{:S(2)}, u32[]{:S(2)}) %collective-permute-start.21) | collective-permute-done | bytes 458784 | tf_op jit(solution)/shard_map/ppermute | solution.py:247
  129.2 2.3 %collective-permute-done.20 = bf16[32,3584]{1,0:T(8,128)(2,1)S(1)} collective-permute-done((bf16[32,3584]{1,0:T(8,128)(2,1)S(1)}, bf16[32,3584]{1,0:T(8,128)(2,1)S(1)}, u32[]{:S(2)}, u32[]{:S(2)}) %collective-permute-start.20) | collective-permute-done | bytes 229408 | tf_op jit(solution)/shard_map/ppermute | solution.py:247
  131.5 3.7 %collective-permute-done.22 = bf16[32,3584]{1,0:T(8,128)(2,1)S(1)} collective-permute-done((bf16[32,3584]{1,0:T(8,128)(2,1)S(1)}, bf16[32,3584]{1,0:T(8,128)(2,1)S(1)}, u32[]{:S(2)}, u32[]{:S(2)}) %collective-permute-start.22) | collective-permute-done | bytes 229408 | tf_op jit(solution)/shard_map/ppermute | solution.py:247
  135.3 2.1 %collective-permute-start.25 = (bf16[8,7168]{1,0:T(8,128)(2,1)S(1)}, bf16[8,7168]{1,0:T(8,128)(2,1)S(1)}, u32[]{:S(2)}, u32[]{:S(2)}) collective-permute-start(bf16[8,7168]{1,0:T(8,128)(2,1)S(1)} %get-tuple-element.40), channel_id=1, source_target_pairs={{0,24},{1,25},{2,26},{3,27},{4,28},{5,29},{6,30},{7,31},{8,16},{9,... | collective-permute-start | bytes 344072 | tf_op jit(solution)/shard_map/ppermute | solution.py:247
  137.4 1.2 collective-permute-start.24
  138.6 1.2 collective-permute-start.23
  139.8 2.3 %collective-permute-done.25 = bf16[8,7168]{1,0:T(8,128)(2,1)S(1)} collective-permute-done((bf16[8,7168]{1,0:T(8,128)(2,1)S(1)}, bf16[8,7168]{1,0:T(8,128)(2,1)S(1)}, u32[]{:S(2)}, u32[]{:S(2)}) %collective-permute-start.25) | collective-permute-done | bytes 114720 | tf_op jit(solution)/shard_map/ppermute | solution.py:247
  142.1 3.0 %collective-permute-done.24 = bf16[8,7168]{1,0:T(8,128)(2,1)S(1)} collective-permute-done((bf16[8,7168]{1,0:T(8,128)(2,1)S(1)}, bf16[8,7168]{1,0:T(8,128)(2,1)S(1)}, u32[]{:S(2)}, u32[]{:S(2)}) %collective-permute-start.24) | collective-permute-done | bytes 114720 | tf_op jit(solution)/shard_map/ppermute | solution.py:247
  145.0 0.7 fusion.24
  (85 shorter events, 4.7 us)
Async XLA Ops:
  0.0 1.3 copy-start
  0.0 3.6 %copy-start.11 = (s32[8]{0:T(128)S(1)}, s32[8]{0:T(128)}, u32[]{:S(2)}) copy-start(s32[8]{0:T(128)} %param.18) | copy-start | bytes 100
  0.0 42.1 %collective-permute-start.1 = (bf16[512,7168]{1,0:T(8,128)(2,1)}, bf16[512,7168]{1,0:T(8,128)(2,1)}, u32[]{:S(2)}, u32[]{:S(2)}) collective-permute-start(bf16[512,7168]{1,0:T(8,128)(2,1)} %own.3), channel_id=1, source_target_pairs={{0,1},{1,0},{2,3},{3,2},{4,5},{5,4},{6,7},{7,6},{8,9},{9,8},{10,11... | collective-permute-start | bytes 22020104 | tf_op jit(solution)/shard_map/ppermute | solution.py:247
  3.6 2.3 %copy-start.2 = (bf16[8,256,576]{1,2,0:T(8,128)(2,1)S(1)}, bf16[8,256,576]{1,2,0:T(8,128)(2,1)}, u32[]{:S(2)}) copy-start(bf16[8,256,576]{1,2,0:T(8,128)(2,1)} %param.17) | copy-start | bytes 7077892
  6.7 10.0 %copy-start.3 = (bf16[4,512,128]{2,1,0:T(8,128)(2,1)S(1)}, bf16[4,512,128]{2,1,0:T(8,128)(2,1)}, u32[]{:S(2)}) copy-start(bf16[4,512,128]{2,1,0:T(8,128)(2,1)} %param.19) | copy-start | bytes 1572868
  6.7 10.1 %copy-start.9 = (s32[16]{0:T(128)S(1)}, s32[16]{0:T(128)}, u32[]{:S(2)}) copy-start(s32[16]{0:T(128)} %constant.71.clone) | copy-start | bytes 196
  6.7 10.1 %copy-start.10 = (s32[16]{0:T(128)S(1)}, s32[16]{0:T(128)}, u32[]{:S(2)}) copy-start(s32[16]{0:T(128)} %constant.70.clone) | copy-start | bytes 196
  8.4 32.8 %all-to-all-start = ((bf16[8,128,512]{2,0,1:T(8,128)(2,1)}), bf16[8,128,512]{2,0,1:T(8,128)(2,1)S(1)}, u32[]{:S(2)}, u32[]{:S(2)}) async-start(bf16[8,128,512]{2,0,1:T(8,128)(2,1)} %copy.33), calls=%async_computation | async-start | bytes 2097152 | tf_op jit(solution)/shard_map/all_to_all | solution.py:282
  16.7 2.0 %collective-permute-start = (bf16[4,512,128]{2,1,0:T(8,128)(2,1)S(1)}, bf16[4,512,128]{2,1,0:T(8,128)(2,1)S(1)}, u32[]{:S(2)}, u32[]{:S(2)}) collective-permute-start(bf16[4,512,128]{2,1,0:T(8,128)(2,1)S(1)} %copy-done.3), channel_id=1, source_target_pairs={{0,1},{1,0},{2,3},{3,2},{4,5},{5,4},{6,7},{7,6},{8,9},{9,8},{10,11... | collective-permute-start | bytes 1572872 | tf_op jit(solution)/shard_map/ppermute | solution.py:247
  42.1 5.7 %copy-start.6 = (s32[8,2]{0,1:T(2,128)S(1)}, s32[8,2]{0,1:T(2,128)}, u32[]{:S(2)}) copy-start(s32[8,2]{0,1:T(2,128)} %param.22) | copy-start | bytes 196
  42.1 5.7 %copy-start.8 = (s32[4]{0:T(128)S(1)}, s32[4]{0:T(128)}, u32[]{:S(2)}) copy-start(s32[4]{0:T(128)} %param.24) | copy-start | bytes 52
  42.1 5.8 %copy-start.7 = (f32[8,2]{0,1:T(2,128)S(1)}, f32[8,2]{0,1:T(2,128)}, u32[]{:S(2)}) copy-start(f32[8,2]{0,1:T(2,128)} %param.23) | copy-start | bytes 196
  45.7 10.4 %collective-permute-start.4 = (bf16[64,3584]{1,0:T(8,128)(2,1)S(1)}, bf16[64,3584]{1,0:T(8,128)(2,1)S(1)}, u32[]{:S(2)}, u32[]{:S(2)}) collective-permute-start(bf16[64,3584]{1,0:T(8,128)(2,1)S(1)} %get-tuple-element.25), channel_id=1, source_target_pairs={{0,4},{1,5},{2,6},{3,7},{4,0},{5,1},{6,2},{7,3},{8,12},{9,13},{10,... | collective-permute-start | bytes 1376264 | tf_op jit(solution)/shard_map/ppermute | solution.py:247
  51.9 12.4 %collective-permute-start.2 = (bf16[64,3584]{1,0:T(8,128)(2,1)S(1)}, bf16[64,3584]{1,0:T(8,128)(2,1)S(1)}, u32[]{:S(2)}, u32[]{:S(2)}) collective-permute-start(bf16[64,3584]{1,0:T(8,128)(2,1)S(1)} %get-tuple-element.23), channel_id=1, source_target_pairs={{0,2},{1,3},{2,0},{3,1},{4,6},{5,7},{6,4},{7,5},{8,10},{9,11},{10,... | collective-permute-start | bytes 1376264 | tf_op jit(solution)/shard_map/ppermute | solution.py:247
  56.3 10.5 %collective-permute-start.5 = (bf16[32,3584]{1,0:T(8,128)(2,1)S(1)}, bf16[32,3584]{1,0:T(8,128)(2,1)S(1)}, u32[]{:S(2)}, u32[]{:S(2)}) collective-permute-start(bf16[32,3584]{1,0:T(8,128)(2,1)S(1)} %slice.170), channel_id=1, source_target_pairs={{0,2},{1,3},{2,0},{3,1},{4,6},{5,7},{6,4},{7,5},{8,10},{9,11},{10,... | collective-permute-start | bytes 688136 | tf_op jit(solution)/shard_map/ppermute | solution.py:247
  64.4 11.2 %copy-start.5 = (bf16[7168]{0:T(1024)(128)(2,1)S(1)}, bf16[7168]{0:T(1024)(128)(2,1)}, u32[]{:S(2)}) copy-start(bf16[7168]{0:T(1024)(128)(2,1)} %param.21) | copy-start | bytes 43012
  64.4 21.6 %copy-start.4 = (bf16[8,7168]{1,0:T(8,128)(2,1)S(1)}, bf16[8,7168]{1,0:T(8,128)(2,1)}, u32[]{:S(2)}) copy-start(bf16[8,7168]{1,0:T(8,128)(2,1)} %param.15) | copy-start | bytes 344068
  64.4 6.1 %collective-permute-start.3 = (bf16[32,3584]{1,0:T(8,128)(2,1)S(1)}, bf16[32,3584]{1,0:T(8,128)(2,1)S(1)}, u32[]{:S(2)}, u32[]{:S(2)}) collective-permute-start(bf16[32,3584]{1,0:T(8,128)(2,1)S(1)} %slice.171), channel_id=1, source_target_pairs={{0,4},{1,5},{2,6},{3,7},{4,0},{5,1},{6,2},{7,3},{8,12},{9,13},{10,... | collective-permute-start | bytes 688136 | tf_op jit(solution)/shard_map/ppermute | solution.py:247
  70.7 6.7 %collective-permute-start.8 = (bf16[8,7168]{1,0:T(8,128)(2,1)S(1)}, bf16[8,7168]{1,0:T(8,128)(2,1)S(1)}, u32[]{:S(2)}, u32[]{:S(2)}) collective-permute-start(bf16[8,7168]{1,0:T(8,128)(2,1)S(1)} %get-tuple-element.43), channel_id=1, source_target_pairs={{0,24},{1,25},{2,26},{3,27},{4,28},{5,29},{6,30},{7,31},{8,16},{9,... | collective-permute-start | bytes 344072 | tf_op jit(solution)/shard_map/ppermute | solution.py:247
  74.4 11.6 %collective-permute-start.7 = (bf16[8,7168]{1,0:T(8,128)(2,1)S(1)}, bf16[8,7168]{1,0:T(8,128)(2,1)S(1)}, u32[]{:S(2)}, u32[]{:S(2)}) collective-permute-start(bf16[8,7168]{1,0:T(8,128)(2,1)S(1)} %get-tuple-element.44), channel_id=1, source_target_pairs={{0,16},{1,17},{2,18},{3,19},{4,20},{5,21},{6,22},{7,23},{8,24},{9,... | collective-permute-start | bytes 344072 | tf_op jit(solution)/shard_map/ppermute | solution.py:247
  75.6 10.4 %collective-permute-start.6 = (bf16[8,7168]{1,0:T(8,128)(2,1)S(1)}, bf16[8,7168]{1,0:T(8,128)(2,1)S(1)}, u32[]{:S(2)}, u32[]{:S(2)}) collective-permute-start(bf16[8,7168]{1,0:T(8,128)(2,1)S(1)} %get-tuple-element.42), channel_id=1, source_target_pairs={{0,8},{1,9},{2,10},{3,11},{4,12},{5,13},{6,14},{7,15},{8,0},{9,1},... | collective-permute-start | bytes 344072 | tf_op jit(solution)/shard_map/ppermute | solution.py:247
  86.3 6.8 %collective-permute-start.11 = (bf16[8,7296]{1,0:T(8,128)(2,1)S(1)}, bf16[8,7296]{1,0:T(8,128)(2,1)S(1)}, u32[]{:S(2)}, u32[]{:S(2)}) collective-permute-start(bf16[8,7296]{1,0:T(8,128)(2,1)S(1)} %pad_maximum_fusion.13), channel_id=1, source_target_pairs={{0,24},{1,25},{2,26},{3,27},{4,28},{5,29},{6,30},{7,31},{8,16},{9,... | collective-permute-start | bytes 350216 | tf_op jit(solution)/shard_map/ppermute | solution.py:247
  88.1 7.4 %collective-permute-start.10 = (bf16[8,7296]{1,0:T(8,128)(2,1)S(1)}, bf16[8,7296]{1,0:T(8,128)(2,1)S(1)}, u32[]{:S(2)}, u32[]{:S(2)}) collective-permute-start(bf16[8,7296]{1,0:T(8,128)(2,1)S(1)} %pad_maximum_fusion.13), channel_id=1, source_target_pairs={{0,16},{1,17},{2,18},{3,19},{4,20},{5,21},{6,22},{7,23},{8,24},{9,... | collective-permute-start | bytes 350216 | tf_op jit(solution)/shard_map/ppermute | solution.py:247
  88.1 7.4 %collective-permute-start.9 = (bf16[8,7296]{1,0:T(8,128)(2,1)S(1)}, bf16[8,7296]{1,0:T(8,128)(2,1)S(1)}, u32[]{:S(2)}, u32[]{:S(2)}) collective-permute-start(bf16[8,7296]{1,0:T(8,128)(2,1)S(1)} %pad_maximum_fusion.13), channel_id=1, source_target_pairs={{0,8},{1,9},{2,10},{3,11},{4,12},{5,13},{6,14},{7,15},{8,0},{9,1},... | collective-permute-start | bytes 350216 | tf_op jit(solution)/shard_map/ppermute | solution.py:247
  90.8 17.6 %collective-permute-start.16 = (bf16[7168,128]{1,0:T(8,128)(2,1)}, bf16[7168,128]{1,0:T(8,128)(2,1)}, u32[]{:S(2)}, u32[]{:S(2)}) collective-permute-start(bf16[7168,128]{1,0:T(8,128)(2,1)} %refs_0_.2), channel_id=1, source_target_pairs={{0,1},{1,0},{2,3},{3,2},{4,5},{5,4},{6,7},{7,6},{8,9},{9,8},{10,11... | collective-permute-start | bytes 5505032 | tf_op jit(solution)/shard_map/ppermute | solution.py:247
  90.8 17.6 %collective-permute-start.17 = (bf16[7168,128]{1,0:T(8,128)(2,1)}, bf16[7168,128]{1,0:T(8,128)(2,1)}, u32[]{:S(2)}, u32[]{:S(2)}) collective-permute-start(bf16[7168,128]{1,0:T(8,128)(2,1)} %refs_2_.1), channel_id=1, source_target_pairs={{0,1},{1,0},{2,3},{3,2},{4,5},{5,4},{6,7},{7,6},{8,9},{9,8},{10,11... | collective-permute-start | bytes 5505032 | tf_op jit(solution)/shard_map/ppermute | solution.py:247
  93.1 12.6 %collective-permute-start.18 = (bf16[128,7168]{1,0:T(8,128)(2,1)}, bf16[128,7168]{1,0:T(8,128)(2,1)}, u32[]{:S(2)}, u32[]{:S(2)}) collective-permute-start(bf16[128,7168]{1,0:T(8,128)(2,1)} %refs_0_.3), channel_id=1, source_target_pairs={{0,1},{1,0},{2,3},{3,2},{4,5},{5,4},{6,7},{7,6},{8,9},{9,8},{10,11... | collective-permute-start | bytes 5505032 | tf_op jit(solution)/shard_map/ppermute | solution.py:247
  95.5 6.2 %collective-permute-start.14 = (bf16[32,3712]{1,0:T(8,128)(2,1)S(1)}, bf16[32,3712]{1,0:T(8,128)(2,1)S(1)}, u32[]{:S(2)}, u32[]{:S(2)}) collective-permute-start(bf16[32,3712]{1,0:T(8,128)(2,1)S(1)} %pad_maximum_fusion.6), channel_id=1, source_target_pairs={{0,2},{1,3},{2,0},{3,1},{4,6},{5,7},{6,4},{7,5},{8,10},{9,11},{10,... | collective-permute-start | bytes 712712 | tf_op jit(solution)/shard_map/ppermute | solution.py:247
  96.2 6.9 %collective-permute-start.12 = (bf16[32,3584]{1,0:T(8,128)(2,1)S(1)}, bf16[32,3584]{1,0:T(8,128)(2,1)S(1)}, u32[]{:S(2)}, u32[]{:S(2)}) collective-permute-start(bf16[32,3584]{1,0:T(8,128)(2,1)S(1)} %pad_maximum_fusion.10), channel_id=1, source_target_pairs={{0,4},{1,5},{2,6},{3,7},{4,0},{5,1},{6,2},{7,3},{8,12},{9,13},{10,... | collective-permute-start | bytes 688136 | tf_op jit(solution)/shard_map/ppermute | solution.py:247
  101.7 10.7 %collective-permute-start.15 = (bf16[64,3712]{1,0:T(8,128)(2,1)S(1)}, bf16[64,3712]{1,0:T(8,128)(2,1)S(1)}, u32[]{:S(2)}, u32[]{:S(2)}) collective-permute-start(bf16[64,3712]{1,0:T(8,128)(2,1)S(1)} %pad_maximum_fusion.3.near_b), channel_id=1, source_target_pairs={{0,4},{1,5},{2,6},{3,7},{4,0},{5,1},{6,2},{7,3},{8,12},{9,13},{10,... | collective-permute-start | bytes 1425416 | tf_op jit(solution)/shard_map/ppermute | solution.py:247
  103.1 9.1 %collective-permute-start.13 = (bf16[64,3584]{1,0:T(8,128)(2,1)S(1)}, bf16[64,3584]{1,0:T(8,128)(2,1)S(1)}, u32[]{:S(2)}, u32[]{:S(2)}) collective-permute-start(bf16[64,3584]{1,0:T(8,128)(2,1)S(1)} %pad_maximum_fusion.4.near_a), channel_id=1, source_target_pairs={{0,2},{1,3},{2,0},{3,1},{4,6},{5,7},{6,4},{7,5},{8,10},{9,11},{10,... | collective-permute-start | bytes 1376264 | tf_op jit(solution)/shard_map/ppermute | solution.py:247
  114.5 10.1 %collective-permute-start.19 = (bf16[64,3584]{1,0:T(8,128)(2,1)S(1)}, bf16[64,3584]{1,0:T(8,128)(2,1)S(1)}, u32[]{:S(2)}, u32[]{:S(2)}) collective-permute-start(bf16[64,3584]{1,0:T(8,128)(2,1)S(1)} %get-tuple-element.29), channel_id=1, source_target_pairs={{0,2},{1,3},{2,0},{3,1},{4,6},{5,7},{6,4},{7,5},{8,10},{9,11},{10,... | collective-permute-start | bytes 1376264 | tf_op jit(solution)/shard_map/ppermute | solution.py:247
  116.7 12.3 %collective-permute-start.21 = (bf16[64,3584]{1,0:T(8,128)(2,1)S(1)}, bf16[64,3584]{1,0:T(8,128)(2,1)S(1)}, u32[]{:S(2)}, u32[]{:S(2)}) collective-permute-start(bf16[64,3584]{1,0:T(8,128)(2,1)S(1)} %get-tuple-element.34), channel_id=1, source_target_pairs={{0,4},{1,5},{2,6},{3,7},{4,0},{5,1},{6,2},{7,3},{8,12},{9,13},{10,... | collective-permute-start | bytes 1376264 | tf_op jit(solution)/shard_map/ppermute | solution.py:247
  124.7 6.7 %collective-permute-start.20 = (bf16[32,3584]{1,0:T(8,128)(2,1)S(1)}, bf16[32,3584]{1,0:T(8,128)(2,1)S(1)}, u32[]{:S(2)}, u32[]{:S(2)}) collective-permute-start(bf16[32,3584]{1,0:T(8,128)(2,1)S(1)} %slice.169), channel_id=1, source_target_pairs={{0,4},{1,5},{2,6},{3,7},{4,0},{5,1},{6,2},{7,3},{8,12},{9,13},{10,... | collective-permute-start | bytes 688136 | tf_op jit(solution)/shard_map/ppermute | solution.py:247
  129.1 6.1 %collective-permute-start.22 = (bf16[32,3584]{1,0:T(8,128)(2,1)S(1)}, bf16[32,3584]{1,0:T(8,128)(2,1)S(1)}, u32[]{:S(2)}, u32[]{:S(2)}) collective-permute-start(bf16[32,3584]{1,0:T(8,128)(2,1)S(1)} %slice.168), channel_id=1, source_target_pairs={{0,2},{1,3},{2,0},{3,1},{4,6},{5,7},{6,4},{7,5},{8,10},{9,11},{10,... | collective-permute-start | bytes 688136 | tf_op jit(solution)/shard_map/ppermute | solution.py:247
  135.2 10.6 %copy-start.1 = (bf16[8,128,576]{1,2,0:T(8,128)(2,1)S(1)}, bf16[8,128,576]{1,2,0:T(8,128)(2,1)}, u32[]{:S(2)}) copy-start(bf16[8,128,576]{1,2,0:T(8,128)(2,1)} %param.16) | copy-start | bytes 3538948
  135.3 6.8 %collective-permute-start.25 = (bf16[8,7168]{1,0:T(8,128)(2,1)S(1)}, bf16[8,7168]{1,0:T(8,128)(2,1)S(1)}, u32[]{:S(2)}, u32[]{:S(2)}) collective-permute-start(bf16[8,7168]{1,0:T(8,128)(2,1)S(1)} %get-tuple-element.40), channel_id=1, source_target_pairs={{0,24},{1,25},{2,26},{3,27},{4,28},{5,29},{6,30},{7,31},{8,16},{9,... | collective-permute-start | bytes 344072 | tf_op jit(solution)/shard_map/ppermute | solution.py:247
  137.4 7.7 %collective-permute-start.24 = (bf16[8,7168]{1,0:T(8,128)(2,1)S(1)}, bf16[8,7168]{1,0:T(8,128)(2,1)S(1)}, u32[]{:S(2)}, u32[]{:S(2)}) collective-permute-start(bf16[8,7168]{1,0:T(8,128)(2,1)S(1)} %get-tuple-element.41), channel_id=1, source_target_pairs={{0,16},{1,17},{2,18},{3,19},{4,20},{5,21},{6,22},{7,23},{8,24},{9,... | collective-permute-start | bytes 344072 | tf_op jit(solution)/shard_map/ppermute | solution.py:247
  138.6 6.5 %collective-permute-start.23 = (bf16[8,7168]{1,0:T(8,128)(2,1)S(1)}, bf16[8,7168]{1,0:T(8,128)(2,1)S(1)}, u32[]{:S(2)}, u32[]{:S(2)}) collective-permute-start(bf16[8,7168]{1,0:T(8,128)(2,1)S(1)} %get-tuple-element.39), channel_id=1, source_target_pairs={{0,8},{1,9},{2,10},{3,11},{4,12},{5,13},{6,14},{7,15},{8,0},{9,1},... | collective-permute-start | bytes 344072 | tf_op jit(solution)/shard_map/ppermute | solution.py:247

commit v4 on v3

--- a/solution.py
+++ b/solution.py
@@ -59,7 +59,8 @@
         body,
         out_shape=tuple(pltpu.VMEM(shape, BF16) for shape in shapes)
         + (jax.ShapeDtypeStruct((8, 128), F32),),
-        in_specs=[pl.BlockSpec(memory_space=pltpu.HBM)] * (len(arrays) + 1),
+        in_specs=[pl.BlockSpec(memory_space=pltpu.HBM)] * len(arrays)
+        + [pl.BlockSpec(memory_space=pl.ANY)],
         out_specs=tuple(in_vmem(len(shapes) + 1)),
         scratch_shapes=[pltpu.SemaphoreType.DMA((count,))],
         compiler_params=pltpu.CompilerParams(vmem_limit_bytes=VMEM_BYTES),
@@ -89,19 +90,6 @@
     return stage(weights, [(depth, wide * len(weights))], copies_of, after)
 
 
-def project_chunks(x, scale, w, send, keep):
-    cut, width = keep.shape
-    for c in range(width // CHUNK):
-        span = pl.ds(c * CHUNK, CHUNK)
-        y = jnp.dot(x, w[:, span], preferred_element_type=F32) * scale
-        keep[:, span] = y[:cut]
-        send[:, span] = y[cut:].astype(BF16)
-
-
-def project_body(x, scale, w, send, keep):
-    project_chunks(x[...], scale[...], w, send, keep)
-
-
 def projected(rows, width):
     return (
         jax.ShapeDtypeStruct((rows // 2, width), BF16),
@@ -109,31 +97,15 @@
     )
 
 
-def project(x, scale, w):
-    rows, depth = x.shape
-    width = w.shape[1]
-    w = pltpu.with_memory_space_constraint(w, pltpu.VMEM)
-    return pl.pallas_call(
-        project_body,
-        out_shape=projected(rows, width),
-        in_specs=in_vmem(3),
-        out_specs=tuple(in_vmem(2)),
-        compiler_params=pltpu.CompilerParams(vmem_limit_bytes=VMEM_BYTES),
-        cost_estimate=pl.CostEstimate(
-            flops=2 * rows * depth * width, bytes_accessed=depth * width, transcendentals=0
-        ),
-    )(x, scale, w)
-
-
-def stream_body(first, x, own, other, send, keep, held, total, sems):
-    cut, width = keep.shape
+def stream_body(picked, own, other, *refs):
+    *outs, held, total, sems = refs
+    groups = len(outs) // 2
+    cut, width = outs[0].shape
     step = min(own.shape[0], 2 * LANES)
     per = own.shape[0] // step
     copies = [
         pltpu.make_async_copy(
-            w.at[pl.ds(r * step, step), pl.ds(first, width)],
-            held.at[pl.ds((i * per + r) * step, step)],
-            sems.at[i, r],
+            w.at[pl.ds(r * step, step)], held.at[pl.ds((i * per + r) * step, step)], sems.at[i, r]
         )
         for i, w in enumerate((own, other))
         for r in range(per)
@@ -142,41 +114,46 @@
         copy.start()
     for k, copy in enumerate(copies):
         copy.wait()
-        rows = x[:, k * step : (k + 1) * step]
-        for c in range(width // CHUNK):
-            span = pl.ds(c * CHUNK, CHUNK)
-            y = jnp.dot(rows, held[pl.ds(k * step, step), span], preferred_element_type=F32)
-            if k > 0:
-                y = y + total[:, span]
-            if k + 1 < len(copies):
-                total[:, span] = y
-            else:
-                keep[:, span] = y[:cut]
-                send[:, span] = y[cut:].astype(BF16)
-
-
-def project_stream(x, own, other, first, width):
-    rows, depth = x.shape
+        for g in range(groups):
+            send, keep = outs[2 * g : 2 * g + 2]
+            rows = picked[g, :, k * step : (k + 1) * step]
+            for c in range(width // CHUNK):
+                span = pl.ds(c * CHUNK, CHUNK)
+                wide = pl.ds(g * width + c * CHUNK, CHUNK)
+                y = jnp.dot(rows, held[pl.ds(k * step, step), wide], preferred_element_type=F32)
+                if k > 0:
+                    y = y + total[:, wide]
+                if k + 1 < len(copies):
+                    total[:, wide] = y
+                else:
+                    keep[:, span] = y[:cut]
+                    send[:, span] = y[cut:].astype(BF16)
+
+
+def project_stream(picked, own, other):
+    groups, rows, depth = picked.shape
+    width = own.shape[1]
     own, other = (pltpu.with_memory_space_constraint(w, pltpu.HBM) for w in (own, other))
-    return pl.pallas_call(
-        functools.partial(stream_body, first),
-        out_shape=projected(rows, width),
+    outs = pl.pallas_call(
+        stream_body,
+        out_shape=projected(rows, width // groups) * groups,
         in_specs=in_vmem(1) + [pl.BlockSpec(memory_space=pltpu.HBM)] * 2,
-        out_specs=tuple(in_vmem(2)),
+        out_specs=tuple(in_vmem(2 * groups)),
         scratch_shapes=[
             pltpu.VMEM((depth, width), BF16),
             pltpu.VMEM((rows, width), F32),
             pltpu.SemaphoreType.DMA((2, max(1, own.shape[0] // (2 * LANES)))),
         ],
-        compiler_params=pltpu.CompilerParams(vmem_limit_bytes=2 * VMEM_BYTES),
+        compiler_params=pltpu.CompilerParams(vmem_limit_bytes=3 * VMEM_BYTES),
         cost_estimate=pl.CostEstimate(
             flops=2 * rows * depth * width, bytes_accessed=2 * depth * width, transcendentals=0
         ),
-    )(x, own, other)
+    )(picked, own, other)
+    return [outs[2 * g : 2 * g + 2] for g in range(groups)]
 
 
 def expert_body(
-    block, label, near_a, far_a, near_b, far_b, w_in, w_out, send, keep, inner_b, weight_b
+    block, label, near_a, far_a, near_b, far_b, w_in, w_out_a, w_out_b, *outs
 ):
     cut, half = near_a.shape
     sums = []
@@ -201,29 +178,35 @@
     lane = lax.broadcasted_iota(jnp.int32, tails.shape, 1)
     mine = lax.rem(lane, label[1]) == label[0]
     weight = jnp.sum(jnp.where(mine, tails, 0.0), axis=1, keepdims=True)
-    weight_b[...] = weight
-    inner_b[...] = turn(inner).astype(BF16)
-    project_chunks(inner.astype(BF16), turn(weight), w_out, send, keep)
+    for g, w_out in enumerate((w_out_a, w_out_b)):
+        send, keep = outs[2 * g : 2 * g + 2]
+        x = (inner if g == 0 else turn(inner)).astype(BF16)
+        scale = turn(weight) if g == 0 else weight
+        for c in range(half // CHUNK):
+            span = pl.ds(c * CHUNK, CHUNK)
+            y = jnp.dot(x, w_out[:, span], preferred_element_type=F32) * scale
+            keep[:, span] = y[:cut]
+            send[:, span] = y[cut:].astype(BF16)
 
 
 def expert(label, tokens, w_in, w_out):
     (near_a, far_a), (near_b, far_b) = tokens
     rows, half = 2 * near_a.shape[0], near_a.shape[1]
-    hid = w_out.shape[0]
-    w_in, w_out = (pltpu.with_memory_space_constraint(w, pltpu.VMEM) for w in (w_in, w_out))
-    return pl.pallas_call(
+    hid = w_out[0].shape[0]
+    w_in, *w_out = (pltpu.with_memory_space_constraint(w, pltpu.VMEM) for w in (w_in, *w_out))
+    outs = pl.pallas_call(
         functools.partial(expert_body, rows // 4),
-        out_shape=projected(rows, half)
-        + (jax.ShapeDtypeStruct((rows, hid), BF16), jax.ShapeDtypeStruct((rows, 1), F32)),
-        in_specs=[pl.BlockSpec(memory_space=pltpu.SMEM)] + in_vmem(6),
+        out_shape=projected(rows, half) * 2,
+        in_specs=[pl.BlockSpec(memory_space=pltpu.SMEM)] + in_vmem(7),
         out_specs=tuple(in_vmem(4)),
         compiler_params=pltpu.CompilerParams(vmem_limit_bytes=VMEM_BYTES),
         cost_estimate=pl.CostEstimate(
-            flops=2 * rows * (w_in.size + w_out.size),
-            bytes_accessed=w_in.size + w_out.size,
+            flops=2 * rows * (w_in.size + 2 * w_out[0].size),
+            bytes_accessed=w_in.size + 2 * w_out[0].size,
             transcendentals=rows * hid,
         ),
-    )(label, near_a, far_a, near_b, far_b, w_in, w_out)
+    )(label, near_a, far_a, near_b, far_b, w_in, *w_out)
+    return outs[:2], outs[2:]
 
 
 def relative_order(first, second, planes):
@@ -284,9 +267,6 @@
             axis_index_groups=[list(range(c, devices, 2)) for c in (0, 1)],
         )
 
-        after = latent_out[0, :16, :128]
-        w_in, _ = stage_beside((w_gate, w_gate_other, w_up, w_up_other), after)
-        *w_out, _ = stage_columns(w_down, w_down_other, 2, after)
         even = core == 0
         heads_up = jnp.concatenate(
             [
@@ -295,7 +275,9 @@
             ],
             axis=0,
         )
-        by_heads, heads_up = lax.optimization_barrier((by_heads, heads_up))
+        by_heads, heads_up, w_gate_other, w_up_other, w_down_other = lax.optimization_barrier(
+            (by_heads, heads_up, w_gate_other, w_up_other, w_down_other)
+        )
 
         orders = [relative_order(first, second, planes) for first, second in axes]
         experts = expert_slot.shape[0]
@@ -329,21 +311,21 @@
         for order in orders:
             place = jnp.bitwise_xor(jnp.asarray(order), me) // 2
             wanted = (place[:, None] * rows + jnp.arange(rows, dtype=jnp.int32)).reshape(-1, 1)
-            pick = (wanted == jnp.arange(total_rows, dtype=jnp.int32)[None, :]).astype(BF16)
-            picks.append(jnp.dot(pick, flat_values, preferred_element_type=F32).astype(BF16))
-        attended = sum_to_owner(
-            [project_stream(picks[g], out_proj, out_proj_other, g * half, half) for g in (0, 1)],
-            rows,
-        )
+            picks.append(wanted == jnp.arange(total_rows, dtype=jnp.int32)[None, :])
+        picks = jnp.concatenate(picks, axis=0).astype(BF16)
+        picked = jnp.dot(picks, flat_values, preferred_element_type=F32).astype(BF16)
+        products = project_stream(picked.reshape(2, total_rows, -1), out_proj, out_proj_other)
+        attended = sum_to_owner(products, rows)
         mixed = hidden.astype(F32) + attended
         scale_rows = lax.rsqrt(jnp.mean(mixed * mixed, axis=1, keepdims=True) + norm_eps)
         normed = (mixed * scale_rows * norm_gain.astype(F32)).astype(BF16)
 
+        w_in, _ = stage_beside((w_gate, w_gate_other, w_up, w_up_other), normed)
+        *w_out, _ = stage_columns(w_down, w_down_other, 2, normed)
         tokens = to_all(jnp.concatenate([normed, tail], axis=1), half)
         label = jnp.stack([me // SLABS, jnp.int32(experts)])
-        *product_a, inner_b, weight_b = expert(label, tokens, w_in, w_out[0])
-        product_b = project(inner_b, weight_b, w_out[1])
-        return (mixed + sum_to_owner([product_a, product_b], rows)).astype(BF16)
+        products = expert(label, tokens, w_in, w_out)
+        return (mixed + sum_to_owner(products, rows)).astype(BF16)
 
     return body
 

time: 146 us -> 141 us (0.966)
  waiting for transfers between devices: 83.6 us -> 72.7 us
  starting transfers between devices: 33.7 us -> 40.9 us
  Pallas kernels: 16.2 us -> 14.7 us
    ppermute x26, waiting for transfers between devices: 61.3 us -> 53.7 us  [swap(): return lax.ppermute(x, 'ep', [(i, i ^ mask) for i in range(devices)])]
    ppermute x26, starting transfers between devices: 25.4 us -> 32.6 us  [swap(): return lax.ppermute(x, 'ep', [(i, i ^ mask) for i in range(devices)])]
    all_to_all x1, waiting for transfers between devices: 22.3 us -> 18.9 us  [body(): lax.all_to_all(latent_out, 'ep', split_axis=1, concat_axis=0, tiled=True,...]
    pallas_call x3 -> x1, Pallas kernels: 7.63 us -> 5.95 us  [project_stream(): pl.pallas_call(stream_body, out_shape=projected(rows, width // groups) *...]
  transfers between devices with their start and end apart: 27 -> 27, of which waited for: 19 -> 17; matrix products, arithmetic and copies ran while one was open for 7% -> 7% of each run, Pallas kernels for 7% -> 5%
where the time goes in v4:
time: 141 us; the launch traced here: 140 us
  waiting for transfers between devices  72.7 us (52%)
  starting transfers between devices  40.9 us (29%)
  Pallas kernels  14.7 us (10%)
  other arithmetic  4.77 us (3%)
  matrix products  3.95 us (3%)
  local copies, waits for them, and re-layouts  2.92 us (2%)
    ppermute x26, waiting for transfers between devices, swap(): return lax.ppermute(x, 'ep', [(i, i ^ mask) for i in range(devices)])  53.7 us
    ppermute x26, starting transfers between devices, swap(): return lax.ppermute(x, 'ep', [(i, i ^ mask) for i in range(devices)])  32.6 us
    all_to_all x1, waiting for transfers between devices, body(): lax.all_to_all(latent_out, 'ep', split_axis=1, concat_axis=0, tiled=True,...  18.9 us
    all_to_all x1, starting transfers between devices, body(): lax.all_to_all(latent_out, 'ep', split_axis=1, concat_axis=0, tiled=True,...  8.31 us
    pallas_call x2, Pallas kernels, stage(): pl.pallas_call(body, out_shape=tuple((pltpu.VMEM(shape, BF16) for shape i...  6.45 us
    pallas_call x1, Pallas kernels, project_stream(): pl.pallas_call(stream_body, out_shape=projected(rows, width // groups) *...  5.95 us
  transfers between devices with their start and end apart: 27, of which 17 were waited for; matrix products, arithmetic and copies ran while one was open for 7% of the time, Pallas kernels for 5%

profile of v4, /device:TPU:0, one launch (start us, length us, event | category | flops | bytes accessed | tf_op | source)
XLA Modules:
  0.0 140.4 jit_solution(17237553516510644912)
XLA Ops:
  0.5 0.8 copy-done
  1.3 2.3 %convolution_multiply_fusion = f32[8,128,256]{2,1,0:T(8,128)S(1)} fusion(bf16[8,128,576]{1,2,0:T(8,128)(2,1)S(1)} %copy-done, bf16[8,256,576]{1,2,0:T(8,128)(2,1)} %param.17), kind=kOutput, calls=%fused_computation.4 | convolution fusion | flops 302252032 | bytes 4587520 | tf_op jit(solution)/shard_map/bhr,bpr->bhp/dot_general | solution.py:23
  3.6 2.2 %fusion.51 = (f32[8,128]{1,0:T(8,128)S(1)}, f32[8,128,256]{2,1,0:T(8,128)S(1)}) fusion(f32[8,128,256]{2,1,0:T(8,128)S(1)} %convolution_multiply_fusion, s32[8]{0:T(128)S(1)} %copy-done.11), kind=kOutput, calls=%fused_computation.109 | output fusion | flops 1573119 | bytes 2101280 | tf_op jit(solution)/shard_map/sub | solution.py:26
  5.9 0.8 fusion.3
  6.7 1.5 %copy.33 = bf16[8,128,512]{2,0,1:T(8,128)(2,1)} copy(bf16[8,128,512]{2,1,0:T(8,128)(2,1)S(1)} %fusion.3) | data formatting | bytes 2097152 | tf_op jit(solution)/shard_map/convert_element_type | solution.py:30
  8.3 8.3 %all-to-all-start = ((bf16[8,128,512]{2,0,1:T(8,128)(2,1)}), bf16[8,128,512]{2,0,1:T(8,128)(2,1)S(1)}, u32[]{:S(2)}, u32[]{:S(2)}) async-start(bf16[8,128,512]{2,0,1:T(8,128)(2,1)} %copy.33), calls=%async_computation | async-start | bytes 2097152 | tf_op jit(solution)/shard_map/all_to_all | solution.py:265
  16.7 0.5 collective-permute-start.2
  18.2 3.7 %collective-permute-done = bf16[4,512,128]{2,1,0:T(8,128)(2,1)S(1)} collective-permute-done((bf16[4,512,128]{2,1,0:T(8,128)(2,1)S(1)}, bf16[4,512,128]{2,1,0:T(8,128)(2,1)S(1)}, u32[]{:S(2)}, u32[]{:S(2)}) %collective-permute-start) | collective-permute-done | bytes 524320 | tf_op jit(solution)/shard_map/ppermute | solution.py:230
  22.1 18.9 %all-to-all-done = bf16[8,128,512]{2,0,1:T(8,128)(2,1)S(1)} async-done(((bf16[8,128,512]{2,0,1:T(8,128)(2,1)}), bf16[8,128,512]{2,0,1:T(8,128)(2,1)S(1)}, u32[]{:S(2)}, u32[]{:S(2)}) %all-to-all-start) | async-done | bytes 1048608 | tf_op jit(solution)/shard_map/all_to_all | solution.py:265
  41.2 0.5 convolution_convert_fusion.1
  42.1 6.0 %shard_map.145 = (bf16[64,3584]{1,0:T(8,128)(2,1)S(1)}, f32[64,3584]{1,0:T(8,128)S(1)}, bf16[64,3584]{1,0:T(8,128)(2,1)S(1)}, f32[64,3584]{1,0:T(8,128)S(1)}) custom-call(bf16[2,128,1024]{2,1,0:T(8,128)(2,1)S(1)} %bitcast.19, bf16[512,7168]{1,0:T(8,128)(2,1)} %own.1, bf16[512,7168]{1,0:T(8,128)(2,1)} %collective-permute-done.4.other), custom_call_target="tpu_custom_call" | custom-call | flops 1879048192 | bytes 14680064 | tf_op jit(solution)/shard_map/pallas_call | solution.py:137
  48.0 0.6 collective-permute-start.5
  48.9 2.0 %collective-permute-start.7 = (bf16[64,3584]{1,0:T(8,128)(2,1)S(1)}, bf16[64,3584]{1,0:T(8,128)(2,1)S(1)}, u32[]{:S(2)}, u32[]{:S(2)}) collective-permute-start(bf16[64,3584]{1,0:T(8,128)(2,1)S(1)} %get-tuple-element.26), channel_id=1, source_target_pairs={{0,4},{1,5},{2,6},{3,7},{4,0},{5,1},{6,2},{7,3},{8,12},{9,13},{10,... | collective-permute-start | bytes 1376264 | tf_op jit(solution)/shard_map/ppermute | solution.py:230
  50.8 7.0 %collective-permute-done.5 = bf16[64,3584]{1,0:T(8,128)(2,1)S(1)} collective-permute-done((bf16[64,3584]{1,0:T(8,128)(2,1)S(1)}, bf16[64,3584]{1,0:T(8,128)(2,1)S(1)}, u32[]{:S(2)}, u32[]{:S(2)}) %collective-permute-start.5) | collective-permute-done | bytes 458784 | tf_op jit(solution)/shard_map/ppermute | solution.py:230
  57.9 2.6 %collective-permute-start.6 = (bf16[32,3584]{1,0:T(8,128)(2,1)S(1)}, bf16[32,3584]{1,0:T(8,128)(2,1)S(1)}, u32[]{:S(2)}, u32[]{:S(2)}) collective-permute-start(bf16[32,3584]{1,0:T(8,128)(2,1)S(1)} %slice.165), channel_id=1, source_target_pairs={{0,4},{1,5},{2,6},{3,7},{4,0},{5,1},{6,2},{7,3},{8,12},{9,13},{10,... | collective-permute-start | bytes 688136 | tf_op jit(solution)/shard_map/ppermute | solution.py:230
  60.7 1.7 %collective-permute-start.8 = (bf16[32,3584]{1,0:T(8,128)(2,1)S(1)}, bf16[32,3584]{1,0:T(8,128)(2,1)S(1)}, u32[]{:S(2)}, u32[]{:S(2)}) collective-permute-start(bf16[32,3584]{1,0:T(8,128)(2,1)S(1)} %slice.164), channel_id=1, source_target_pairs={{0,2},{1,3},{2,0},{3,1},{4,6},{5,7},{6,4},{7,5},{8,10},{9,11},{10,... | collective-permute-start | bytes 688136 | tf_op jit(solution)/shard_map/ppermute | solution.py:230
  62.4 2.2 %collective-permute-done.6 = bf16[32,3584]{1,0:T(8,128)(2,1)S(1)} collective-permute-done((bf16[32,3584]{1,0:T(8,128)(2,1)S(1)}, bf16[32,3584]{1,0:T(8,128)(2,1)S(1)}, u32[]{:S(2)}, u32[]{:S(2)}) %collective-permute-start.6) | collective-permute-done | bytes 229408 | tf_op jit(solution)/shard_map/ppermute | solution.py:230
  64.6 2.2 %collective-permute-done.8 = bf16[32,3584]{1,0:T(8,128)(2,1)S(1)} collective-permute-done((bf16[32,3584]{1,0:T(8,128)(2,1)S(1)}, bf16[32,3584]{1,0:T(8,128)(2,1)S(1)}, u32[]{:S(2)}, u32[]{:S(2)}) %collective-permute-start.8) | collective-permute-done | bytes 229408 | tf_op jit(solution)/shard_map/ppermute | solution.py:230
  66.9 3.6 %collective-permute-start.10 = (bf16[8,7168]{1,0:T(8,128)(2,1)S(1)}, bf16[8,7168]{1,0:T(8,128)(2,1)S(1)}, u32[]{:S(2)}, u32[]{:S(2)}) collective-permute-start(bf16[8,7168]{1,0:T(8,128)(2,1)S(1)} %get-tuple-element.46), channel_id=1, source_target_pairs={{0,16},{1,17},{2,18},{3,19},{4,20},{5,21},{6,22},{7,23},{8,24},{9,... | collective-permute-start | bytes 344072 | tf_op jit(solution)/shard_map/ppermute | solution.py:230
  70.5 2.1 %collective-permute-start.11 = (bf16[8,7168]{1,0:T(8,128)(2,1)S(1)}, bf16[8,7168]{1,0:T(8,128)(2,1)S(1)}, u32[]{:S(2)}, u32[]{:S(2)}) collective-permute-start(bf16[8,7168]{1,0:T(8,128)(2,1)S(1)} %get-tuple-element.45), channel_id=1, source_target_pairs={{0,24},{1,25},{2,26},{3,27},{4,28},{5,29},{6,30},{7,31},{8,16},{9,... | collective-permute-start | bytes 344072 | tf_op jit(solution)/shard_map/ppermute | solution.py:230
  72.7 1.4 %collective-permute-done.10 = bf16[8,7168]{1,0:T(8,128)(2,1)S(1)} collective-permute-done((bf16[8,7168]{1,0:T(8,128)(2,1)S(1)}, bf16[8,7168]{1,0:T(8,128)(2,1)S(1)}, u32[]{:S(2)}, u32[]{:S(2)}) %collective-permute-start.10) | collective-permute-done | bytes 114720 | tf_op jit(solution)/shard_map/ppermute | solution.py:230
  74.1 3.3 %collective-permute-done.11 = bf16[8,7168]{1,0:T(8,128)(2,1)S(1)} collective-permute-done((bf16[8,7168]{1,0:T(8,128)(2,1)S(1)}, bf16[8,7168]{1,0:T(8,128)(2,1)S(1)}, u32[]{:S(2)}, u32[]{:S(2)}) %collective-permute-start.11) | collective-permute-done | bytes 114720 | tf_op jit(solution)/shard_map/ppermute | solution.py:230
  77.4 2.7 %collective-permute-done.9 = bf16[8,7168]{1,0:T(8,128)(2,1)S(1)} collective-permute-done((bf16[8,7168]{1,0:T(8,128)(2,1)S(1)}, bf16[8,7168]{1,0:T(8,128)(2,1)S(1)}, u32[]{:S(2)}, u32[]{:S(2)}) %collective-permute-start.9) | collective-permute-done | bytes 114720 | tf_op jit(solution)/shard_map/ppermute | solution.py:230
  80.5 3.1 %collective-permute-start.13 = (bf16[8,7296]{1,0:T(8,128)(2,1)S(1)}, bf16[8,7296]{1,0:T(8,128)(2,1)S(1)}, u32[]{:S(2)}, u32[]{:S(2)}) collective-permute-start(bf16[8,7296]{1,0:T(8,128)(2,1)S(1)} %pad_maximum_fusion.10), channel_id=1, source_target_pairs={{0,16},{1,17},{2,18},{3,19},{4,20},{5,21},{6,22},{7,23},{8,24},{9,... | collective-permute-start | bytes 350216 | tf_op jit(solution)/shard_map/ppermute | solution.py:230
  83.5 1.3 collective-permute-start.14
  84.8 1.7 %collective-permute-done.12 = bf16[8,7296]{1,0:T(8,128)(2,1)S(1)} collective-permute-done((bf16[8,7296]{1,0:T(8,128)(2,1)S(1)}, bf16[8,7296]{1,0:T(8,128)(2,1)S(1)}, u32[]{:S(2)}, u32[]{:S(2)}) %collective-permute-start.12) | collective-permute-done | bytes 116768 | tf_op jit(solution)/shard_map/ppermute | solution.py:230
  86.5 3.6 %collective-permute-done.14 = bf16[8,7296]{1,0:T(8,128)(2,1)S(1)} collective-permute-done((bf16[8,7296]{1,0:T(8,128)(2,1)S(1)}, bf16[8,7296]{1,0:T(8,128)(2,1)S(1)}, u32[]{:S(2)}, u32[]{:S(2)}) %collective-permute-start.14) | collective-permute-done | bytes 116768 | tf_op jit(solution)/shard_map/ppermute | solution.py:230
  90.1 0.8 collective-permute-start.17
  90.9 1.6 %collective-permute-start.15 = (bf16[32,3584]{1,0:T(8,128)(2,1)S(1)}, bf16[32,3584]{1,0:T(8,128)(2,1)S(1)}, u32[]{:S(2)}, u32[]{:S(2)}) collective-permute-start(bf16[32,3584]{1,0:T(8,128)(2,1)S(1)} %pad_maximum_fusion.9), channel_id=1, source_target_pairs={{0,4},{1,5},{2,6},{3,7},{4,0},{5,1},{6,2},{7,3},{8,12},{9,13},{10,... | collective-permute-start | bytes 688136 | tf_op jit(solution)/shard_map/ppermute | solution.py:230
  92.6 5.2 %collective-permute-done.17 = bf16[32,3712]{1,0:T(8,128)(2,1)S(1)} collective-permute-done((bf16[32,3712]{1,0:T(8,128)(2,1)S(1)}, bf16[32,3712]{1,0:T(8,128)(2,1)S(1)}, u32[]{:S(2)}, u32[]{:S(2)}) %collective-permute-start.17) | collective-permute-done | bytes 237600 | tf_op jit(solution)/shard_map/ppermute | solution.py:230
  97.8 1.6 %collective-permute-start.18 = (bf16[64,3712]{1,0:T(8,128)(2,1)S(1)}, bf16[64,3712]{1,0:T(8,128)(2,1)S(1)}, u32[]{:S(2)}, u32[]{:S(2)}) collective-permute-start(bf16[64,3712]{1,0:T(8,128)(2,1)S(1)} %pad_maximum_fusion.3.near_b), channel_id=1, source_target_pairs={{0,4},{1,5},{2,6},{3,7},{4,0},{5,1},{6,2},{7,3},{8,12},{9,13},{10,... | collective-permute-start | bytes 1425416 | tf_op jit(solution)/shard_map/ppermute | solution.py:230
  99.4 1.0 collective-permute-start.16
  100.5 2.6 %shard_map.147 = (bf16[256,3584]{1,0:T(8,128)(2,1)S(1)}, bf16[256,3584]{1,0:T(8,128)(2,1)S(1)}, f32[8,128]{1,0:T(8,128)}) custom-call(bf16[128,7168]{1,0:T(8,128)(2,1)} %refs_0_.3, bf16[128,7168]{1,0:T(8,128)(2,1)} %collective-permute-done.3.refs_1_, bf16[8,7168]{1,0:T(8,128)(2,1)S(1)} %multiply_convert_fusion.refs_4_.refs_2_), custom_call_target="tpu_custom_call" | custom-call | bytes 7340032 | tf_op jit(solution)/shard_map/pallas_call | solution.py:58
  103.1 3.8 %shard_map.146 = (bf16[7168,512]{1,0:T(8,128)(2,1)S(1)}, f32[8,128]{1,0:T(8,128)}) custom-call(bf16[7168,128]{1,0:T(8,128)(2,1)} %refs_0_.2, bf16[7168,128]{1,0:T(8,128)(2,1)} %collective-permute-done.1.refs_1_, bf16[7168,128]{1,0:T(8,128)(2,1)} %refs_2_.1, bf16[7168,128]{1,0:T(8,128)(2,1)} %collective-permute-done.2.refs_3_, ...), custom_call_target="tpu_custom_call" | custom-call | bytes 14680064 | tf_op jit(solution)/shard_map/pallas_call | solution.py:58
  106.9 4.9 %collective-permute-done.16.far_a = bf16[64,3584]{1,0:T(8,128)(2,1)S(1)} collective-permute-done((bf16[64,3584]{1,0:T(8,128)(2,1)S(1)}, bf16[64,3584]{1,0:T(8,128)(2,1)S(1)}, u32[]{:S(2)}, u32[]{:S(2)}) %collective-permute-start.16) | collective-permute-done | bytes 458784 | tf_op jit(solution)/shard_map/ppermute | solution.py:230
  111.9 2.3 %shard_map.148 = (bf16[64,3584]{1,0:T(8,128)(2,1)S(1)}, f32[64,3584]{1,0:T(8,128)S(1)}, bf16[64,3584]{1,0:T(8,128)(2,1)S(1)}, f32[64,3584]{1,0:T(8,128)S(1)}) custom-call(s32[2]{0:T(128)S(1)} %pad_add_fusion.label, bf16[64,3584]{1,0:T(8,128)(2,1)S(1)} %pad_maximum_fusion.4.near_a, bf16[64,3584]{1,0:T(8,128)(2,1)S(1)} %collective-permute-done.16.far_a, ...), custom_call_target="tpu_custom_call" | custom-call | flops 1409286144 | bytes 5505024 | tf_op jit(solution)/shard_map/pallas_call | solution.py:197
  114.2 0.7 collective-permute-start.21
  114.9 1.8 %collective-permute-start.19 = (bf16[64,3584]{1,0:T(8,128)(2,1)S(1)}, bf16[64,3584]{1,0:T(8,128)(2,1)S(1)}, u32[]{:S(2)}, u32[]{:S(2)}) collective-permute-start(bf16[64,3584]{1,0:T(8,128)(2,1)S(1)} %get-tuple-element.34), channel_id=1, source_target_pairs={{0,2},{1,3},{2,0},{3,1},{4,6},{5,7},{6,4},{7,5},{8,10},{9,11},{10,... | collective-permute-start | bytes 1376264 | tf_op jit(solution)/shard_map/ppermute | solution.py:230
  116.7 6.4 %collective-permute-done.21 = bf16[64,3584]{1,0:T(8,128)(2,1)S(1)} collective-permute-done((bf16[64,3584]{1,0:T(8,128)(2,1)S(1)}, bf16[64,3584]{1,0:T(8,128)(2,1)S(1)}, u32[]{:S(2)}, u32[]{:S(2)}) %collective-permute-start.21) | collective-permute-done | bytes 458784 | tf_op jit(solution)/shard_map/ppermute | solution.py:230
  123.2 1.3 collective-permute-start.22
  124.6 0.9 collective-permute-start.20
  125.5 3.7 %collective-permute-done.22 = bf16[32,3584]{1,0:T(8,128)(2,1)S(1)} collective-permute-done((bf16[32,3584]{1,0:T(8,128)(2,1)S(1)}, bf16[32,3584]{1,0:T(8,128)(2,1)S(1)}, u32[]{:S(2)}, u32[]{:S(2)}) %collective-permute-start.22) | collective-permute-done | bytes 229408 | tf_op jit(solution)/shard_map/ppermute | solution.py:230
  129.4 1.4 collective-permute-done.20
  130.9 2.1 %collective-permute-start.24 = (bf16[8,7168]{1,0:T(8,128)(2,1)S(1)}, bf16[8,7168]{1,0:T(8,128)(2,1)S(1)}, u32[]{:S(2)}, u32[]{:S(2)}) collective-permute-start(bf16[8,7168]{1,0:T(8,128)(2,1)S(1)} %get-tuple-element.43), channel_id=1, source_target_pairs={{0,16},{1,17},{2,18},{3,19},{4,20},{5,21},{6,22},{7,23},{8,24},{9,... | collective-permute-start | bytes 344072 | tf_op jit(solution)/shard_map/ppermute | solution.py:230
  133.0 2.3 %collective-permute-start.25 = (bf16[8,7168]{1,0:T(8,128)(2,1)S(1)}, bf16[8,7168]{1,0:T(8,128)(2,1)S(1)}, u32[]{:S(2)}, u32[]{:S(2)}) collective-permute-start(bf16[8,7168]{1,0:T(8,128)(2,1)S(1)} %get-tuple-element.42), channel_id=1, source_target_pairs={{0,24},{1,25},{2,26},{3,27},{4,28},{5,29},{6,30},{7,31},{8,16},{9,... | collective-permute-start | bytes 344072 | tf_op jit(solution)/shard_map/ppermute | solution.py:230
  135.3 1.6 %collective-permute-done.23 = bf16[8,7168]{1,0:T(8,128)(2,1)S(1)} collective-permute-done((bf16[8,7168]{1,0:T(8,128)(2,1)S(1)}, bf16[8,7168]{1,0:T(8,128)(2,1)S(1)}, u32[]{:S(2)}, u32[]{:S(2)}) %collective-permute-start.23) | collective-permute-done | bytes 114720 | tf_op jit(solution)/shard_map/ppermute | solution.py:230
  136.9 2.7 %collective-permute-done.25 = bf16[8,7168]{1,0:T(8,128)(2,1)S(1)} collective-permute-done((bf16[8,7168]{1,0:T(8,128)(2,1)S(1)}, bf16[8,7168]{1,0:T(8,128)(2,1)S(1)}, u32[]{:S(2)}, u32[]{:S(2)}) %collective-permute-start.25) | collective-permute-done | bytes 114720 | tf_op jit(solution)/shard_map/ppermute | solution.py:230
  139.7 0.7 fusion.27
  (83 shorter events, 3.9 us)
Async XLA Ops:
  0.0 1.3 copy-start
  0.0 3.6 %copy-start.11 = (s32[8]{0:T(128)S(1)}, s32[8]{0:T(128)}, u32[]{:S(2)}) copy-start(s32[8]{0:T(128)} %param.18) | copy-start | bytes 100
  0.0 42.0 %collective-permute-start.4 = (bf16[512,7168]{1,0:T(8,128)(2,1)}, bf16[512,7168]{1,0:T(8,128)(2,1)}, u32[]{:S(2)}, u32[]{:S(2)}) collective-permute-start(bf16[512,7168]{1,0:T(8,128)(2,1)} %own.1), channel_id=1, source_target_pairs={{0,1},{1,0},{2,3},{3,2},{4,5},{5,4},{6,7},{7,6},{8,9},{9,8},{10,11... | collective-permute-start | bytes 22020104 | tf_op jit(solution)/shard_map/ppermute | solution.py:230
  3.6 2.3 %copy-start.2 = (bf16[8,256,576]{1,2,0:T(8,128)(2,1)S(1)}, bf16[8,256,576]{1,2,0:T(8,128)(2,1)}, u32[]{:S(2)}) copy-start(bf16[8,256,576]{1,2,0:T(8,128)(2,1)} %param.17) | copy-start | bytes 7077892
  6.7 10.6 %copy-start.3 = (bf16[4,512,128]{2,1,0:T(8,128)(2,1)S(1)}, bf16[4,512,128]{2,1,0:T(8,128)(2,1)}, u32[]{:S(2)}) copy-start(bf16[4,512,128]{2,1,0:T(8,128)(2,1)} %param.19) | copy-start | bytes 1572868
  6.7 11.0 %copy-start.9 = (s32[16]{0:T(128)S(1)}, s32[16]{0:T(128)}, u32[]{:S(2)}) copy-start(s32[16]{0:T(128)} %constant.70.clone) | copy-start | bytes 196
  6.7 11.0 %copy-start.10 = (s32[16]{0:T(128)S(1)}, s32[16]{0:T(128)}, u32[]{:S(2)}) copy-start(s32[16]{0:T(128)} %constant.71.clone) | copy-start | bytes 196
  8.3 32.8 %all-to-all-start = ((bf16[8,128,512]{2,0,1:T(8,128)(2,1)}), bf16[8,128,512]{2,0,1:T(8,128)(2,1)S(1)}, u32[]{:S(2)}, u32[]{:S(2)}) async-start(bf16[8,128,512]{2,0,1:T(8,128)(2,1)} %copy.33), calls=%async_computation | async-start | bytes 2097152 | tf_op jit(solution)/shard_map/all_to_all | solution.py:265
  16.6 24.5 %collective-permute-start.1 = (bf16[7168,128]{1,0:T(8,128)(2,1)}, bf16[7168,128]{1,0:T(8,128)(2,1)}, u32[]{:S(2)}, u32[]{:S(2)}) collective-permute-start(bf16[7168,128]{1,0:T(8,128)(2,1)} %refs_0_.2), channel_id=1, source_target_pairs={{0,1},{1,0},{2,3},{3,2},{4,5},{5,4},{6,7},{7,6},{8,9},{9,8},{10,11... | collective-permute-start | bytes 5505032 | tf_op jit(solution)/shard_map/ppermute | solution.py:230
  16.7 24.5 %collective-permute-start.2 = (bf16[7168,128]{1,0:T(8,128)(2,1)}, bf16[7168,128]{1,0:T(8,128)(2,1)}, u32[]{:S(2)}, u32[]{:S(2)}) collective-permute-start(bf16[7168,128]{1,0:T(8,128)(2,1)} %refs_2_.1), channel_id=1, source_target_pairs={{0,1},{1,0},{2,3},{3,2},{4,5},{5,4},{6,7},{7,6},{8,9},{9,8},{10,11... | collective-permute-start | bytes 5505032 | tf_op jit(solution)/shard_map/ppermute | solution.py:230
  17.2 24.0 %collective-permute-start.3 = (bf16[128,7168]{1,0:T(8,128)(2,1)}, bf16[128,7168]{1,0:T(8,128)(2,1)}, u32[]{:S(2)}, u32[]{:S(2)}) collective-permute-start(bf16[128,7168]{1,0:T(8,128)(2,1)} %refs_0_.3), channel_id=1, source_target_pairs={{0,1},{1,0},{2,3},{3,2},{4,5},{5,4},{6,7},{7,6},{8,9},{9,8},{10,11... | collective-permute-start | bytes 5505032 | tf_op jit(solution)/shard_map/ppermute | solution.py:230
  17.3 4.7 %collective-permute-start = (bf16[4,512,128]{2,1,0:T(8,128)(2,1)S(1)}, bf16[4,512,128]{2,1,0:T(8,128)(2,1)S(1)}, u32[]{:S(2)}, u32[]{:S(2)}) collective-permute-start(bf16[4,512,128]{2,1,0:T(8,128)(2,1)S(1)} %copy-done.3), channel_id=1, source_target_pairs={{0,1},{1,0},{2,3},{3,2},{4,5},{5,4},{6,7},{7,6},{8,9},{9,8},{10,11... | collective-permute-start | bytes 1572872 | tf_op jit(solution)/shard_map/ppermute | solution.py:230
  42.0 6.6 %copy-start.6 = (s32[8,2]{0,1:T(2,128)S(1)}, s32[8,2]{0,1:T(2,128)}, u32[]{:S(2)}) copy-start(s32[8,2]{0,1:T(2,128)} %param.22) | copy-start | bytes 196
  42.1 6.6 %copy-start.8 = (s32[4]{0:T(128)S(1)}, s32[4]{0:T(128)}, u32[]{:S(2)}) copy-start(s32[4]{0:T(128)} %param.24) | copy-start | bytes 52
  42.1 6.7 %copy-start.7 = (f32[8,2]{0,1:T(2,128)S(1)}, f32[8,2]{0,1:T(2,128)}, u32[]{:S(2)}) copy-start(f32[8,2]{0,1:T(2,128)} %param.23) | copy-start | bytes 196
  48.0 9.8 %collective-permute-start.5 = (bf16[64,3584]{1,0:T(8,128)(2,1)S(1)}, bf16[64,3584]{1,0:T(8,128)(2,1)S(1)}, u32[]{:S(2)}, u32[]{:S(2)}) collective-permute-start(bf16[64,3584]{1,0:T(8,128)(2,1)S(1)} %get-tuple-element.24), channel_id=1, source_target_pairs={{0,2},{1,3},{2,0},{3,1},{4,6},{5,7},{6,4},{7,5},{8,10},{9,11},{10,... | collective-permute-start | bytes 1376264 | tf_op jit(solution)/shard_map/ppermute | solution.py:230
  48.9 11.7 %collective-permute-start.7 = (bf16[64,3584]{1,0:T(8,128)(2,1)S(1)}, bf16[64,3584]{1,0:T(8,128)(2,1)S(1)}, u32[]{:S(2)}, u32[]{:S(2)}) collective-permute-start(bf16[64,3584]{1,0:T(8,128)(2,1)S(1)} %get-tuple-element.26), channel_id=1, source_target_pairs={{0,4},{1,5},{2,6},{3,7},{4,0},{5,1},{6,2},{7,3},{8,12},{9,13},{10,... | collective-permute-start | bytes 1376264 | tf_op jit(solution)/shard_map/ppermute | solution.py:230
  57.9 6.6 %collective-permute-start.6 = (bf16[32,3584]{1,0:T(8,128)(2,1)S(1)}, bf16[32,3584]{1,0:T(8,128)(2,1)S(1)}, u32[]{:S(2)}, u32[]{:S(2)}) collective-permute-start(bf16[32,3584]{1,0:T(8,128)(2,1)S(1)} %slice.165), channel_id=1, source_target_pairs={{0,4},{1,5},{2,6},{3,7},{4,0},{5,1},{6,2},{7,3},{8,12},{9,13},{10,... | collective-permute-start | bytes 688136 | tf_op jit(solution)/shard_map/ppermute | solution.py:230
  60.6 11.9 %copy-start.5 = (bf16[7168]{0:T(1024)(128)(2,1)S(1)}, bf16[7168]{0:T(1024)(128)(2,1)}, u32[]{:S(2)}) copy-start(bf16[7168]{0:T(1024)(128)(2,1)} %param.21) | copy-start | bytes 43012
  60.7 19.4 %copy-start.4 = (bf16[8,7168]{1,0:T(8,128)(2,1)S(1)}, bf16[8,7168]{1,0:T(8,128)(2,1)}, u32[]{:S(2)}) copy-start(bf16[8,7168]{1,0:T(8,128)(2,1)} %param.15) | copy-start | bytes 344068
  60.7 6.1 %collective-permute-start.8 = (bf16[32,3584]{1,0:T(8,128)(2,1)S(1)}, bf16[32,3584]{1,0:T(8,128)(2,1)S(1)}, u32[]{:S(2)}, u32[]{:S(2)}) collective-permute-start(bf16[32,3584]{1,0:T(8,128)(2,1)S(1)} %slice.164), channel_id=1, source_target_pairs={{0,2},{1,3},{2,0},{3,1},{4,6},{5,7},{6,4},{7,5},{8,10},{9,11},{10,... | collective-permute-start | bytes 688136 | tf_op jit(solution)/shard_map/ppermute | solution.py:230
  66.9 7.2 %collective-permute-start.10 = (bf16[8,7168]{1,0:T(8,128)(2,1)S(1)}, bf16[8,7168]{1,0:T(8,128)(2,1)S(1)}, u32[]{:S(2)}, u32[]{:S(2)}) collective-permute-start(bf16[8,7168]{1,0:T(8,128)(2,1)S(1)} %get-tuple-element.46), channel_id=1, source_target_pairs={{0,16},{1,17},{2,18},{3,19},{4,20},{5,21},{6,22},{7,23},{8,24},{9,... | collective-permute-start | bytes 344072 | tf_op jit(solution)/shard_map/ppermute | solution.py:230
  70.5 6.9 %collective-permute-start.11 = (bf16[8,7168]{1,0:T(8,128)(2,1)S(1)}, bf16[8,7168]{1,0:T(8,128)(2,1)S(1)}, u32[]{:S(2)}, u32[]{:S(2)}) collective-permute-start(bf16[8,7168]{1,0:T(8,128)(2,1)S(1)} %get-tuple-element.45), channel_id=1, source_target_pairs={{0,24},{1,25},{2,26},{3,27},{4,28},{5,29},{6,30},{7,31},{8,16},{9,... | collective-permute-start | bytes 344072 | tf_op jit(solution)/shard_map/ppermute | solution.py:230
  72.6 7.5 %collective-permute-start.9 = (bf16[8,7168]{1,0:T(8,128)(2,1)S(1)}, bf16[8,7168]{1,0:T(8,128)(2,1)S(1)}, u32[]{:S(2)}, u32[]{:S(2)}) collective-permute-start(bf16[8,7168]{1,0:T(8,128)(2,1)S(1)} %get-tuple-element.44), channel_id=1, source_target_pairs={{0,8},{1,9},{2,10},{3,11},{4,12},{5,13},{6,14},{7,15},{8,0},{9,1},... | collective-permute-start | bytes 344072 | tf_op jit(solution)/shard_map/ppermute | solution.py:230
  80.4 6.1 %collective-permute-start.12 = (bf16[8,7296]{1,0:T(8,128)(2,1)S(1)}, bf16[8,7296]{1,0:T(8,128)(2,1)S(1)}, u32[]{:S(2)}, u32[]{:S(2)}) collective-permute-start(bf16[8,7296]{1,0:T(8,128)(2,1)S(1)} %pad_maximum_fusion.10), channel_id=1, source_target_pairs={{0,8},{1,9},{2,10},{3,11},{4,12},{5,13},{6,14},{7,15},{8,0},{9,1},... | collective-permute-start | bytes 350216 | tf_op jit(solution)/shard_map/ppermute | solution.py:230
  80.5 6.1 %collective-permute-start.13 = (bf16[8,7296]{1,0:T(8,128)(2,1)S(1)}, bf16[8,7296]{1,0:T(8,128)(2,1)S(1)}, u32[]{:S(2)}, u32[]{:S(2)}) collective-permute-start(bf16[8,7296]{1,0:T(8,128)(2,1)S(1)} %pad_maximum_fusion.10), channel_id=1, source_target_pairs={{0,16},{1,17},{2,18},{3,19},{4,20},{5,21},{6,22},{7,23},{8,24},{9,... | collective-permute-start | bytes 350216 | tf_op jit(solution)/shard_map/ppermute | solution.py:230
  83.5 6.6 %collective-permute-start.14 = (bf16[8,7296]{1,0:T(8,128)(2,1)S(1)}, bf16[8,7296]{1,0:T(8,128)(2,1)S(1)}, u32[]{:S(2)}, u32[]{:S(2)}) collective-permute-start(bf16[8,7296]{1,0:T(8,128)(2,1)S(1)} %pad_maximum_fusion.10), channel_id=1, source_target_pairs={{0,24},{1,25},{2,26},{3,27},{4,28},{5,29},{6,30},{7,31},{8,16},{9,... | collective-permute-start | bytes 350216 | tf_op jit(solution)/shard_map/ppermute | solution.py:230
  90.1 7.6 %collective-permute-start.17 = (bf16[32,3712]{1,0:T(8,128)(2,1)S(1)}, bf16[32,3712]{1,0:T(8,128)(2,1)S(1)}, u32[]{:S(2)}, u32[]{:S(2)}) collective-permute-start(bf16[32,3712]{1,0:T(8,128)(2,1)S(1)} %pad_maximum_fusion.5), channel_id=1, source_target_pairs={{0,2},{1,3},{2,0},{3,1},{4,6},{5,7},{6,4},{7,5},{8,10},{9,11},{10,... | collective-permute-start | bytes 712712 | tf_op jit(solution)/shard_map/ppermute | solution.py:230
  90.9 8.5 %collective-permute-start.15 = (bf16[32,3584]{1,0:T(8,128)(2,1)S(1)}, bf16[32,3584]{1,0:T(8,128)(2,1)S(1)}, u32[]{:S(2)}, u32[]{:S(2)}) collective-permute-start(bf16[32,3584]{1,0:T(8,128)(2,1)S(1)} %pad_maximum_fusion.9), channel_id=1, source_target_pairs={{0,4},{1,5},{2,6},{3,7},{4,0},{5,1},{6,2},{7,3},{8,12},{9,13},{10,... | collective-permute-start | bytes 688136 | tf_op jit(solution)/shard_map/ppermute | solution.py:230
  97.8 14.1 %collective-permute-start.18 = (bf16[64,3712]{1,0:T(8,128)(2,1)S(1)}, bf16[64,3712]{1,0:T(8,128)(2,1)S(1)}, u32[]{:S(2)}, u32[]{:S(2)}) collective-permute-start(bf16[64,3712]{1,0:T(8,128)(2,1)S(1)} %pad_maximum_fusion.3.near_b), channel_id=1, source_target_pairs={{0,4},{1,5},{2,6},{3,7},{4,0},{5,1},{6,2},{7,3},{8,12},{9,13},{10,... | collective-permute-start | bytes 1425416 | tf_op jit(solution)/shard_map/ppermute | solution.py:230
  99.4 12.4 %collective-permute-start.16 = (bf16[64,3584]{1,0:T(8,128)(2,1)S(1)}, bf16[64,3584]{1,0:T(8,128)(2,1)S(1)}, u32[]{:S(2)}, u32[]{:S(2)}) collective-permute-start(bf16[64,3584]{1,0:T(8,128)(2,1)S(1)} %pad_maximum_fusion.4.near_a), channel_id=1, source_target_pairs={{0,2},{1,3},{2,0},{3,1},{4,6},{5,7},{6,4},{7,5},{8,10},{9,11},{10,... | collective-permute-start | bytes 1376264 | tf_op jit(solution)/shard_map/ppermute | solution.py:230
  114.2 8.9 %collective-permute-start.21 = (bf16[64,3584]{1,0:T(8,128)(2,1)S(1)}, bf16[64,3584]{1,0:T(8,128)(2,1)S(1)}, u32[]{:S(2)}, u32[]{:S(2)}) collective-permute-start(bf16[64,3584]{1,0:T(8,128)(2,1)S(1)} %get-tuple-element.36), channel_id=1, source_target_pairs={{0,4},{1,5},{2,6},{3,7},{4,0},{5,1},{6,2},{7,3},{8,12},{9,13},{10,... | collective-permute-start | bytes 1376264 | tf_op jit(solution)/shard_map/ppermute | solution.py:230
  114.9 9.6 %collective-permute-start.19 = (bf16[64,3584]{1,0:T(8,128)(2,1)S(1)}, bf16[64,3584]{1,0:T(8,128)(2,1)S(1)}, u32[]{:S(2)}, u32[]{:S(2)}) collective-permute-start(bf16[64,3584]{1,0:T(8,128)(2,1)S(1)} %get-tuple-element.34), channel_id=1, source_target_pairs={{0,2},{1,3},{2,0},{3,1},{4,6},{5,7},{6,4},{7,5},{8,10},{9,11},{10,... | collective-permute-start | bytes 1376264 | tf_op jit(solution)/shard_map/ppermute | solution.py:230
  123.2 6.1 %collective-permute-start.22 = (bf16[32,3584]{1,0:T(8,128)(2,1)S(1)}, bf16[32,3584]{1,0:T(8,128)(2,1)S(1)}, u32[]{:S(2)}, u32[]{:S(2)}) collective-permute-start(bf16[32,3584]{1,0:T(8,128)(2,1)S(1)} %slice.162), channel_id=1, source_target_pairs={{0,2},{1,3},{2,0},{3,1},{4,6},{5,7},{6,4},{7,5},{8,10},{9,11},{10,... | collective-permute-start | bytes 688136 | tf_op jit(solution)/shard_map/ppermute | solution.py:230
  124.6 6.1 %collective-permute-start.20 = (bf16[32,3584]{1,0:T(8,128)(2,1)S(1)}, bf16[32,3584]{1,0:T(8,128)(2,1)S(1)}, u32[]{:S(2)}, u32[]{:S(2)}) collective-permute-start(bf16[32,3584]{1,0:T(8,128)(2,1)S(1)} %slice.163), channel_id=1, source_target_pairs={{0,4},{1,5},{2,6},{3,7},{4,0},{5,1},{6,2},{7,3},{8,12},{9,13},{10,... | collective-permute-start | bytes 688136 | tf_op jit(solution)/shard_map/ppermute | solution.py:230
  130.7 9.7 %copy-start.1 = (bf16[8,128,576]{1,2,0:T(8,128)(2,1)S(1)}, bf16[8,128,576]{1,2,0:T(8,128)(2,1)}, u32[]{:S(2)}) copy-start(bf16[8,128,576]{1,2,0:T(8,128)(2,1)} %param.16) | copy-start | bytes 3538948
  130.8 6.1 %collective-permute-start.23 = (bf16[8,7168]{1,0:T(8,128)(2,1)S(1)}, bf16[8,7168]{1,0:T(8,128)(2,1)S(1)}, u32[]{:S(2)}, u32[]{:S(2)}) collective-permute-start(bf16[8,7168]{1,0:T(8,128)(2,1)S(1)} %get-tuple-element.41), channel_id=1, source_target_pairs={{0,8},{1,9},{2,10},{3,11},{4,12},{5,13},{6,14},{7,15},{8,0},{9,1},... | collective-permute-start | bytes 344072 | tf_op jit(solution)/shard_map/ppermute | solution.py:230
  130.9 6.0 %collective-permute-start.24 = (bf16[8,7168]{1,0:T(8,128)(2,1)S(1)}, bf16[8,7168]{1,0:T(8,128)(2,1)S(1)}, u32[]{:S(2)}, u32[]{:S(2)}) collective-permute-start(bf16[8,7168]{1,0:T(8,128)(2,1)S(1)} %get-tuple-element.43), channel_id=1, source_target_pairs={{0,16},{1,17},{2,18},{3,19},{4,20},{5,21},{6,22},{7,23},{8,24},{9,... | collective-permute-start | bytes 344072 | tf_op jit(solution)/shard_map/ppermute | solution.py:230
  133.0 6.6 %collective-permute-start.25 = (bf16[8,7168]{1,0:T(8,128)(2,1)S(1)}, bf16[8,7168]{1,0:T(8,128)(2,1)S(1)}, u32[]{:S(2)}, u32[]{:S(2)}) collective-permute-start(bf16[8,7168]{1,0:T(8,128)(2,1)S(1)} %get-tuple-element.42), channel_id=1, source_target_pairs={{0,24},{1,25},{2,26},{3,27},{4,28},{5,29},{6,30},{7,31},{8,16},{9,... | collective-permute-start | bytes 344072 | tf_op jit(solution)/shard_map/ppermute | solution.py:230

commit v5 on v4

--- a/solution.py
+++ b/solution.py
@@ -237,12 +237,13 @@
             outs.append(x[:half] + swap(x[half:].astype(BF16), axes[g][1]).astype(F32))
         x = jnp.concatenate(outs, axis=1)
         total = x[:rows]
-        for d in range(1, planes):
+        for d in reversed(range(1, planes)):
             total = total + swap(x[d * rows : (d + 1) * rows].astype(BF16), d * SLABS).astype(F32)
         return total
 
     def to_all(x, cut):
-        x = jnp.concatenate([x] + [swap(x, d * SLABS) for d in range(1, planes)], axis=0)
+        far = [swap(x, d * SLABS) for d in reversed(range(1, planes))]
+        x = jnp.concatenate([x] + far[::-1], axis=0)
         near = [
             jnp.concatenate([part, swap(part, axes[g][1])], axis=0)
             for g, part in enumerate((x[:, :cut], x[:, cut:]))

time: 141 us -> 141 us (level)
  transfers between devices with their start and end apart: 27 -> 27, of which waited for: 17 -> 16; matrix products, arithmetic and copies ran while one was open for 7% -> 7% of each run, Pallas kernels for 5% -> 5%
where the time goes in v5:
time: 141 us; the launch traced here: 140 us
  waiting for transfers between devices  71.5 us (51%)
  starting transfers between devices  42 us (30%)
  Pallas kernels  14.7 us (10%)
  other arithmetic  4.77 us (3%)
  matrix products  3.95 us (3%)
  local copies, waits for them, and re-layouts  2.92 us (2%)
    ppermute x26, waiting for transfers between devices, swap(): return lax.ppermute(x, 'ep', [(i, i ^ mask) for i in range(devices)])  52.6 us
    ppermute x26, starting transfers between devices, swap(): return lax.ppermute(x, 'ep', [(i, i ^ mask) for i in range(devices)])  33.7 us
    all_to_all x1, waiting for transfers between devices, body(): lax.all_to_all(latent_out, 'ep', split_axis=1, concat_axis=0, tiled=True,...  18.9 us
    all_to_all x1, starting transfers between devices, body(): lax.all_to_all(latent_out, 'ep', split_axis=1, concat_axis=0, tiled=True,...  8.31 us
    pallas_call x2, Pallas kernels, stage(): pl.pallas_call(body, out_shape=tuple((pltpu.VMEM(shape, BF16) for shape i...  6.45 us
    pallas_call x1, Pallas kernels, project_stream(): pl.pallas_call(stream_body, out_shape=projected(rows, width // groups) *...  5.95 us
  transfers between devices with their start and end apart: 27, of which 16 were waited for; matrix products, arithmetic and copies ran while one was open for 7% of the time, Pallas kernels for 5%

profile of v5, /device:TPU:0, one launch (start us, length us, event | category | flops | bytes accessed | tf_op | source)
XLA Modules:
  0.0 140.3 jit_solution(3796285841873310376)
XLA Ops:
  0.5 0.8 copy-done
  1.3 2.3 %convolution_multiply_fusion = f32[8,128,256]{2,1,0:T(8,128)S(1)} fusion(bf16[8,128,576]{1,2,0:T(8,128)(2,1)S(1)} %copy-done, bf16[8,256,576]{1,2,0:T(8,128)(2,1)} %param.17), kind=kOutput, calls=%fused_computation.4 | convolution fusion | flops 302252032 | bytes 4587520 | tf_op jit(solution)/shard_map/bhr,bpr->bhp/dot_general | solution.py:23
  3.6 2.2 %fusion.51 = (f32[8,128]{1,0:T(8,128)S(1)}, f32[8,128,256]{2,1,0:T(8,128)S(1)}) fusion(f32[8,128,256]{2,1,0:T(8,128)S(1)} %convolution_multiply_fusion, s32[8]{0:T(128)S(1)} %copy-done.11), kind=kOutput, calls=%fused_computation.109 | output fusion | flops 1573119 | bytes 2101280 | tf_op jit(solution)/shard_map/sub | solution.py:26
  5.9 0.8 fusion.3
  6.7 1.5 %copy.33 = bf16[8,128,512]{2,0,1:T(8,128)(2,1)} copy(bf16[8,128,512]{2,1,0:T(8,128)(2,1)S(1)} %fusion.3) | data formatting | bytes 2097152 | tf_op jit(solution)/shard_map/convert_element_type | solution.py:30
  8.3 8.3 %all-to-all-start = ((bf16[8,128,512]{2,0,1:T(8,128)(2,1)}), bf16[8,128,512]{2,0,1:T(8,128)(2,1)S(1)}, u32[]{:S(2)}, u32[]{:S(2)}) async-start(bf16[8,128,512]{2,0,1:T(8,128)(2,1)} %copy.33), calls=%async_computation | async-start | bytes 2097152 | tf_op jit(solution)/shard_map/all_to_all | solution.py:266
  16.7 0.5 collective-permute-start.2
  18.2 3.7 %collective-permute-done = bf16[4,512,128]{2,1,0:T(8,128)(2,1)S(1)} collective-permute-done((bf16[4,512,128]{2,1,0:T(8,128)(2,1)S(1)}, bf16[4,512,128]{2,1,0:T(8,128)(2,1)S(1)}, u32[]{:S(2)}, u32[]{:S(2)}) %collective-permute-start) | collective-permute-done | bytes 524320 | tf_op jit(solution)/shard_map/ppermute | solution.py:230
  22.1 18.9 %all-to-all-done = bf16[8,128,512]{2,0,1:T(8,128)(2,1)S(1)} async-done(((bf16[8,128,512]{2,0,1:T(8,128)(2,1)}), bf16[8,128,512]{2,0,1:T(8,128)(2,1)S(1)}, u32[]{:S(2)}, u32[]{:S(2)}) %all-to-all-start) | async-done | bytes 1048608 | tf_op jit(solution)/shard_map/all_to_all | solution.py:266
  41.2 0.5 convolution_convert_fusion.1
  42.1 6.0 %shard_map.145 = (bf16[64,3584]{1,0:T(8,128)(2,1)S(1)}, f32[64,3584]{1,0:T(8,128)S(1)}, bf16[64,3584]{1,0:T(8,128)(2,1)S(1)}, f32[64,3584]{1,0:T(8,128)S(1)}) custom-call(bf16[2,128,1024]{2,1,0:T(8,128)(2,1)S(1)} %bitcast.19, bf16[512,7168]{1,0:T(8,128)(2,1)} %own.1, bf16[512,7168]{1,0:T(8,128)(2,1)} %collective-permute-done.4.other), custom_call_target="tpu_custom_call" | custom-call | flops 1879048192 | bytes 14680064 | tf_op jit(solution)/shard_map/pallas_call | solution.py:137
  48.0 0.6 collective-permute-start.5
  48.9 2.0 %collective-permute-start.7 = (bf16[64,3584]{1,0:T(8,128)(2,1)S(1)}, bf16[64,3584]{1,0:T(8,128)(2,1)S(1)}, u32[]{:S(2)}, u32[]{:S(2)}) collective-permute-start(bf16[64,3584]{1,0:T(8,128)(2,1)S(1)} %get-tuple-element.26), channel_id=1, source_target_pairs={{0,4},{1,5},{2,6},{3,7},{4,0},{5,1},{6,2},{7,3},{8,12},{9,13},{10,... | collective-permute-start | bytes 1376264 | tf_op jit(solution)/shard_map/ppermute | solution.py:230
  50.8 7.0 %collective-permute-done.5 = bf16[64,3584]{1,0:T(8,128)(2,1)S(1)} collective-permute-done((bf16[64,3584]{1,0:T(8,128)(2,1)S(1)}, bf16[64,3584]{1,0:T(8,128)(2,1)S(1)}, u32[]{:S(2)}, u32[]{:S(2)}) %collective-permute-start.5) | collective-permute-done | bytes 458784 | tf_op jit(solution)/shard_map/ppermute | solution.py:230
  57.9 2.6 %collective-permute-start.6 = (bf16[32,3584]{1,0:T(8,128)(2,1)S(1)}, bf16[32,3584]{1,0:T(8,128)(2,1)S(1)}, u32[]{:S(2)}, u32[]{:S(2)}) collective-permute-start(bf16[32,3584]{1,0:T(8,128)(2,1)S(1)} %slice.165), channel_id=1, source_target_pairs={{0,4},{1,5},{2,6},{3,7},{4,0},{5,1},{6,2},{7,3},{8,12},{9,13},{10,... | collective-permute-start | bytes 688136 | tf_op jit(solution)/shard_map/ppermute | solution.py:230
  60.7 1.7 %collective-permute-start.8 = (bf16[32,3584]{1,0:T(8,128)(2,1)S(1)}, bf16[32,3584]{1,0:T(8,128)(2,1)S(1)}, u32[]{:S(2)}, u32[]{:S(2)}) collective-permute-start(bf16[32,3584]{1,0:T(8,128)(2,1)S(1)} %slice.164), channel_id=1, source_target_pairs={{0,2},{1,3},{2,0},{3,1},{4,6},{5,7},{6,4},{7,5},{8,10},{9,11},{10,... | collective-permute-start | bytes 688136 | tf_op jit(solution)/shard_map/ppermute | solution.py:230
  62.4 2.2 %collective-permute-done.6 = bf16[32,3584]{1,0:T(8,128)(2,1)S(1)} collective-permute-done((bf16[32,3584]{1,0:T(8,128)(2,1)S(1)}, bf16[32,3584]{1,0:T(8,128)(2,1)S(1)}, u32[]{:S(2)}, u32[]{:S(2)}) %collective-permute-start.6) | collective-permute-done | bytes 229408 | tf_op jit(solution)/shard_map/ppermute | solution.py:230
  64.6 2.2 %collective-permute-done.8 = bf16[32,3584]{1,0:T(8,128)(2,1)S(1)} collective-permute-done((bf16[32,3584]{1,0:T(8,128)(2,1)S(1)}, bf16[32,3584]{1,0:T(8,128)(2,1)S(1)}, u32[]{:S(2)}, u32[]{:S(2)}) %collective-permute-start.8) | collective-permute-done | bytes 229408 | tf_op jit(solution)/shard_map/ppermute | solution.py:230
  66.9 3.6 %collective-permute-start.10 = (bf16[8,7168]{1,0:T(8,128)(2,1)S(1)}, bf16[8,7168]{1,0:T(8,128)(2,1)S(1)}, u32[]{:S(2)}, u32[]{:S(2)}) collective-permute-start(bf16[8,7168]{1,0:T(8,128)(2,1)S(1)} %get-tuple-element.46), channel_id=1, source_target_pairs={{0,16},{1,17},{2,18},{3,19},{4,20},{5,21},{6,22},{7,23},{8,24},{9,... | collective-permute-start | bytes 344072 | tf_op jit(solution)/shard_map/ppermute | solution.py:230
  70.5 0.6 collective-permute-start.11
  71.1 1.5 %collective-permute-start.9 = (bf16[8,7168]{1,0:T(8,128)(2,1)S(1)}, bf16[8,7168]{1,0:T(8,128)(2,1)S(1)}, u32[]{:S(2)}, u32[]{:S(2)}) collective-permute-start(bf16[8,7168]{1,0:T(8,128)(2,1)S(1)} %get-tuple-element.44), channel_id=1, source_target_pairs={{0,24},{1,25},{2,26},{3,27},{4,28},{5,29},{6,30},{7,31},{8,16},{9,... | collective-permute-start | bytes 344072 | tf_op jit(solution)/shard_map/ppermute | solution.py:230
  72.7 3.3 %collective-permute-done.10 = bf16[8,7168]{1,0:T(8,128)(2,1)S(1)} collective-permute-done((bf16[8,7168]{1,0:T(8,128)(2,1)S(1)}, bf16[8,7168]{1,0:T(8,128)(2,1)S(1)}, u32[]{:S(2)}, u32[]{:S(2)}) %collective-permute-start.10) | collective-permute-done | bytes 114720 | tf_op jit(solution)/shard_map/ppermute | solution.py:230
  76.0 3.1 %collective-permute-done.9 = bf16[8,7168]{1,0:T(8,128)(2,1)S(1)} collective-permute-done((bf16[8,7168]{1,0:T(8,128)(2,1)S(1)}, bf16[8,7168]{1,0:T(8,128)(2,1)S(1)}, u32[]{:S(2)}, u32[]{:S(2)}) %collective-permute-start.9) | collective-permute-done | bytes 114720 | tf_op jit(solution)/shard_map/ppermute | solution.py:230
  79.4 1.6 %collective-permute-start.13 = (bf16[8,7296]{1,0:T(8,128)(2,1)S(1)}, bf16[8,7296]{1,0:T(8,128)(2,1)S(1)}, u32[]{:S(2)}, u32[]{:S(2)}) collective-permute-start(bf16[8,7296]{1,0:T(8,128)(2,1)S(1)} %pad_maximum_fusion.10), channel_id=1, source_target_pairs={{0,16},{1,17},{2,18},{3,19},{4,20},{5,21},{6,22},{7,23},{8,24},{9,... | collective-permute-start | bytes 350216 | tf_op jit(solution)/shard_map/ppermute | solution.py:230
  81.1 2.7 %collective-permute-start.14 = (bf16[8,7296]{1,0:T(8,128)(2,1)S(1)}, bf16[8,7296]{1,0:T(8,128)(2,1)S(1)}, u32[]{:S(2)}, u32[]{:S(2)}) collective-permute-start(bf16[8,7296]{1,0:T(8,128)(2,1)S(1)} %pad_maximum_fusion.10), channel_id=1, source_target_pairs={{0,24},{1,25},{2,26},{3,27},{4,28},{5,29},{6,30},{7,31},{8,16},{9,... | collective-permute-start | bytes 350216 | tf_op jit(solution)/shard_map/ppermute | solution.py:230
  83.8 1.7 %collective-permute-done.12 = bf16[8,7296]{1,0:T(8,128)(2,1)S(1)} collective-permute-done((bf16[8,7296]{1,0:T(8,128)(2,1)S(1)}, bf16[8,7296]{1,0:T(8,128)(2,1)S(1)}, u32[]{:S(2)}, u32[]{:S(2)}) %collective-permute-start.12) | collective-permute-done | bytes 116768 | tf_op jit(solution)/shard_map/ppermute | solution.py:230
  85.5 2.5 %collective-permute-done.14 = bf16[8,7296]{1,0:T(8,128)(2,1)S(1)} collective-permute-done((bf16[8,7296]{1,0:T(8,128)(2,1)S(1)}, bf16[8,7296]{1,0:T(8,128)(2,1)S(1)}, u32[]{:S(2)}, u32[]{:S(2)}) %collective-permute-start.14) | collective-permute-done | bytes 116768 | tf_op jit(solution)/shard_map/ppermute | solution.py:230
  88.0 1.3 collective-permute-start.17
  89.3 1.9 %collective-permute-start.15 = (bf16[32,3584]{1,0:T(8,128)(2,1)S(1)}, bf16[32,3584]{1,0:T(8,128)(2,1)S(1)}, u32[]{:S(2)}, u32[]{:S(2)}) collective-permute-start(bf16[32,3584]{1,0:T(8,128)(2,1)S(1)} %pad_maximum_fusion.9), channel_id=1, source_target_pairs={{0,4},{1,5},{2,6},{3,7},{4,0},{5,1},{6,2},{7,3},{8,12},{9,13},{10,... | collective-permute-start | bytes 688136 | tf_op jit(solution)/shard_map/ppermute | solution.py:230
  91.2 5.5 %collective-permute-done.17 = bf16[32,3712]{1,0:T(8,128)(2,1)S(1)} collective-permute-done((bf16[32,3712]{1,0:T(8,128)(2,1)S(1)}, bf16[32,3712]{1,0:T(8,128)(2,1)S(1)}, u32[]{:S(2)}, u32[]{:S(2)}) %collective-permute-start.17) | collective-permute-done | bytes 237600 | tf_op jit(solution)/shard_map/ppermute | solution.py:230
  96.8 1.1 collective-permute-start.18
  97.9 2.0 %collective-permute-start.16 = (bf16[64,3584]{1,0:T(8,128)(2,1)S(1)}, bf16[64,3584]{1,0:T(8,128)(2,1)S(1)}, u32[]{:S(2)}, u32[]{:S(2)}) collective-permute-start(bf16[64,3584]{1,0:T(8,128)(2,1)S(1)} %pad_maximum_fusion.4.near_a), channel_id=1, source_target_pairs={{0,2},{1,3},{2,0},{3,1},{4,6},{5,7},{6,4},{7,5},{8,10},{9,11},{10,... | collective-permute-start | bytes 1376264 | tf_op jit(solution)/shard_map/ppermute | solution.py:230
  100.0 2.6 %shard_map.147 = (bf16[256,3584]{1,0:T(8,128)(2,1)S(1)}, bf16[256,3584]{1,0:T(8,128)(2,1)S(1)}, f32[8,128]{1,0:T(8,128)}) custom-call(bf16[128,7168]{1,0:T(8,128)(2,1)} %refs_0_.3, bf16[128,7168]{1,0:T(8,128)(2,1)} %collective-permute-done.3.refs_1_, bf16[8,7168]{1,0:T(8,128)(2,1)S(1)} %multiply_convert_fusion.refs_4_.refs_2_), custom_call_target="tpu_custom_call" | custom-call | bytes 7340032 | tf_op jit(solution)/shard_map/pallas_call | solution.py:58
  102.6 3.8 %shard_map.146 = (bf16[7168,512]{1,0:T(8,128)(2,1)S(1)}, f32[8,128]{1,0:T(8,128)}) custom-call(bf16[7168,128]{1,0:T(8,128)(2,1)} %refs_0_.2, bf16[7168,128]{1,0:T(8,128)(2,1)} %collective-permute-done.1.refs_1_, bf16[7168,128]{1,0:T(8,128)(2,1)} %refs_2_.1, bf16[7168,128]{1,0:T(8,128)(2,1)} %collective-permute-done.2.refs_3_, ...), custom_call_target="tpu_custom_call" | custom-call | bytes 14680064 | tf_op jit(solution)/shard_map/pallas_call | solution.py:58
  106.4 3.5 %collective-permute-done.16.far_a = bf16[64,3584]{1,0:T(8,128)(2,1)S(1)} collective-permute-done((bf16[64,3584]{1,0:T(8,128)(2,1)S(1)}, bf16[64,3584]{1,0:T(8,128)(2,1)S(1)}, u32[]{:S(2)}, u32[]{:S(2)}) %collective-permute-start.16) | collective-permute-done | bytes 458784 | tf_op jit(solution)/shard_map/ppermute | solution.py:230
  110.0 2.3 %shard_map.148 = (bf16[64,3584]{1,0:T(8,128)(2,1)S(1)}, f32[64,3584]{1,0:T(8,128)S(1)}, bf16[64,3584]{1,0:T(8,128)(2,1)S(1)}, f32[64,3584]{1,0:T(8,128)S(1)}) custom-call(s32[2]{0:T(128)S(1)} %pad_add_fusion.label, bf16[64,3584]{1,0:T(8,128)(2,1)S(1)} %pad_maximum_fusion.4.near_a, bf16[64,3584]{1,0:T(8,128)(2,1)S(1)} %collective-permute-done.16.far_a, ...), custom_call_target="tpu_custom_call" | custom-call | flops 1409286144 | bytes 5505024 | tf_op jit(solution)/shard_map/pallas_call | solution.py:197
  112.3 0.5 collective-permute-start.21
  112.8 2.1 %collective-permute-start.19 = (bf16[64,3584]{1,0:T(8,128)(2,1)S(1)}, bf16[64,3584]{1,0:T(8,128)(2,1)S(1)}, u32[]{:S(2)}, u32[]{:S(2)}) collective-permute-start(bf16[64,3584]{1,0:T(8,128)(2,1)S(1)} %get-tuple-element.34), channel_id=1, source_target_pairs={{0,2},{1,3},{2,0},{3,1},{4,6},{5,7},{6,4},{7,5},{8,10},{9,11},{10,... | collective-permute-start | bytes 1376264 | tf_op jit(solution)/shard_map/ppermute | solution.py:230
  114.9 6.9 %collective-permute-done.21 = bf16[64,3584]{1,0:T(8,128)(2,1)S(1)} collective-permute-done((bf16[64,3584]{1,0:T(8,128)(2,1)S(1)}, bf16[64,3584]{1,0:T(8,128)(2,1)S(1)}, u32[]{:S(2)}, u32[]{:S(2)}) %collective-permute-start.21) | collective-permute-done | bytes 458784 | tf_op jit(solution)/shard_map/ppermute | solution.py:230
  122.0 1.5 %collective-permute-start.22 = (bf16[32,3584]{1,0:T(8,128)(2,1)S(1)}, bf16[32,3584]{1,0:T(8,128)(2,1)S(1)}, u32[]{:S(2)}, u32[]{:S(2)}) collective-permute-start(bf16[32,3584]{1,0:T(8,128)(2,1)S(1)} %slice.162), channel_id=1, source_target_pairs={{0,2},{1,3},{2,0},{3,1},{4,6},{5,7},{6,4},{7,5},{8,10},{9,11},{10,... | collective-permute-start | bytes 688136 | tf_op jit(solution)/shard_map/ppermute | solution.py:230
  124.0 4.1 %collective-permute-done.22 = bf16[32,3584]{1,0:T(8,128)(2,1)S(1)} collective-permute-done((bf16[32,3584]{1,0:T(8,128)(2,1)S(1)}, bf16[32,3584]{1,0:T(8,128)(2,1)S(1)}, u32[]{:S(2)}, u32[]{:S(2)}) %collective-permute-start.22) | collective-permute-done | bytes 229408 | tf_op jit(solution)/shard_map/ppermute | solution.py:230
  128.1 1.6 %collective-permute-done.20 = bf16[32,3584]{1,0:T(8,128)(2,1)S(1)} collective-permute-done((bf16[32,3584]{1,0:T(8,128)(2,1)S(1)}, bf16[32,3584]{1,0:T(8,128)(2,1)S(1)}, u32[]{:S(2)}, u32[]{:S(2)}) %collective-permute-start.20) | collective-permute-done | bytes 229408 | tf_op jit(solution)/shard_map/ppermute | solution.py:230
  129.8 2.5 %collective-permute-start.23 = (bf16[8,7168]{1,0:T(8,128)(2,1)S(1)}, bf16[8,7168]{1,0:T(8,128)(2,1)S(1)}, u32[]{:S(2)}, u32[]{:S(2)}) collective-permute-start(bf16[8,7168]{1,0:T(8,128)(2,1)S(1)} %get-tuple-element.41), channel_id=1, source_target_pairs={{0,24},{1,25},{2,26},{3,27},{4,28},{5,29},{6,30},{7,31},{8,16},{9,... | collective-permute-start | bytes 344072 | tf_op jit(solution)/shard_map/ppermute | solution.py:230
  132.3 0.8 collective-permute-start.24
  133.1 1.2 collective-permute-start.25
  134.3 2.3 %collective-permute-done.23 = bf16[8,7168]{1,0:T(8,128)(2,1)S(1)} collective-permute-done((bf16[8,7168]{1,0:T(8,128)(2,1)S(1)}, bf16[8,7168]{1,0:T(8,128)(2,1)S(1)}, u32[]{:S(2)}, u32[]{:S(2)}) %collective-permute-start.23) | collective-permute-done | bytes 114720 | tf_op jit(solution)/shard_map/ppermute | solution.py:230
  136.6 3.0 %collective-permute-done.24 = bf16[8,7168]{1,0:T(8,128)(2,1)S(1)} collective-permute-done((bf16[8,7168]{1,0:T(8,128)(2,1)S(1)}, bf16[8,7168]{1,0:T(8,128)(2,1)S(1)}, u32[]{:S(2)}, u32[]{:S(2)}) %collective-permute-start.24) | collective-permute-done | bytes 114720 | tf_op jit(solution)/shard_map/ppermute | solution.py:230
  139.6 0.7 fusion.27
  (83 shorter events, 4.2 us)
Async XLA Ops:
  0.0 1.3 copy-start
  0.0 3.6 %copy-start.11 = (s32[8]{0:T(128)S(1)}, s32[8]{0:T(128)}, u32[]{:S(2)}) copy-start(s32[8]{0:T(128)} %param.18) | copy-start | bytes 100
  0.0 42.0 %collective-permute-start.4 = (bf16[512,7168]{1,0:T(8,128)(2,1)}, bf16[512,7168]{1,0:T(8,128)(2,1)}, u32[]{:S(2)}, u32[]{:S(2)}) collective-permute-start(bf16[512,7168]{1,0:T(8,128)(2,1)} %own.1), channel_id=1, source_target_pairs={{0,1},{1,0},{2,3},{3,2},{4,5},{5,4},{6,7},{7,6},{8,9},{9,8},{10,11... | collective-permute-start | bytes 22020104 | tf_op jit(solution)/shard_map/ppermute | solution.py:230
  3.6 2.3 %copy-start.2 = (bf16[8,256,576]{1,2,0:T(8,128)(2,1)S(1)}, bf16[8,256,576]{1,2,0:T(8,128)(2,1)}, u32[]{:S(2)}) copy-start(bf16[8,256,576]{1,2,0:T(8,128)(2,1)} %param.17) | copy-start | bytes 7077892
  6.7 10.6 %copy-start.3 = (bf16[4,512,128]{2,1,0:T(8,128)(2,1)S(1)}, bf16[4,512,128]{2,1,0:T(8,128)(2,1)}, u32[]{:S(2)}) copy-start(bf16[4,512,128]{2,1,0:T(8,128)(2,1)} %param.19) | copy-start | bytes 1572868
  6.7 11.0 %copy-start.9 = (s32[16]{0:T(128)S(1)}, s32[16]{0:T(128)}, u32[]{:S(2)}) copy-start(s32[16]{0:T(128)} %constant.70.clone) | copy-start | bytes 196
  6.7 11.0 %copy-start.10 = (s32[16]{0:T(128)S(1)}, s32[16]{0:T(128)}, u32[]{:S(2)}) copy-start(s32[16]{0:T(128)} %constant.71.clone) | copy-start | bytes 196
  8.3 32.8 %all-to-all-start = ((bf16[8,128,512]{2,0,1:T(8,128)(2,1)}), bf16[8,128,512]{2,0,1:T(8,128)(2,1)S(1)}, u32[]{:S(2)}, u32[]{:S(2)}) async-start(bf16[8,128,512]{2,0,1:T(8,128)(2,1)} %copy.33), calls=%async_computation | async-start | bytes 2097152 | tf_op jit(solution)/shard_map/all_to_all | solution.py:266
  16.6 24.5 %collective-permute-start.1 = (bf16[7168,128]{1,0:T(8,128)(2,1)}, bf16[7168,128]{1,0:T(8,128)(2,1)}, u32[]{:S(2)}, u32[]{:S(2)}) collective-permute-start(bf16[7168,128]{1,0:T(8,128)(2,1)} %refs_0_.2), channel_id=1, source_target_pairs={{0,1},{1,0},{2,3},{3,2},{4,5},{5,4},{6,7},{7,6},{8,9},{9,8},{10,11... | collective-permute-start | bytes 5505032 | tf_op jit(solution)/shard_map/ppermute | solution.py:230
  16.7 24.5 %collective-permute-start.2 = (bf16[7168,128]{1,0:T(8,128)(2,1)}, bf16[7168,128]{1,0:T(8,128)(2,1)}, u32[]{:S(2)}, u32[]{:S(2)}) collective-permute-start(bf16[7168,128]{1,0:T(8,128)(2,1)} %refs_2_.1), channel_id=1, source_target_pairs={{0,1},{1,0},{2,3},{3,2},{4,5},{5,4},{6,7},{7,6},{8,9},{9,8},{10,11... | collective-permute-start | bytes 5505032 | tf_op jit(solution)/shard_map/ppermute | solution.py:230
  17.2 24.0 %collective-permute-start.3 = (bf16[128,7168]{1,0:T(8,128)(2,1)}, bf16[128,7168]{1,0:T(8,128)(2,1)}, u32[]{:S(2)}, u32[]{:S(2)}) collective-permute-start(bf16[128,7168]{1,0:T(8,128)(2,1)} %refs_0_.3), channel_id=1, source_target_pairs={{0,1},{1,0},{2,3},{3,2},{4,5},{5,4},{6,7},{7,6},{8,9},{9,8},{10,11... | collective-permute-start | bytes 5505032 | tf_op jit(solution)/shard_map/ppermute | solution.py:230
  17.3 4.7 %collective-permute-start = (bf16[4,512,128]{2,1,0:T(8,128)(2,1)S(1)}, bf16[4,512,128]{2,1,0:T(8,128)(2,1)S(1)}, u32[]{:S(2)}, u32[]{:S(2)}) collective-permute-start(bf16[4,512,128]{2,1,0:T(8,128)(2,1)S(1)} %copy-done.3), channel_id=1, source_target_pairs={{0,1},{1,0},{2,3},{3,2},{4,5},{5,4},{6,7},{7,6},{8,9},{9,8},{10,11... | collective-permute-start | bytes 1572872 | tf_op jit(solution)/shard_map/ppermute | solution.py:230
  42.0 6.6 %copy-start.6 = (s32[8,2]{0,1:T(2,128)S(1)}, s32[8,2]{0,1:T(2,128)}, u32[]{:S(2)}) copy-start(s32[8,2]{0,1:T(2,128)} %param.22) | copy-start | bytes 196
  42.1 6.6 %copy-start.8 = (s32[4]{0:T(128)S(1)}, s32[4]{0:T(128)}, u32[]{:S(2)}) copy-start(s32[4]{0:T(128)} %param.24) | copy-start | bytes 52
  42.1 6.7 %copy-start.7 = (f32[8,2]{0,1:T(2,128)S(1)}, f32[8,2]{0,1:T(2,128)}, u32[]{:S(2)}) copy-start(f32[8,2]{0,1:T(2,128)} %param.23) | copy-start | bytes 196
  48.0 9.8 %collective-permute-start.5 = (bf16[64,3584]{1,0:T(8,128)(2,1)S(1)}, bf16[64,3584]{1,0:T(8,128)(2,1)S(1)}, u32[]{:S(2)}, u32[]{:S(2)}) collective-permute-start(bf16[64,3584]{1,0:T(8,128)(2,1)S(1)} %get-tuple-element.24), channel_id=1, source_target_pairs={{0,2},{1,3},{2,0},{3,1},{4,6},{5,7},{6,4},{7,5},{8,10},{9,11},{10,... | collective-permute-start | bytes 1376264 | tf_op jit(solution)/shard_map/ppermute | solution.py:230
  48.9 11.7 %collective-permute-start.7 = (bf16[64,3584]{1,0:T(8,128)(2,1)S(1)}, bf16[64,3584]{1,0:T(8,128)(2,1)S(1)}, u32[]{:S(2)}, u32[]{:S(2)}) collective-permute-start(bf16[64,3584]{1,0:T(8,128)(2,1)S(1)} %get-tuple-element.26), channel_id=1, source_target_pairs={{0,4},{1,5},{2,6},{3,7},{4,0},{5,1},{6,2},{7,3},{8,12},{9,13},{10,... | collective-permute-start | bytes 1376264 | tf_op jit(solution)/shard_map/ppermute | solution.py:230
  57.9 6.6 %collective-permute-start.6 = (bf16[32,3584]{1,0:T(8,128)(2,1)S(1)}, bf16[32,3584]{1,0:T(8,128)(2,1)S(1)}, u32[]{:S(2)}, u32[]{:S(2)}) collective-permute-start(bf16[32,3584]{1,0:T(8,128)(2,1)S(1)} %slice.165), channel_id=1, source_target_pairs={{0,4},{1,5},{2,6},{3,7},{4,0},{5,1},{6,2},{7,3},{8,12},{9,13},{10,... | collective-permute-start | bytes 688136 | tf_op jit(solution)/shard_map/ppermute | solution.py:230
  60.6 11.9 %copy-start.5 = (bf16[7168]{0:T(1024)(128)(2,1)S(1)}, bf16[7168]{0:T(1024)(128)(2,1)}, u32[]{:S(2)}) copy-start(bf16[7168]{0:T(1024)(128)(2,1)} %param.21) | copy-start | bytes 43012
  60.7 18.4 %copy-start.4 = (bf16[8,7168]{1,0:T(8,128)(2,1)S(1)}, bf16[8,7168]{1,0:T(8,128)(2,1)}, u32[]{:S(2)}) copy-start(bf16[8,7168]{1,0:T(8,128)(2,1)} %param.15) | copy-start | bytes 344068
  60.7 6.1 %collective-permute-start.8 = (bf16[32,3584]{1,0:T(8,128)(2,1)S(1)}, bf16[32,3584]{1,0:T(8,128)(2,1)S(1)}, u32[]{:S(2)}, u32[]{:S(2)}) collective-permute-start(bf16[32,3584]{1,0:T(8,128)(2,1)S(1)} %slice.164), channel_id=1, source_target_pairs={{0,2},{1,3},{2,0},{3,1},{4,6},{5,7},{6,4},{7,5},{8,10},{9,11},{10,... | collective-permute-start | bytes 688136 | tf_op jit(solution)/shard_map/ppermute | solution.py:230
  66.9 9.1 %collective-permute-start.10 = (bf16[8,7168]{1,0:T(8,128)(2,1)S(1)}, bf16[8,7168]{1,0:T(8,128)(2,1)S(1)}, u32[]{:S(2)}, u32[]{:S(2)}) collective-permute-start(bf16[8,7168]{1,0:T(8,128)(2,1)S(1)} %get-tuple-element.46), channel_id=1, source_target_pairs={{0,16},{1,17},{2,18},{3,19},{4,20},{5,21},{6,22},{7,23},{8,24},{9,... | collective-permute-start | bytes 344072 | tf_op jit(solution)/shard_map/ppermute | solution.py:230
  70.5 5.5 %collective-permute-start.11 = (bf16[8,7168]{1,0:T(8,128)(2,1)S(1)}, bf16[8,7168]{1,0:T(8,128)(2,1)S(1)}, u32[]{:S(2)}, u32[]{:S(2)}) collective-permute-start(bf16[8,7168]{1,0:T(8,128)(2,1)S(1)} %get-tuple-element.45), channel_id=1, source_target_pairs={{0,8},{1,9},{2,10},{3,11},{4,12},{5,13},{6,14},{7,15},{8,0},{9,1},... | collective-permute-start | bytes 344072 | tf_op jit(solution)/shard_map/ppermute | solution.py:230
  71.1 8.0 %collective-permute-start.9 = (bf16[8,7168]{1,0:T(8,128)(2,1)S(1)}, bf16[8,7168]{1,0:T(8,128)(2,1)S(1)}, u32[]{:S(2)}, u32[]{:S(2)}) collective-permute-start(bf16[8,7168]{1,0:T(8,128)(2,1)S(1)} %get-tuple-element.44), channel_id=1, source_target_pairs={{0,24},{1,25},{2,26},{3,27},{4,28},{5,29},{6,30},{7,31},{8,16},{9,... | collective-permute-start | bytes 344072 | tf_op jit(solution)/shard_map/ppermute | solution.py:230
  79.4 6.1 %collective-permute-start.12 = (bf16[8,7296]{1,0:T(8,128)(2,1)S(1)}, bf16[8,7296]{1,0:T(8,128)(2,1)S(1)}, u32[]{:S(2)}, u32[]{:S(2)}) collective-permute-start(bf16[8,7296]{1,0:T(8,128)(2,1)S(1)} %pad_maximum_fusion.10), channel_id=1, source_target_pairs={{0,8},{1,9},{2,10},{3,11},{4,12},{5,13},{6,14},{7,15},{8,0},{9,1},... | collective-permute-start | bytes 350216 | tf_op jit(solution)/shard_map/ppermute | solution.py:230
  79.4 6.1 %collective-permute-start.13 = (bf16[8,7296]{1,0:T(8,128)(2,1)S(1)}, bf16[8,7296]{1,0:T(8,128)(2,1)S(1)}, u32[]{:S(2)}, u32[]{:S(2)}) collective-permute-start(bf16[8,7296]{1,0:T(8,128)(2,1)S(1)} %pad_maximum_fusion.10), channel_id=1, source_target_pairs={{0,16},{1,17},{2,18},{3,19},{4,20},{5,21},{6,22},{7,23},{8,24},{9,... | collective-permute-start | bytes 350216 | tf_op jit(solution)/shard_map/ppermute | solution.py:230
  81.1 6.9 %collective-permute-start.14 = (bf16[8,7296]{1,0:T(8,128)(2,1)S(1)}, bf16[8,7296]{1,0:T(8,128)(2,1)S(1)}, u32[]{:S(2)}, u32[]{:S(2)}) collective-permute-start(bf16[8,7296]{1,0:T(8,128)(2,1)S(1)} %pad_maximum_fusion.10), channel_id=1, source_target_pairs={{0,24},{1,25},{2,26},{3,27},{4,28},{5,29},{6,30},{7,31},{8,16},{9,... | collective-permute-start | bytes 350216 | tf_op jit(solution)/shard_map/ppermute | solution.py:230
  88.0 8.8 %collective-permute-start.17 = (bf16[32,3712]{1,0:T(8,128)(2,1)S(1)}, bf16[32,3712]{1,0:T(8,128)(2,1)S(1)}, u32[]{:S(2)}, u32[]{:S(2)}) collective-permute-start(bf16[32,3712]{1,0:T(8,128)(2,1)S(1)} %pad_maximum_fusion.5), channel_id=1, source_target_pairs={{0,2},{1,3},{2,0},{3,1},{4,6},{5,7},{6,4},{7,5},{8,10},{9,11},{10,... | collective-permute-start | bytes 712712 | tf_op jit(solution)/shard_map/ppermute | solution.py:230
  89.3 8.5 %collective-permute-start.15 = (bf16[32,3584]{1,0:T(8,128)(2,1)S(1)}, bf16[32,3584]{1,0:T(8,128)(2,1)S(1)}, u32[]{:S(2)}, u32[]{:S(2)}) collective-permute-start(bf16[32,3584]{1,0:T(8,128)(2,1)S(1)} %pad_maximum_fusion.9), channel_id=1, source_target_pairs={{0,4},{1,5},{2,6},{3,7},{4,0},{5,1},{6,2},{7,3},{8,12},{9,13},{10,... | collective-permute-start | bytes 688136 | tf_op jit(solution)/shard_map/ppermute | solution.py:230
  96.8 13.2 %collective-permute-start.18 = (bf16[64,3712]{1,0:T(8,128)(2,1)S(1)}, bf16[64,3712]{1,0:T(8,128)(2,1)S(1)}, u32[]{:S(2)}, u32[]{:S(2)}) collective-permute-start(bf16[64,3712]{1,0:T(8,128)(2,1)S(1)} %pad_maximum_fusion.3.near_b), channel_id=1, source_target_pairs={{0,4},{1,5},{2,6},{3,7},{4,0},{5,1},{6,2},{7,3},{8,12},{9,13},{10,... | collective-permute-start | bytes 1425416 | tf_op jit(solution)/shard_map/ppermute | solution.py:230
  97.9 12.1 %collective-permute-start.16 = (bf16[64,3584]{1,0:T(8,128)(2,1)S(1)}, bf16[64,3584]{1,0:T(8,128)(2,1)S(1)}, u32[]{:S(2)}, u32[]{:S(2)}) collective-permute-start(bf16[64,3584]{1,0:T(8,128)(2,1)S(1)} %pad_maximum_fusion.4.near_a), channel_id=1, source_target_pairs={{0,2},{1,3},{2,0},{3,1},{4,6},{5,7},{6,4},{7,5},{8,10},{9,11},{10,... | collective-permute-start | bytes 1376264 | tf_op jit(solution)/shard_map/ppermute | solution.py:230
  112.3 9.6 %collective-permute-start.21 = (bf16[64,3584]{1,0:T(8,128)(2,1)S(1)}, bf16[64,3584]{1,0:T(8,128)(2,1)S(1)}, u32[]{:S(2)}, u32[]{:S(2)}) collective-permute-start(bf16[64,3584]{1,0:T(8,128)(2,1)S(1)} %get-tuple-element.36), channel_id=1, source_target_pairs={{0,4},{1,5},{2,6},{3,7},{4,0},{5,1},{6,2},{7,3},{8,12},{9,13},{10,... | collective-permute-start | bytes 1376264 | tf_op jit(solution)/shard_map/ppermute | solution.py:230
  112.8 10.7 %collective-permute-start.19 = (bf16[64,3584]{1,0:T(8,128)(2,1)S(1)}, bf16[64,3584]{1,0:T(8,128)(2,1)S(1)}, u32[]{:S(2)}, u32[]{:S(2)}) collective-permute-start(bf16[64,3584]{1,0:T(8,128)(2,1)S(1)} %get-tuple-element.34), channel_id=1, source_target_pairs={{0,2},{1,3},{2,0},{3,1},{4,6},{5,7},{6,4},{7,5},{8,10},{9,11},{10,... | collective-permute-start | bytes 1376264 | tf_op jit(solution)/shard_map/ppermute | solution.py:230
  122.0 6.1 %collective-permute-start.22 = (bf16[32,3584]{1,0:T(8,128)(2,1)S(1)}, bf16[32,3584]{1,0:T(8,128)(2,1)S(1)}, u32[]{:S(2)}, u32[]{:S(2)}) collective-permute-start(bf16[32,3584]{1,0:T(8,128)(2,1)S(1)} %slice.162), channel_id=1, source_target_pairs={{0,2},{1,3},{2,0},{3,1},{4,6},{5,7},{6,4},{7,5},{8,10},{9,11},{10,... | collective-permute-start | bytes 688136 | tf_op jit(solution)/shard_map/ppermute | solution.py:230
  123.6 6.1 %collective-permute-start.20 = (bf16[32,3584]{1,0:T(8,128)(2,1)S(1)}, bf16[32,3584]{1,0:T(8,128)(2,1)S(1)}, u32[]{:S(2)}, u32[]{:S(2)}) collective-permute-start(bf16[32,3584]{1,0:T(8,128)(2,1)S(1)} %slice.163), channel_id=1, source_target_pairs={{0,4},{1,5},{2,6},{3,7},{4,0},{5,1},{6,2},{7,3},{8,12},{9,13},{10,... | collective-permute-start | bytes 688136 | tf_op jit(solution)/shard_map/ppermute | solution.py:230
  129.7 10.6 %copy-start.1 = (bf16[8,128,576]{1,2,0:T(8,128)(2,1)S(1)}, bf16[8,128,576]{1,2,0:T(8,128)(2,1)}, u32[]{:S(2)}) copy-start(bf16[8,128,576]{1,2,0:T(8,128)(2,1)} %param.16) | copy-start | bytes 3538948
  129.8 6.8 %collective-permute-start.23 = (bf16[8,7168]{1,0:T(8,128)(2,1)S(1)}, bf16[8,7168]{1,0:T(8,128)(2,1)S(1)}, u32[]{:S(2)}, u32[]{:S(2)}) collective-permute-start(bf16[8,7168]{1,0:T(8,128)(2,1)S(1)} %get-tuple-element.41), channel_id=1, source_target_pairs={{0,24},{1,25},{2,26},{3,27},{4,28},{5,29},{6,30},{7,31},{8,16},{9,... | collective-permute-start | bytes 344072 | tf_op jit(solution)/shard_map/ppermute | solution.py:230
  132.3 7.3 %collective-permute-start.24 = (bf16[8,7168]{1,0:T(8,128)(2,1)S(1)}, bf16[8,7168]{1,0:T(8,128)(2,1)S(1)}, u32[]{:S(2)}, u32[]{:S(2)}) collective-permute-start(bf16[8,7168]{1,0:T(8,128)(2,1)S(1)} %get-tuple-element.43), channel_id=1, source_target_pairs={{0,16},{1,17},{2,18},{3,19},{4,20},{5,21},{6,22},{7,23},{8,24},{9,... | collective-permute-start | bytes 344072 | tf_op jit(solution)/shard_map/ppermute | solution.py:230
  133.1 6.5 %collective-permute-start.25 = (bf16[8,7168]{1,0:T(8,128)(2,1)S(1)}, bf16[8,7168]{1,0:T(8,128)(2,1)S(1)}, u32[]{:S(2)}, u32[]{:S(2)}) collective-permute-start(bf16[8,7168]{1,0:T(8,128)(2,1)S(1)} %get-tuple-element.42), channel_id=1, source_target_pairs={{0,8},{1,9},{2,10},{3,11},{4,12},{5,13},{6,14},{7,15},{8,0},{9,1},... | collective-permute-start | bytes 344072 | tf_op jit(solution)/shard_map/ppermute | solution.py:230

commit v6 on v5

--- a/solution.py
+++ b/solution.py
@@ -209,10 +209,14 @@
     return outs[:2], outs[2:]
 
 
-def relative_order(first, second, planes):
+def plane_masks(block, planes):
+    return block, (planes - block) % planes
+
+
+def relative_order(first, second, planes, core):
     return np.array(
         [
-            z * SLABS + b * second + a * first
+            plane_masks(z, planes)[core] * SLABS + b * second + a * first
             for a in (0, 1)
             for b in (0, 1)
             for z in range(planes)
@@ -228,6 +232,10 @@
 
     def swap(x, mask):
         return lax.ppermute(x, "ep", [(i, i ^ mask) for i in range(devices)])
+
+    def swap_plane(x, block):
+        masks = plane_masks(block, planes)
+        return lax.ppermute(x, "ep", [(i, i ^ (masks[i % 2] * SLABS)) for i in range(devices)])
 
     def sum_to_owner(products, rows):
         outs = []
@@ -238,11 +246,11 @@
         x = jnp.concatenate(outs, axis=1)
         total = x[:rows]
         for d in reversed(range(1, planes)):
-            total = total + swap(x[d * rows : (d + 1) * rows].astype(BF16), d * SLABS).astype(F32)
+            total = total + swap_plane(x[d * rows : (d + 1) * rows].astype(BF16), d).astype(F32)
         return total
 
     def to_all(x, cut):
-        far = [swap(x, d * SLABS) for d in reversed(range(1, planes))]
+        far = [swap_plane(x, d) for d in reversed(range(1, planes))]
         x = jnp.concatenate([x] + far[::-1], axis=0)
         near = [
             jnp.concatenate([part, swap(part, axes[g][1])], axis=0)
@@ -280,7 +288,10 @@
             (by_heads, heads_up, w_gate_other, w_up_other, w_down_other)
         )
 
-        orders = [relative_order(first, second, planes) for first, second in axes]
+        orders = [
+            jnp.where(core == 0, *(jnp.asarray(relative_order(*pair, planes, c)) for c in (0, 1)))
+            for pair in axes
+        ]
         experts = expert_slot.shape[0]
         labels = jnp.arange(experts, dtype=jnp.int32)
         physical = jnp.sum(
@@ -310,7 +321,7 @@
         )
         picks = []
         for order in orders:
-            place = jnp.bitwise_xor(jnp.asarray(order), me) // 2
+            place = jnp.bitwise_xor(order, me) // 2
             wanted = (place[:, None] * rows + jnp.arange(rows, dtype=jnp.int32)).reshape(-1, 1)
             picks.append(wanted == jnp.arange(total_rows, dtype=jnp.int32)[None, :])
         picks = jnp.concatenate(picks, axis=0).astype(BF16)

time: 141 us -> 142 us (level)
  starting transfers between devices: 42 us -> 46.3 us
  waiting for transfers between devices: 71.5 us -> 68.6 us
    ppermute x26 -> x17, waiting for transfers between devices: 52.6 us -> 33.7 us  [swap(): return lax.ppermute(x, 'ep', [(i, i ^ mask) for i in range(devices)])]
    ppermute x0 -> x9, waiting for transfers between devices: none -> 16 us  [swap_plane(): lax.ppermute(x, 'ep', [(i, i ^ masks[i % 2] * SLABS) for i in range(devic...]
    ppermute x0 -> x9, starting transfers between devices: none -> 14.6 us  [swap_plane(): lax.ppermute(x, 'ep', [(i, i ^ masks[i % 2] * SLABS) for i in range(devic...]
    ppermute x26 -> x17, starting transfers between devices: 33.7 us -> 23.4 us  [swap(): return lax.ppermute(x, 'ep', [(i, i ^ mask) for i in range(devices)])]
  transfers between devices with their start and end apart: 27 -> 27, of which waited for: 16 -> 18; matrix products, arithmetic and copies ran while one was open for 7% -> 7% of each run, Pallas kernels for 5% -> 5%
where the time goes in v6:
time: 142 us
  waiting for transfers between devices  68.6 us (48%)
  starting transfers between devices  46.3 us (33%)
  Pallas kernels  14.7 us (10%)
  other arithmetic  4.78 us (3%)
  matrix products  3.95 us (3%)
  local copies, waits for them, and re-layouts  2.95 us (2%)
    ppermute x17, waiting for transfers between devices, swap(): return lax.ppermute(x, 'ep', [(i, i ^ mask) for i in range(devices)])  33.7 us
    ppermute x17, starting transfers between devices, swap(): return lax.ppermute(x, 'ep', [(i, i ^ mask) for i in range(devices)])  23.4 us
    all_to_all x1, waiting for transfers between devices, body(): lax.all_to_all(latent_out, 'ep', split_axis=1, concat_axis=0, tiled=True,...  18.9 us
    ppermute x9, waiting for transfers between devices, swap_plane(): lax.ppermute(x, 'ep', [(i, i ^ masks[i % 2] * SLABS) for i in range(devic...  16 us
    ppermute x9, starting transfers between devices, swap_plane(): lax.ppermute(x, 'ep', [(i, i ^ masks[i % 2] * SLABS) for i in range(devic...  14.6 us
    all_to_all x1, starting transfers between devices, body(): lax.all_to_all(latent_out, 'ep', split_axis=1, concat_axis=0, tiled=True,...  8.31 us
    pallas_call x2, Pallas kernels, stage(): pl.pallas_call(body, out_shape=tuple((pltpu.VMEM(shape, BF16) for shape i...  6.46 us
    pallas_call x1, Pallas kernels, project_stream(): pl.pallas_call(stream_body, out_shape=projected(rows, width // groups) *...  5.95 us
  transfers between devices with their start and end apart: 27, of which 18 were waited for; matrix products, arithmetic and copies ran while one was open for 7% of the time, Pallas kernels for 5%

profile of v6, /device:TPU:0, one launch (start us, length us, event | category | flops | bytes accessed | tf_op | source)
XLA Modules:
  0.0 141.7 jit_solution(12294374127678758924)
XLA Ops:
  0.5 0.8 copy-done
  1.3 2.3 %convolution_multiply_fusion = f32[8,128,256]{2,1,0:T(8,128)S(1)} fusion(bf16[8,128,576]{1,2,0:T(8,128)(2,1)S(1)} %copy-done, bf16[8,256,576]{1,2,0:T(8,128)(2,1)} %param.19), kind=kOutput, calls=%fused_computation.4 | convolution fusion | flops 302252032 | bytes 4587520 | tf_op jit(solution)/shard_map/bhr,bpr->bhp/dot_general | solution.py:23
  3.6 2.2 %fusion.53 = (f32[8,128]{1,0:T(8,128)S(1)}, f32[8,128,256]{2,1,0:T(8,128)S(1)}) fusion(f32[8,128,256]{2,1,0:T(8,128)S(1)} %convolution_multiply_fusion, s32[8]{0:T(128)S(1)} %copy-done.13), kind=kOutput, calls=%fused_computation.111 | output fusion | flops 1573119 | bytes 2101280 | tf_op jit(solution)/shard_map/sub | solution.py:26
  5.9 0.8 fusion.3
  6.8 1.6 %copy.35 = bf16[8,128,512]{2,0,1:T(8,128)(2,1)} copy(bf16[8,128,512]{2,1,0:T(8,128)(2,1)S(1)} %fusion.3) | data formatting | bytes 2097152 | tf_op jit(solution)/shard_map/convert_element_type | solution.py:30
  8.3 8.3 %all-to-all-start = ((bf16[8,128,512]{2,0,1:T(8,128)(2,1)}), bf16[8,128,512]{2,0,1:T(8,128)(2,1)S(1)}, u32[]{:S(2)}, u32[]{:S(2)}) async-start(bf16[8,128,512]{2,0,1:T(8,128)(2,1)} %copy.35), calls=%async_computation | async-start | bytes 2097152 | tf_op jit(solution)/shard_map/all_to_all | solution.py:274
  18.3 3.7 %collective-permute-done = bf16[4,512,128]{2,1,0:T(8,128)(2,1)S(1)} collective-permute-done((bf16[4,512,128]{2,1,0:T(8,128)(2,1)S(1)}, bf16[4,512,128]{2,1,0:T(8,128)(2,1)S(1)}, u32[]{:S(2)}, u32[]{:S(2)}) %collective-permute-start) | collective-permute-done | bytes 524320 | tf_op jit(solution)/shard_map/ppermute | solution.py:234
  22.2 18.9 %all-to-all-done = bf16[8,128,512]{2,0,1:T(8,128)(2,1)S(1)} async-done(((bf16[8,128,512]{2,0,1:T(8,128)(2,1)}), bf16[8,128,512]{2,0,1:T(8,128)(2,1)S(1)}, u32[]{:S(2)}, u32[]{:S(2)}) %all-to-all-start) | async-done | bytes 1048608 | tf_op jit(solution)/shard_map/all_to_all | solution.py:274
  42.1 6.0 %shard_map.163 = (bf16[64,3584]{1,0:T(8,128)(2,1)S(1)}, f32[64,3584]{1,0:T(8,128)S(1)}, bf16[64,3584]{1,0:T(8,128)(2,1)S(1)}, f32[64,3584]{1,0:T(8,128)S(1)}) custom-call(bf16[2,128,1024]{2,1,0:T(8,128)(2,1)S(1)} %bitcast.19, bf16[512,7168]{1,0:T(8,128)(2,1)} %own.1, bf16[512,7168]{1,0:T(8,128)(2,1)} %collective-permute-done.4.other), custom_call_target="tpu_custom_call" | custom-call | flops 1879048192 | bytes 14680064 | tf_op jit(solution)/shard_map/pallas_call | solution.py:137
  48.1 0.6 collective-permute-start.5
  48.9 2.0 %collective-permute-start.7 = (bf16[64,3584]{1,0:T(8,128)(2,1)S(1)}, bf16[64,3584]{1,0:T(8,128)(2,1)S(1)}, u32[]{:S(2)}, u32[]{:S(2)}) collective-permute-start(bf16[64,3584]{1,0:T(8,128)(2,1)S(1)} %get-tuple-element.26), channel_id=1, source_target_pairs={{0,4},{1,5},{2,6},{3,7},{4,0},{5,1},{6,2},{7,3},{8,12},{9,13},{10,... | collective-permute-start | bytes 1376264 | tf_op jit(solution)/shard_map/ppermute | solution.py:234
  50.9 7.0 %collective-permute-done.5 = bf16[64,3584]{1,0:T(8,128)(2,1)S(1)} collective-permute-done((bf16[64,3584]{1,0:T(8,128)(2,1)S(1)}, bf16[64,3584]{1,0:T(8,128)(2,1)S(1)}, u32[]{:S(2)}, u32[]{:S(2)}) %collective-permute-start.5) | collective-permute-done | bytes 458784 | tf_op jit(solution)/shard_map/ppermute | solution.py:234
  58.0 2.6 %collective-permute-start.6 = (bf16[32,3584]{1,0:T(8,128)(2,1)S(1)}, bf16[32,3584]{1,0:T(8,128)(2,1)S(1)}, u32[]{:S(2)}, u32[]{:S(2)}) collective-permute-start(bf16[32,3584]{1,0:T(8,128)(2,1)S(1)} %slice.165), channel_id=1, source_target_pairs={{0,4},{1,5},{2,6},{3,7},{4,0},{5,1},{6,2},{7,3},{8,12},{9,13},{10,... | collective-permute-start | bytes 688136 | tf_op jit(solution)/shard_map/ppermute | solution.py:234
  60.7 1.7 %collective-permute-start.8 = (bf16[32,3584]{1,0:T(8,128)(2,1)S(1)}, bf16[32,3584]{1,0:T(8,128)(2,1)S(1)}, u32[]{:S(2)}, u32[]{:S(2)}) collective-permute-start(bf16[32,3584]{1,0:T(8,128)(2,1)S(1)} %slice.164), channel_id=1, source_target_pairs={{0,2},{1,3},{2,0},{3,1},{4,6},{5,7},{6,4},{7,5},{8,10},{9,11},{10,... | collective-permute-start | bytes 688136 | tf_op jit(solution)/shard_map/ppermute | solution.py:234
  62.4 2.2 %collective-permute-done.6 = bf16[32,3584]{1,0:T(8,128)(2,1)S(1)} collective-permute-done((bf16[32,3584]{1,0:T(8,128)(2,1)S(1)}, bf16[32,3584]{1,0:T(8,128)(2,1)S(1)}, u32[]{:S(2)}, u32[]{:S(2)}) %collective-permute-start.6) | collective-permute-done | bytes 229408 | tf_op jit(solution)/shard_map/ppermute | solution.py:234
  64.6 2.2 %collective-permute-done.8 = bf16[32,3584]{1,0:T(8,128)(2,1)S(1)} collective-permute-done((bf16[32,3584]{1,0:T(8,128)(2,1)S(1)}, bf16[32,3584]{1,0:T(8,128)(2,1)S(1)}, u32[]{:S(2)}, u32[]{:S(2)}) %collective-permute-start.8) | collective-permute-done | bytes 229408 | tf_op jit(solution)/shard_map/ppermute | solution.py:234
  66.9 3.6 %collective-permute-start.10 = (bf16[8,7168]{1,0:T(8,128)(2,1)S(1)}, bf16[8,7168]{1,0:T(8,128)(2,1)S(1)}, u32[]{:S(2)}, u32[]{:S(2)}) collective-permute-start(bf16[8,7168]{1,0:T(8,128)(2,1)S(1)} %get-tuple-element.46), channel_id=1, source_target_pairs={{0,16},{1,17},{2,18},{3,19},{4,20},{5,21},{6,22},{7,23},{8,24},{9,... | collective-permute-start | bytes 344072 | tf_op jit(solution)/shard_map/ppermute | solution.py:238
  70.5 0.6 collective-permute-start.11
  71.1 1.5 %collective-permute-start.9 = (bf16[8,7168]{1,0:T(8,128)(2,1)S(1)}, bf16[8,7168]{1,0:T(8,128)(2,1)S(1)}, u32[]{:S(2)}, u32[]{:S(2)}) collective-permute-start(bf16[8,7168]{1,0:T(8,128)(2,1)S(1)} %get-tuple-element.44), channel_id=1, source_target_pairs={{0,24},{1,9},{2,26},{3,11},{4,28},{5,13},{6,30},{7,15},{8,16},{9,1... | collective-permute-start | bytes 344072 | tf_op jit(solution)/shard_map/ppermute | solution.py:238
  72.7 1.4 %collective-permute-done.10 = bf16[8,7168]{1,0:T(8,128)(2,1)S(1)} collective-permute-done((bf16[8,7168]{1,0:T(8,128)(2,1)S(1)}, bf16[8,7168]{1,0:T(8,128)(2,1)S(1)}, u32[]{:S(2)}, u32[]{:S(2)}) %collective-permute-start.10) | collective-permute-done | bytes 114720 | tf_op jit(solution)/shard_map/ppermute | solution.py:238
  74.1 2.0 %collective-permute-done.11 = bf16[8,7168]{1,0:T(8,128)(2,1)S(1)} collective-permute-done((bf16[8,7168]{1,0:T(8,128)(2,1)S(1)}, bf16[8,7168]{1,0:T(8,128)(2,1)S(1)}, u32[]{:S(2)}, u32[]{:S(2)}) %collective-permute-start.11) | collective-permute-done | bytes 114720 | tf_op jit(solution)/shard_map/ppermute | solution.py:238
  76.1 1.8 %collective-permute-done.9 = bf16[8,7168]{1,0:T(8,128)(2,1)S(1)} collective-permute-done((bf16[8,7168]{1,0:T(8,128)(2,1)S(1)}, bf16[8,7168]{1,0:T(8,128)(2,1)S(1)}, u32[]{:S(2)}, u32[]{:S(2)}) %collective-permute-start.9) | collective-permute-done | bytes 114720 | tf_op jit(solution)/shard_map/ppermute | solution.py:238
  78.3 0.7 collective-permute-start.12
  78.9 1.8 %collective-permute-start.13 = (bf16[8,7296]{1,0:T(8,128)(2,1)S(1)}, bf16[8,7296]{1,0:T(8,128)(2,1)S(1)}, u32[]{:S(2)}, u32[]{:S(2)}) collective-permute-start(bf16[8,7296]{1,0:T(8,128)(2,1)S(1)} %pad_maximum_fusion.10), channel_id=1, source_target_pairs={{0,16},{1,17},{2,18},{3,19},{4,20},{5,21},{6,22},{7,23},{8,24},{9,... | collective-permute-start | bytes 350216 | tf_op jit(solution)/shard_map/ppermute | solution.py:238
  80.7 2.0 %collective-permute-start.14 = (bf16[8,7296]{1,0:T(8,128)(2,1)S(1)}, bf16[8,7296]{1,0:T(8,128)(2,1)S(1)}, u32[]{:S(2)}, u32[]{:S(2)}) collective-permute-start(bf16[8,7296]{1,0:T(8,128)(2,1)S(1)} %pad_maximum_fusion.10), channel_id=1, source_target_pairs={{0,24},{1,9},{2,26},{3,11},{4,28},{5,13},{6,30},{7,15},{8,16},{9,1... | collective-permute-start | bytes 350216 | tf_op jit(solution)/shard_map/ppermute | solution.py:238
  82.7 3.2 %collective-permute-done.12 = bf16[8,7296]{1,0:T(8,128)(2,1)S(1)} collective-permute-done((bf16[8,7296]{1,0:T(8,128)(2,1)S(1)}, bf16[8,7296]{1,0:T(8,128)(2,1)S(1)}, u32[]{:S(2)}, u32[]{:S(2)}) %collective-permute-start.12) | collective-permute-done | bytes 116768 | tf_op jit(solution)/shard_map/ppermute | solution.py:238
  85.9 2.2 %collective-permute-done.14 = bf16[8,7296]{1,0:T(8,128)(2,1)S(1)} collective-permute-done((bf16[8,7296]{1,0:T(8,128)(2,1)S(1)}, bf16[8,7296]{1,0:T(8,128)(2,1)S(1)}, u32[]{:S(2)}, u32[]{:S(2)}) %collective-permute-start.14) | collective-permute-done | bytes 116768 | tf_op jit(solution)/shard_map/ppermute | solution.py:238
  88.2 2.4 %collective-permute-start.17 = (bf16[32,3712]{1,0:T(8,128)(2,1)S(1)}, bf16[32,3712]{1,0:T(8,128)(2,1)S(1)}, u32[]{:S(2)}, u32[]{:S(2)}) collective-permute-start(bf16[32,3712]{1,0:T(8,128)(2,1)S(1)} %pad_maximum_fusion.5), channel_id=1, source_target_pairs={{0,2},{1,3},{2,0},{3,1},{4,6},{5,7},{6,4},{7,5},{8,10},{9,11},{10,... | collective-permute-start | bytes 712712 | tf_op jit(solution)/shard_map/ppermute | solution.py:234
  90.6 1.9 %collective-permute-start.15 = (bf16[32,3584]{1,0:T(8,128)(2,1)S(1)}, bf16[32,3584]{1,0:T(8,128)(2,1)S(1)}, u32[]{:S(2)}, u32[]{:S(2)}) collective-permute-start(bf16[32,3584]{1,0:T(8,128)(2,1)S(1)} %pad_maximum_fusion.9), channel_id=1, source_target_pairs={{0,4},{1,5},{2,6},{3,7},{4,0},{5,1},{6,2},{7,3},{8,12},{9,13},{10,... | collective-permute-start | bytes 688136 | tf_op jit(solution)/shard_map/ppermute | solution.py:234
  92.5 2.9 %collective-permute-done.17 = bf16[32,3712]{1,0:T(8,128)(2,1)S(1)} collective-permute-done((bf16[32,3712]{1,0:T(8,128)(2,1)S(1)}, bf16[32,3712]{1,0:T(8,128)(2,1)S(1)}, u32[]{:S(2)}, u32[]{:S(2)}) %collective-permute-start.17) | collective-permute-done | bytes 237600 | tf_op jit(solution)/shard_map/ppermute | solution.py:234
  95.4 3.3 %collective-permute-start.18 = (bf16[64,3712]{1,0:T(8,128)(2,1)S(1)}, bf16[64,3712]{1,0:T(8,128)(2,1)S(1)}, u32[]{:S(2)}, u32[]{:S(2)}) collective-permute-start(bf16[64,3712]{1,0:T(8,128)(2,1)S(1)} %pad_maximum_fusion.3.near_b), channel_id=1, source_target_pairs={{0,4},{1,5},{2,6},{3,7},{4,0},{5,1},{6,2},{7,3},{8,12},{9,13},{10,... | collective-permute-start | bytes 1425416 | tf_op jit(solution)/shard_map/ppermute | solution.py:234
  99.1 2.2 %collective-permute-start.16 = (bf16[64,3584]{1,0:T(8,128)(2,1)S(1)}, bf16[64,3584]{1,0:T(8,128)(2,1)S(1)}, u32[]{:S(2)}, u32[]{:S(2)}) collective-permute-start(bf16[64,3584]{1,0:T(8,128)(2,1)S(1)} %pad_maximum_fusion.4.near_a), channel_id=1, source_target_pairs={{0,2},{1,3},{2,0},{3,1},{4,6},{5,7},{6,4},{7,5},{8,10},{9,11},{10,... | collective-permute-start | bytes 1376264 | tf_op jit(solution)/shard_map/ppermute | solution.py:234
  101.3 2.6 %shard_map.165 = (bf16[256,3584]{1,0:T(8,128)(2,1)S(1)}, bf16[256,3584]{1,0:T(8,128)(2,1)S(1)}, f32[8,128]{1,0:T(8,128)}) custom-call(bf16[128,7168]{1,0:T(8,128)(2,1)} %refs_0_.3, bf16[128,7168]{1,0:T(8,128)(2,1)} %collective-permute-done.3.refs_1_, bf16[8,7168]{1,0:T(8,128)(2,1)S(1)} %multiply_convert_fusion.refs_4_.refs_2_), custom_call_target="tpu_custom_call" | custom-call | bytes 7340032 | tf_op jit(solution)/shard_map/pallas_call | solution.py:58
  104.0 3.8 %shard_map.164 = (bf16[7168,512]{1,0:T(8,128)(2,1)S(1)}, f32[8,128]{1,0:T(8,128)}) custom-call(bf16[7168,128]{1,0:T(8,128)(2,1)} %refs_0_.2, bf16[7168,128]{1,0:T(8,128)(2,1)} %collective-permute-done.1.refs_1_, bf16[7168,128]{1,0:T(8,128)(2,1)} %refs_2_.1, bf16[7168,128]{1,0:T(8,128)(2,1)} %collective-permute-done.2.refs_3_, ...), custom_call_target="tpu_custom_call" | custom-call | bytes 14680064 | tf_op jit(solution)/shard_map/pallas_call | solution.py:58
  107.8 1.3 collective-permute-done.16.far_a
  109.1 2.3 %shard_map.166 = (bf16[64,3584]{1,0:T(8,128)(2,1)S(1)}, f32[64,3584]{1,0:T(8,128)S(1)}, bf16[64,3584]{1,0:T(8,128)(2,1)S(1)}, f32[64,3584]{1,0:T(8,128)S(1)}) custom-call(s32[2]{0:T(128)S(1)} %pad_add_fusion.label, bf16[64,3584]{1,0:T(8,128)(2,1)S(1)} %pad_maximum_fusion.4.near_a, bf16[64,3584]{1,0:T(8,128)(2,1)S(1)} %collective-permute-done.16.far_a, ...), custom_call_target="tpu_custom_call" | custom-call | flops 1409286144 | bytes 5505024 | tf_op jit(solution)/shard_map/pallas_call | solution.py:197
  111.5 1.1 collective-permute-start.21
  112.5 1.6 %collective-permute-start.19 = (bf16[64,3584]{1,0:T(8,128)(2,1)S(1)}, bf16[64,3584]{1,0:T(8,128)(2,1)S(1)}, u32[]{:S(2)}, u32[]{:S(2)}) collective-permute-start(bf16[64,3584]{1,0:T(8,128)(2,1)S(1)} %get-tuple-element.34), channel_id=1, source_target_pairs={{0,2},{1,3},{2,0},{3,1},{4,6},{5,7},{6,4},{7,5},{8,10},{9,11},{10,... | collective-permute-start | bytes 1376264 | tf_op jit(solution)/shard_map/ppermute | solution.py:234
  114.1 8.4 %collective-permute-done.21 = bf16[64,3584]{1,0:T(8,128)(2,1)S(1)} collective-permute-done((bf16[64,3584]{1,0:T(8,128)(2,1)S(1)}, bf16[64,3584]{1,0:T(8,128)(2,1)S(1)}, u32[]{:S(2)}, u32[]{:S(2)}) %collective-permute-start.21) | collective-permute-done | bytes 458784 | tf_op jit(solution)/shard_map/ppermute | solution.py:234
  122.6 2.2 %collective-permute-start.22 = (bf16[32,3584]{1,0:T(8,128)(2,1)S(1)}, bf16[32,3584]{1,0:T(8,128)(2,1)S(1)}, u32[]{:S(2)}, u32[]{:S(2)}) collective-permute-start(bf16[32,3584]{1,0:T(8,128)(2,1)S(1)} %slice.162), channel_id=1, source_target_pairs={{0,2},{1,3},{2,0},{3,1},{4,6},{5,7},{6,4},{7,5},{8,10},{9,11},{10,... | collective-permute-start | bytes 688136 | tf_op jit(solution)/shard_map/ppermute | solution.py:234
  125.3 3.5 %collective-permute-done.22 = bf16[32,3584]{1,0:T(8,128)(2,1)S(1)} collective-permute-done((bf16[32,3584]{1,0:T(8,128)(2,1)S(1)}, bf16[32,3584]{1,0:T(8,128)(2,1)S(1)}, u32[]{:S(2)}, u32[]{:S(2)}) %collective-permute-start.22) | collective-permute-done | bytes 229408 | tf_op jit(solution)/shard_map/ppermute | solution.py:234
  128.9 2.2 %collective-permute-done.20 = bf16[32,3584]{1,0:T(8,128)(2,1)S(1)} collective-permute-done((bf16[32,3584]{1,0:T(8,128)(2,1)S(1)}, bf16[32,3584]{1,0:T(8,128)(2,1)S(1)}, u32[]{:S(2)}, u32[]{:S(2)}) %collective-permute-start.20) | collective-permute-done | bytes 229408 | tf_op jit(solution)/shard_map/ppermute | solution.py:234
  131.2 2.3 %collective-permute-start.23 = (bf16[8,7168]{1,0:T(8,128)(2,1)S(1)}, bf16[8,7168]{1,0:T(8,128)(2,1)S(1)}, u32[]{:S(2)}, u32[]{:S(2)}) collective-permute-start(bf16[8,7168]{1,0:T(8,128)(2,1)S(1)} %get-tuple-element.41), channel_id=1, source_target_pairs={{0,24},{1,9},{2,26},{3,11},{4,28},{5,13},{6,30},{7,15},{8,16},{9,1... | collective-permute-start | bytes 344072 | tf_op jit(solution)/shard_map/ppermute | solution.py:238
  133.5 1.0 collective-permute-start.24
  134.5 1.1 collective-permute-start.25
  135.6 2.3 %collective-permute-done.23 = bf16[8,7168]{1,0:T(8,128)(2,1)S(1)} collective-permute-done((bf16[8,7168]{1,0:T(8,128)(2,1)S(1)}, bf16[8,7168]{1,0:T(8,128)(2,1)S(1)}, u32[]{:S(2)}, u32[]{:S(2)}) %collective-permute-start.23) | collective-permute-done | bytes 114720 | tf_op jit(solution)/shard_map/ppermute | solution.py:238
  138.0 3.0 %collective-permute-done.24 = bf16[8,7168]{1,0:T(8,128)(2,1)S(1)} collective-permute-done((bf16[8,7168]{1,0:T(8,128)(2,1)S(1)}, bf16[8,7168]{1,0:T(8,128)(2,1)S(1)}, u32[]{:S(2)}, u32[]{:S(2)}) %collective-permute-start.24) | collective-permute-done | bytes 114720 | tf_op jit(solution)/shard_map/ppermute | solution.py:238
  141.0 0.7 fusion.27
  (87 shorter events, 5.5 us)
Async XLA Ops:
  0.0 1.3 copy-start
  0.0 3.6 %copy-start.13 = (s32[8]{0:T(128)S(1)}, s32[8]{0:T(128)}, u32[]{:S(2)}) copy-start(s32[8]{0:T(128)} %param.20) | copy-start | bytes 100
  0.0 42.1 %collective-permute-start.4 = (bf16[512,7168]{1,0:T(8,128)(2,1)}, bf16[512,7168]{1,0:T(8,128)(2,1)}, u32[]{:S(2)}, u32[]{:S(2)}) collective-permute-start(bf16[512,7168]{1,0:T(8,128)(2,1)} %own.1), channel_id=1, source_target_pairs={{0,1},{1,0},{2,3},{3,2},{4,5},{5,4},{6,7},{7,6},{8,9},{9,8},{10,11... | collective-permute-start | bytes 22020104 | tf_op jit(solution)/shard_map/ppermute | solution.py:234
  3.6 2.3 %copy-start.2 = (bf16[8,256,576]{1,2,0:T(8,128)(2,1)S(1)}, bf16[8,256,576]{1,2,0:T(8,128)(2,1)}, u32[]{:S(2)}) copy-start(bf16[8,256,576]{1,2,0:T(8,128)(2,1)} %param.19) | copy-start | bytes 7077892
  6.7 10.6 %copy-start.3 = (bf16[4,512,128]{2,1,0:T(8,128)(2,1)S(1)}, bf16[4,512,128]{2,1,0:T(8,128)(2,1)}, u32[]{:S(2)}) copy-start(bf16[4,512,128]{2,1,0:T(8,128)(2,1)} %param.21) | copy-start | bytes 1572868
  6.7 11.0 %copy-start.9 = (s32[16]{0:T(128)S(1)}, s32[16]{0:T(128)}, u32[]{:S(2)}) copy-start(s32[16]{0:T(128)} %constant.74.clone) | copy-start | bytes 196
  6.7 11.0 %copy-start.10 = (s32[16]{0:T(128)S(1)}, s32[16]{0:T(128)}, u32[]{:S(2)}) copy-start(s32[16]{0:T(128)} %constant.75.clone) | copy-start | bytes 196
  6.7 11.0 %copy-start.11 = (s32[16]{0:T(128)S(1)}, s32[16]{0:T(128)}, u32[]{:S(2)}) copy-start(s32[16]{0:T(128)} %constant.76.clone) | copy-start | bytes 196
  6.8 11.0 %copy-start.12 = (s32[16]{0:T(128)S(1)}, s32[16]{0:T(128)}, u32[]{:S(2)}) copy-start(s32[16]{0:T(128)} %constant.77.clone) | copy-start | bytes 196
  8.3 32.8 %all-to-all-start = ((bf16[8,128,512]{2,0,1:T(8,128)(2,1)}), bf16[8,128,512]{2,0,1:T(8,128)(2,1)S(1)}, u32[]{:S(2)}, u32[]{:S(2)}) async-start(bf16[8,128,512]{2,0,1:T(8,128)(2,1)} %copy.35), calls=%async_computation | async-start | bytes 2097152 | tf_op jit(solution)/shard_map/all_to_all | solution.py:274
  16.6 24.5 %collective-permute-start.1 = (bf16[7168,128]{1,0:T(8,128)(2,1)}, bf16[7168,128]{1,0:T(8,128)(2,1)}, u32[]{:S(2)}, u32[]{:S(2)}) collective-permute-start(bf16[7168,128]{1,0:T(8,128)(2,1)} %refs_0_.2), channel_id=1, source_target_pairs={{0,1},{1,0},{2,3},{3,2},{4,5},{5,4},{6,7},{7,6},{8,9},{9,8},{10,11... | collective-permute-start | bytes 5505032 | tf_op jit(solution)/shard_map/ppermute | solution.py:234
  16.7 24.5 %collective-permute-start.2 = (bf16[7168,128]{1,0:T(8,128)(2,1)}, bf16[7168,128]{1,0:T(8,128)(2,1)}, u32[]{:S(2)}, u32[]{:S(2)}) collective-permute-start(bf16[7168,128]{1,0:T(8,128)(2,1)} %refs_2_.1), channel_id=1, source_target_pairs={{0,1},{1,0},{2,3},{3,2},{4,5},{5,4},{6,7},{7,6},{8,9},{9,8},{10,11... | collective-permute-start | bytes 5505032 | tf_op jit(solution)/shard_map/ppermute | solution.py:234
  17.2 24.0 %collective-permute-start.3 = (bf16[128,7168]{1,0:T(8,128)(2,1)}, bf16[128,7168]{1,0:T(8,128)(2,1)}, u32[]{:S(2)}, u32[]{:S(2)}) collective-permute-start(bf16[128,7168]{1,0:T(8,128)(2,1)} %refs_0_.3), channel_id=1, source_target_pairs={{0,1},{1,0},{2,3},{3,2},{4,5},{5,4},{6,7},{7,6},{8,9},{9,8},{10,11... | collective-permute-start | bytes 5505032 | tf_op jit(solution)/shard_map/ppermute | solution.py:234
  17.3 4.7 %collective-permute-start = (bf16[4,512,128]{2,1,0:T(8,128)(2,1)S(1)}, bf16[4,512,128]{2,1,0:T(8,128)(2,1)S(1)}, u32[]{:S(2)}, u32[]{:S(2)}) collective-permute-start(bf16[4,512,128]{2,1,0:T(8,128)(2,1)S(1)} %copy-done.3), channel_id=1, source_target_pairs={{0,1},{1,0},{2,3},{3,2},{4,5},{5,4},{6,7},{7,6},{8,9},{9,8},{10,11... | collective-permute-start | bytes 1572872 | tf_op jit(solution)/shard_map/ppermute | solution.py:234
  42.1 6.6 %copy-start.6 = (s32[8,2]{0,1:T(2,128)S(1)}, s32[8,2]{0,1:T(2,128)}, u32[]{:S(2)}) copy-start(s32[8,2]{0,1:T(2,128)} %param.24) | copy-start | bytes 196
  42.1 6.6 %copy-start.8 = (s32[4]{0:T(128)S(1)}, s32[4]{0:T(128)}, u32[]{:S(2)}) copy-start(s32[4]{0:T(128)} %param.26) | copy-start | bytes 52
  42.1 6.7 %copy-start.7 = (f32[8,2]{0,1:T(2,128)S(1)}, f32[8,2]{0,1:T(2,128)}, u32[]{:S(2)}) copy-start(f32[8,2]{0,1:T(2,128)} %param.25) | copy-start | bytes 196
  48.1 9.8 %collective-permute-start.5 = (bf16[64,3584]{1,0:T(8,128)(2,1)S(1)}, bf16[64,3584]{1,0:T(8,128)(2,1)S(1)}, u32[]{:S(2)}, u32[]{:S(2)}) collective-permute-start(bf16[64,3584]{1,0:T(8,128)(2,1)S(1)} %get-tuple-element.24), channel_id=1, source_target_pairs={{0,2},{1,3},{2,0},{3,1},{4,6},{5,7},{6,4},{7,5},{8,10},{9,11},{10,... | collective-permute-start | bytes 1376264 | tf_op jit(solution)/shard_map/ppermute | solution.py:234
  48.9 11.7 %collective-permute-start.7 = (bf16[64,3584]{1,0:T(8,128)(2,1)S(1)}, bf16[64,3584]{1,0:T(8,128)(2,1)S(1)}, u32[]{:S(2)}, u32[]{:S(2)}) collective-permute-start(bf16[64,3584]{1,0:T(8,128)(2,1)S(1)} %get-tuple-element.26), channel_id=1, source_target_pairs={{0,4},{1,5},{2,6},{3,7},{4,0},{5,1},{6,2},{7,3},{8,12},{9,13},{10,... | collective-permute-start | bytes 1376264 | tf_op jit(solution)/shard_map/ppermute | solution.py:234
  58.0 6.6 %collective-permute-start.6 = (bf16[32,3584]{1,0:T(8,128)(2,1)S(1)}, bf16[32,3584]{1,0:T(8,128)(2,1)S(1)}, u32[]{:S(2)}, u32[]{:S(2)}) collective-permute-start(bf16[32,3584]{1,0:T(8,128)(2,1)S(1)} %slice.165), channel_id=1, source_target_pairs={{0,4},{1,5},{2,6},{3,7},{4,0},{5,1},{6,2},{7,3},{8,12},{9,13},{10,... | collective-permute-start | bytes 688136 | tf_op jit(solution)/shard_map/ppermute | solution.py:234
  60.7 11.9 %copy-start.5 = (bf16[7168]{0:T(1024)(128)(2,1)S(1)}, bf16[7168]{0:T(1024)(128)(2,1)}, u32[]{:S(2)}) copy-start(bf16[7168]{0:T(1024)(128)(2,1)} %param.23) | copy-start | bytes 43012
  60.7 17.2 %copy-start.4 = (bf16[8,7168]{1,0:T(8,128)(2,1)S(1)}, bf16[8,7168]{1,0:T(8,128)(2,1)}, u32[]{:S(2)}) copy-start(bf16[8,7168]{1,0:T(8,128)(2,1)} %param.17) | copy-start | bytes 344068
  60.7 6.1 %collective-permute-start.8 = (bf16[32,3584]{1,0:T(8,128)(2,1)S(1)}, bf16[32,3584]{1,0:T(8,128)(2,1)S(1)}, u32[]{:S(2)}, u32[]{:S(2)}) collective-permute-start(bf16[32,3584]{1,0:T(8,128)(2,1)S(1)} %slice.164), channel_id=1, source_target_pairs={{0,2},{1,3},{2,0},{3,1},{4,6},{5,7},{6,4},{7,5},{8,10},{9,11},{10,... | collective-permute-start | bytes 688136 | tf_op jit(solution)/shard_map/ppermute | solution.py:234
  66.9 7.2 %collective-permute-start.10 = (bf16[8,7168]{1,0:T(8,128)(2,1)S(1)}, bf16[8,7168]{1,0:T(8,128)(2,1)S(1)}, u32[]{:S(2)}, u32[]{:S(2)}) collective-permute-start(bf16[8,7168]{1,0:T(8,128)(2,1)S(1)} %get-tuple-element.46), channel_id=1, source_target_pairs={{0,16},{1,17},{2,18},{3,19},{4,20},{5,21},{6,22},{7,23},{8,24},{9,... | collective-permute-start | bytes 344072 | tf_op jit(solution)/shard_map/ppermute | solution.py:238
  70.5 5.6 %collective-permute-start.11 = (bf16[8,7168]{1,0:T(8,128)(2,1)S(1)}, bf16[8,7168]{1,0:T(8,128)(2,1)S(1)}, u32[]{:S(2)}, u32[]{:S(2)}) collective-permute-start(bf16[8,7168]{1,0:T(8,128)(2,1)S(1)} %get-tuple-element.45), channel_id=1, source_target_pairs={{0,8},{1,25},{2,10},{3,27},{4,12},{5,29},{6,14},{7,31},{8,0},{9,17... | collective-permute-start | bytes 344072 | tf_op jit(solution)/shard_map/ppermute | solution.py:238
  71.1 6.8 %collective-permute-start.9 = (bf16[8,7168]{1,0:T(8,128)(2,1)S(1)}, bf16[8,7168]{1,0:T(8,128)(2,1)S(1)}, u32[]{:S(2)}, u32[]{:S(2)}) collective-permute-start(bf16[8,7168]{1,0:T(8,128)(2,1)S(1)} %get-tuple-element.44), channel_id=1, source_target_pairs={{0,24},{1,9},{2,26},{3,11},{4,28},{5,13},{6,30},{7,15},{8,16},{9,1... | collective-permute-start | bytes 344072 | tf_op jit(solution)/shard_map/ppermute | solution.py:238
  78.3 7.7 %collective-permute-start.12 = (bf16[8,7296]{1,0:T(8,128)(2,1)S(1)}, bf16[8,7296]{1,0:T(8,128)(2,1)S(1)}, u32[]{:S(2)}, u32[]{:S(2)}) collective-permute-start(bf16[8,7296]{1,0:T(8,128)(2,1)S(1)} %pad_maximum_fusion.10), channel_id=1, source_target_pairs={{0,8},{1,25},{2,10},{3,27},{4,12},{5,29},{6,14},{7,31},{8,0},{9,17... | collective-permute-start | bytes 350216 | tf_op jit(solution)/shard_map/ppermute | solution.py:238
  78.9 7.0 %collective-permute-start.13 = (bf16[8,7296]{1,0:T(8,128)(2,1)S(1)}, bf16[8,7296]{1,0:T(8,128)(2,1)S(1)}, u32[]{:S(2)}, u32[]{:S(2)}) collective-permute-start(bf16[8,7296]{1,0:T(8,128)(2,1)S(1)} %pad_maximum_fusion.10), channel_id=1, source_target_pairs={{0,16},{1,17},{2,18},{3,19},{4,20},{5,21},{6,22},{7,23},{8,24},{9,... | collective-permute-start | bytes 350216 | tf_op jit(solution)/shard_map/ppermute | solution.py:238
  80.7 7.4 %collective-permute-start.14 = (bf16[8,7296]{1,0:T(8,128)(2,1)S(1)}, bf16[8,7296]{1,0:T(8,128)(2,1)S(1)}, u32[]{:S(2)}, u32[]{:S(2)}) collective-permute-start(bf16[8,7296]{1,0:T(8,128)(2,1)S(1)} %pad_maximum_fusion.10), channel_id=1, source_target_pairs={{0,24},{1,9},{2,26},{3,11},{4,28},{5,13},{6,30},{7,15},{8,16},{9,1... | collective-permute-start | bytes 350216 | tf_op jit(solution)/shard_map/ppermute | solution.py:238
  88.2 7.2 %collective-permute-start.17 = (bf16[32,3712]{1,0:T(8,128)(2,1)S(1)}, bf16[32,3712]{1,0:T(8,128)(2,1)S(1)}, u32[]{:S(2)}, u32[]{:S(2)}) collective-permute-start(bf16[32,3712]{1,0:T(8,128)(2,1)S(1)} %pad_maximum_fusion.5), channel_id=1, source_target_pairs={{0,2},{1,3},{2,0},{3,1},{4,6},{5,7},{6,4},{7,5},{8,10},{9,11},{10,... | collective-permute-start | bytes 712712 | tf_op jit(solution)/shard_map/ppermute | solution.py:234
  90.6 8.5 %collective-permute-start.15 = (bf16[32,3584]{1,0:T(8,128)(2,1)S(1)}, bf16[32,3584]{1,0:T(8,128)(2,1)S(1)}, u32[]{:S(2)}, u32[]{:S(2)}) collective-permute-start(bf16[32,3584]{1,0:T(8,128)(2,1)S(1)} %pad_maximum_fusion.9), channel_id=1, source_target_pairs={{0,4},{1,5},{2,6},{3,7},{4,0},{5,1},{6,2},{7,3},{8,12},{9,13},{10,... | collective-permute-start | bytes 688136 | tf_op jit(solution)/shard_map/ppermute | solution.py:234
  95.4 13.7 %collective-permute-start.18 = (bf16[64,3712]{1,0:T(8,128)(2,1)S(1)}, bf16[64,3712]{1,0:T(8,128)(2,1)S(1)}, u32[]{:S(2)}, u32[]{:S(2)}) collective-permute-start(bf16[64,3712]{1,0:T(8,128)(2,1)S(1)} %pad_maximum_fusion.3.near_b), channel_id=1, source_target_pairs={{0,4},{1,5},{2,6},{3,7},{4,0},{5,1},{6,2},{7,3},{8,12},{9,13},{10,... | collective-permute-start | bytes 1425416 | tf_op jit(solution)/shard_map/ppermute | solution.py:234
  99.1 10.1 %collective-permute-start.16 = (bf16[64,3584]{1,0:T(8,128)(2,1)S(1)}, bf16[64,3584]{1,0:T(8,128)(2,1)S(1)}, u32[]{:S(2)}, u32[]{:S(2)}) collective-permute-start(bf16[64,3584]{1,0:T(8,128)(2,1)S(1)} %pad_maximum_fusion.4.near_a), channel_id=1, source_target_pairs={{0,2},{1,3},{2,0},{3,1},{4,6},{5,7},{6,4},{7,5},{8,10},{9,11},{10,... | collective-permute-start | bytes 1376264 | tf_op jit(solution)/shard_map/ppermute | solution.py:234
  111.5 11.0 %collective-permute-start.21 = (bf16[64,3584]{1,0:T(8,128)(2,1)S(1)}, bf16[64,3584]{1,0:T(8,128)(2,1)S(1)}, u32[]{:S(2)}, u32[]{:S(2)}) collective-permute-start(bf16[64,3584]{1,0:T(8,128)(2,1)S(1)} %get-tuple-element.36), channel_id=1, source_target_pairs={{0,4},{1,5},{2,6},{3,7},{4,0},{5,1},{6,2},{7,3},{8,12},{9,13},{10,... | collective-permute-start | bytes 1376264 | tf_op jit(solution)/shard_map/ppermute | solution.py:234
  112.5 12.3 %collective-permute-start.19 = (bf16[64,3584]{1,0:T(8,128)(2,1)S(1)}, bf16[64,3584]{1,0:T(8,128)(2,1)S(1)}, u32[]{:S(2)}, u32[]{:S(2)}) collective-permute-start(bf16[64,3584]{1,0:T(8,128)(2,1)S(1)} %get-tuple-element.34), channel_id=1, source_target_pairs={{0,2},{1,3},{2,0},{3,1},{4,6},{5,7},{6,4},{7,5},{8,10},{9,11},{10,... | collective-permute-start | bytes 1376264 | tf_op jit(solution)/shard_map/ppermute | solution.py:234
  122.6 6.2 %collective-permute-start.22 = (bf16[32,3584]{1,0:T(8,128)(2,1)S(1)}, bf16[32,3584]{1,0:T(8,128)(2,1)S(1)}, u32[]{:S(2)}, u32[]{:S(2)}) collective-permute-start(bf16[32,3584]{1,0:T(8,128)(2,1)S(1)} %slice.162), channel_id=1, source_target_pairs={{0,2},{1,3},{2,0},{3,1},{4,6},{5,7},{6,4},{7,5},{8,10},{9,11},{10,... | collective-permute-start | bytes 688136 | tf_op jit(solution)/shard_map/ppermute | solution.py:234
  125.0 6.1 %collective-permute-start.20 = (bf16[32,3584]{1,0:T(8,128)(2,1)S(1)}, bf16[32,3584]{1,0:T(8,128)(2,1)S(1)}, u32[]{:S(2)}, u32[]{:S(2)}) collective-permute-start(bf16[32,3584]{1,0:T(8,128)(2,1)S(1)} %slice.163), channel_id=1, source_target_pairs={{0,4},{1,5},{2,6},{3,7},{4,0},{5,1},{6,2},{7,3},{8,12},{9,13},{10,... | collective-permute-start | bytes 688136 | tf_op jit(solution)/shard_map/ppermute | solution.py:234
  131.1 10.6 %copy-start.1 = (bf16[8,128,576]{1,2,0:T(8,128)(2,1)S(1)}, bf16[8,128,576]{1,2,0:T(8,128)(2,1)}, u32[]{:S(2)}) copy-start(bf16[8,128,576]{1,2,0:T(8,128)(2,1)} %param.18) | copy-start | bytes 3538948
  131.2 6.8 %collective-permute-start.23 = (bf16[8,7168]{1,0:T(8,128)(2,1)S(1)}, bf16[8,7168]{1,0:T(8,128)(2,1)S(1)}, u32[]{:S(2)}, u32[]{:S(2)}) collective-permute-start(bf16[8,7168]{1,0:T(8,128)(2,1)S(1)} %get-tuple-element.41), channel_id=1, source_target_pairs={{0,24},{1,9},{2,26},{3,11},{4,28},{5,13},{6,30},{7,15},{8,16},{9,1... | collective-permute-start | bytes 344072 | tf_op jit(solution)/shard_map/ppermute | solution.py:238
  133.5 7.4 %collective-permute-start.24 = (bf16[8,7168]{1,0:T(8,128)(2,1)S(1)}, bf16[8,7168]{1,0:T(8,128)(2,1)S(1)}, u32[]{:S(2)}, u32[]{:S(2)}) collective-permute-start(bf16[8,7168]{1,0:T(8,128)(2,1)S(1)} %get-tuple-element.43), channel_id=1, source_target_pairs={{0,16},{1,17},{2,18},{3,19},{4,20},{5,21},{6,22},{7,23},{8,24},{9,... | collective-permute-start | bytes 344072 | tf_op jit(solution)/shard_map/ppermute | solution.py:238
  134.5 6.5 %collective-permute-start.25 = (bf16[8,7168]{1,0:T(8,128)(2,1)S(1)}, bf16[8,7168]{1,0:T(8,128)(2,1)S(1)}, u32[]{:S(2)}, u32[]{:S(2)}) collective-permute-start(bf16[8,7168]{1,0:T(8,128)(2,1)S(1)} %get-tuple-element.42), channel_id=1, source_target_pairs={{0,8},{1,25},{2,10},{3,27},{4,12},{5,29},{6,14},{7,31},{8,0},{9,17... | collective-permute-start | bytes 344072 | tf_op jit(solution)/shard_map/ppermute | solution.py:238
